TPU v7x, 32 devices: a whole 2x2x4 slice. The times are simulated.
32 devices in a mesh: head: 2 (over x), ctx: 16 (over z, y, core).
Axes of the slice: x: 2, y: 2, z: 4, core: 2. Of those that a mesh axis runs over, the one named last changes fastest.
Arguments:
- queries: bfloat16 [8192, 1024], P('ctx', 'head'), may hold values from -26.25 to 26.25
- keys: bfloat16 [8192, 256], P(('ctx', 'head')), may hold values from -7.5 to 7.5
- values: bfloat16 [8192, 256], P(('ctx', 'head')), may hold values from -5 to 5
- selected: int32 [2, 16, 3], P('head'), may hold values from 0 to 15, as said below
Outputs:
- attended: bfloat16 [8192, 1024], P('ctx', 'head')
Inputs may be any that keep to these rules, and one draw needn't show every extreme that they name: `selected`: row b of every key-value head holds b in slot 0; its other 2 slots hold distinct blocks below b, or b again where fewer than 2 blocks lie below b.
All inputs are finite; a program needn't handle non-finite values.
Results may differ from a plain program's by a relative error of at most 0.0041.
Values may be sent and summed in bfloat16 or wider, within the bound.
No kernel may reach another device: no remote copies, remote signals or barrier semaphores. Data moves between devices by JAX's collectives and lax.ppermute only.
A program may use at most 64 MiB of HBM per device.

v0:
```python
import jax
import jax.numpy as jnp
from jax import lax
from jax.sharding import PartitionSpec as P

HD = 128
QH = 4
BLK = 512


def attend_block(inputs):
    query_block, own_keys, own_values, tile_keys, tile_values, slot_live = inputs
    block_len = own_keys.shape[0]
    head_size = own_keys.shape[1]
    factor = head_size ** (-0.5)
    key_rows = jnp.concatenate([own_keys[None], tile_keys], axis=0).reshape(-1, head_size)
    value_rows = jnp.concatenate([own_values[None], tile_values], axis=0).reshape(-1, head_size)
    positions = jnp.arange(block_len, dtype=jnp.int32)
    causal = positions[:, None] >= positions[None, :]
    others = jnp.broadcast_to(slot_live[None, :, None], (block_len, slot_live.shape[0], block_len))
    allowed = jnp.concatenate([causal[:, None, :], others], axis=1).reshape(block_len, -1)

    def per_head(query_head):
        scores = (
            jnp.einsum("qd,kd->qk", query_head, key_rows, preferred_element_type=jnp.float32)
            * factor
        )
        scores = jnp.where(allowed, scores, -jnp.inf)
        top_score = jnp.max(scores, axis=1, keepdims=True)
        weights = jnp.exp(scores - top_score)
        weight_sum = jnp.sum(weights, axis=1)
        product = jnp.dot(
            weights.astype(jnp.bfloat16), value_rows, preferred_element_type=jnp.float32
        )
        return (product / weight_sum[:, None]).astype(jnp.bfloat16)

    return lax.map(per_head, query_block)


def on_device(queries, keys, values, selected):
    key_local, value_local = (
        lax.all_to_all(keys, "head", split_axis=1, concat_axis=0, tiled=True),
        lax.all_to_all(values, "head", split_axis=1, concat_axis=0, tiled=True),
    )
    rows_here = key_local.shape[0]
    query_blocks = rows_here // BLK
    ctx_rank = lax.axis_index("ctx")
    first_block = ctx_rank * query_blocks
    chosen = selected[0]
    own_lists = lax.dynamic_slice_in_dim(chosen, first_block, query_blocks, 0)
    query_heads = queries.reshape(query_blocks, BLK, QH, HD).transpose(0, 2, 1, 3)
    own_keys = key_local.reshape(query_blocks, BLK, HD)
    own_values = value_local.reshape(query_blocks, BLK, HD)
    full_keys, full_values = (
        lax.all_gather(key_local, "ctx", axis=0, tiled=True),
        lax.all_gather(value_local, "ctx", axis=0, tiled=True),
    )
    full_keys = full_keys.reshape(-1, BLK, HD)
    full_values = full_values.reshape(-1, BLK, HD)
    tile_keys = full_keys[own_lists[:, 1:]]
    tile_values = full_values[own_lists[:, 1:]]
    block_ids = first_block + jnp.arange(query_blocks, dtype=jnp.int32)
    slot_live = own_lists[:, 1:] != block_ids[:, None]
    stacked = lax.map(
        attend_block, (query_heads, own_keys, own_values, tile_keys, tile_values, slot_live)
    )
    return stacked.transpose(0, 2, 1, 3).reshape(rows_here, QH * HD)


def solution(mesh):
    return jax.shard_map(
        on_device,
        mesh=mesh,
        in_specs=(
            P("ctx", "head"),
            P(("ctx", "head"), None),
            P(("ctx", "head"), None),
            P("head", None, None),
        ),
        out_specs=P("ctx", "head"),
        check_vma=False,
    )
```

profile of v0, /device:TPU:0, one launch (start us, length us, event | category | flops | bytes accessed | tf_op | source)
XLA Modules:
  0.0 120.1 jit_solution(6310541799460549363)
XLA Ops:
  6.5 1.1 copy.21
  7.6 8.5 %all_to_all.38 = bf16[256,2,128]{0,2,1:T(8,128)(2,1)S(1)} all-to-all(bf16[256,2,128]{0,2,1:T(8,128)(2,1)S(1)} %bitcast.62), channel_id=1, replica_groups=mesh['head'=2,'ctx'=16] {'head'}, dimensions={1} | all-to-all | bytes 262144 | tf_op jit(solution)/shard_map/all_to_all | solution.py:42
  16.1 0.8 copy.22
  16.9 1.0 copy.24
  17.9 6.8 %all_to_all.39 = bf16[256,2,128]{0,2,1:T(8,128)(2,1)S(1)} all-to-all(bf16[256,2,128]{0,2,1:T(8,128)(2,1)S(1)} %bitcast.63), channel_id=1, replica_groups=mesh['head'=2,'ctx'=16] {'head'}, dimensions={1} | all-to-all | bytes 262144 | tf_op jit(solution)/shard_map/all_to_all | solution.py:43
  24.8 0.8 copy.25
  26.4 0.9 copy.28
  27.6 31.1 %all-gather.3.cloned.1.call-done = bf16[8192,128]{1,0:T(8,128)(2,1)} async-done(((bf16[512,128]{1,0:T(8,128)(2,1)}), bf16[8192,128]{1,0:T(8,128)(2,1)}) %all-gather.3.cloned.1.call-update) | async-done | bytes 2097168 | tf_op jit(solution)/shard_map/all_gather | solution.py:55
  58.8 2.2 %gather_fusion = bf16[2,512,128]{2,1,0:T(8,128)(2,1)S(1)} fusion(bf16[16,512,128]{2,1,0:T(8,128)(2,1)} %bitcast.65, s32[1024]{0:T(1024)S(1)} %pad_clamp_fusion), kind=kCustom, calls=%fused_computation | custom fusion | bytes 524296 | tf_op jit(solution)/shard_map/gather | solution.py:60
  60.9 40.2 %all-gather.5.cloned.1.call-done = bf16[8192,128]{1,0:T(8,128)(2,1)} async-done(((bf16[512,128]{1,0:T(8,128)(2,1)}), bf16[8192,128]{1,0:T(8,128)(2,1)}) %all-gather.5.cloned.1.call-update) | async-done | bytes 2097168 | tf_op jit(solution)/shard_map/all_gather | solution.py:56
  101.1 2.2 %gather_fusion.1 = bf16[2,512,128]{2,1,0:T(8,128)(2,1)S(1)} fusion(bf16[16,512,128]{2,1,0:T(8,128)(2,1)} %bitcast.66, s32[1024]{0:T(1024)S(1)} %pad_clamp_fusion), kind=kCustom, calls=%fused_computation.1 | custom fusion | bytes 524296 | tf_op jit(solution)/shard_map/gather | solution.py:61
  103.4 8.5 %while.17 = (s32[]{:T(128)}, bf16[4,512,128]{2,1,0:T(8,128)(2,1)S(1)}, bf16[4,512,128]{1,2,0:T(8,128)(2,1)S(1)}, bf16[1536,128]{1,0:T(8,128)(2,1)S(1)}, pred[512...) while((s32[]{:T(128)}, bf16[4,512,128]{2,1,0:T(8,128)(2,1)S(1)}, ...), condition=%wide.region_3.4_spmd, body=%wide.region_0.3_spmd.sunk | while | flops 408288256 | bytes 11282517 | solution.py:37
  103.4 0.8 fusion.34
  104.3 0.6 fusion.35
  104.8 0.7 fusion.36
  105.6 0.8 fusion.34
  106.4 0.6 fusion.35
  107.0 0.7 fusion.36
  107.7 0.8 fusion.34
  108.5 0.6 fusion.35
  109.1 0.7 fusion.36
  109.8 0.8 fusion.34
  111.2 0.7 fusion.36
  112.3 0.9 copy.33
  (25 shorter events, 2.2 us)
Async XLA Ops:
  6.5 19.0 %copy-start = (s32[1,16,3]{1,0,2:T(1,128)S(1)}, s32[1,16,3]{1,0,2:T(1,128)}, u32[]{:S(2)}) copy-start(s32[1,16,3]{1,0,2:T(1,128)} %param.9) | copy-start | bytes 580
  6.5 20.8 %copy-start.3 = (bf16[512,512]{1,0:T(8,128)(2,1)S(1)}, bf16[512,512]{1,0:T(8,128)(2,1)}, u32[]{:S(2)}) copy-start(bf16[512,512]{1,0:T(8,128)(2,1)} %param.6) | copy-start | bytes 1572868
  6.5 52.2 %all-gather.3.cloned.1.call-start = ((), (), s32[]{:S(2)}) async-start(), calls=%async_computation.2 | async-start | bytes 2228224 | tf_op jit(solution)/shard_map/all_gather | solution.py:55
  16.8 86.5 %copy-start.1 = (bf16[2,256,128]{2,1,0:T(8,128)(2,1)S(1)}, bf16[2,256,128]{2,1,0:T(8,128)(2,1)}, u32[]{:S(2)}) copy-start(bf16[2,256,128]{2,1,0:T(8,128)(2,1)} %copy.22) | copy-start | bytes 393220
  16.9 84.2 %all-gather.5.cloned.1.call-start = ((), (), s32[]{:S(2)}) async-start(), calls=%async_computation.3 | async-start | bytes 2228224 | tf_op jit(solution)/shard_map/all_gather | solution.py:56
  25.5 77.8 %copy-start.2 = (bf16[2,256,128]{2,1,0:T(8,128)(2,1)S(1)}, bf16[2,256,128]{2,1,0:T(8,128)(2,1)}, u32[]{:S(2)}) copy-start(bf16[2,256,128]{2,1,0:T(8,128)(2,1)} %copy.25) | copy-start | bytes 393220
Sparse Core Ops, SparseCore 0:
  17.0 41.7 all-gather.2
  60.9 40.1 all-gather.4
where the time goes:
time: 120 us
  waiting for transfers between devices  71.3 us (59%)
  blocking collectives  15.3 us (13%)
  between operations  13.5 us (11%)
  local copies, waits for them, and re-layouts  10.6 us (9%)
  matrix products  6.15 us (5%)
  other arithmetic  2.95 us (2%)
    all_gather x1, waiting for transfers between devices, on_device(): lax.all_gather(value_local, 'ctx', axis=0, tiled=True)  40.2 us
    all_gather x1, waiting for transfers between devices, on_device(): lax.all_gather(key_local, 'ctx', axis=0, tiled=True)  31.1 us
    all_to_all x1, blocking collectives, on_device(): lax.all_to_all(keys, 'head', split_axis=1, concat_axis=0, tiled=True)  8.48 us
    all_to_all x1, blocking collectives, on_device(): lax.all_to_all(values, 'head', split_axis=1, concat_axis=0, tiled=True)  6.85 us
    dot_general x4, matrix products, per_head(): jnp.einsum('qd,kd->qk', query_head, key_rows, preferred_element_type=jnp....  3.31 us
    unnamed x12, local copies, waits for them, and re-layouts  3.17 us
    dot_general x4, matrix products, per_head(): jnp.dot(weights.astype(jnp.bfloat16), value_rows, preferred_element_type=...  2.84 us
  transfers between devices with their start and end apart: 2, of which 2 were waited for; matrix products, arithmetic and copies ran while one was open for 5% of the time, Pallas kernels for 0%

commit v1 on v0

v1 whole, which is shorter than its diff:
```python
import functools
import math

import jax
import jax.numpy as jnp
from jax import lax
from jax.experimental import pallas as pl
from jax.experimental.pallas import tpu as pltpu
from jax.sharding import PartitionSpec as P

HD = 128
QH = 4
BLK = 512
CHUNK = 256


def pick_kernel(lists_ref, pieces_ref, out_ref):
    receivers, _, picks, parts, rows, _ = out_ref.shape

    def one(receiver, carry):
        for s in range(picks):
            block = lists_ref[receiver, s + 1]
            for part in range(parts):
                for kv in range(2):
                    out_ref[receiver, kv, s, part] = pieces_ref[part, block, kv]
        return carry

    lax.fori_loop(0, receivers, one, 0, unroll=4)


def pick_pieces(lists, pieces, receivers, picks):
    parts, _, _, rows, _ = pieces.shape
    return pl.pallas_call(
        pick_kernel,
        out_shape=jax.ShapeDtypeStruct((receivers, 2, picks, parts, rows, HD), pieces.dtype),
        in_specs=[
            pl.BlockSpec(memory_space=pltpu.SMEM),
            pl.BlockSpec(memory_space=pltpu.VMEM),
        ],
        out_specs=pl.BlockSpec(memory_space=pltpu.VMEM),
    )(lists, pieces)


def scores_of(query_rows, key_rows):
    return lax.dot_general(
        query_rows, key_rows, (((1,), (1,)), ((), ())), preferred_element_type=jnp.float32
    )


def attend_kernel(live_ref, query_ref, own_key_ref, own_value_ref, far_ref, out_ref):
    factor = math.log2(math.e) / math.sqrt(HD)
    picks = far_ref.shape[2]
    far_rows = (BLK, HD)
    far_keys = [far_ref[:, 0, s].reshape(far_rows) for s in range(picks)]
    far_values = [far_ref[:, 1, s].reshape(far_rows) for s in range(picks)]
    for begin in range(0, BLK, CHUNK):
        end = begin + CHUNK
        query_rows = query_ref[begin:end, :]
        near = scores_of(query_rows, own_key_ref[0:end, :])
        row_ids = lax.broadcasted_iota(jnp.int32, near.shape, 0) + begin
        col_ids = lax.broadcasted_iota(jnp.int32, near.shape, 1)
        near = jnp.where(row_ids >= col_ids, near, -jnp.inf)
        pieces = [near]
        for s in range(picks):
            far = scores_of(query_rows, far_keys[s])
            pieces.append(jnp.where(live_ref[s] > 0, far, -jnp.inf))
        top = functools.reduce(
            jnp.maximum, [jnp.max(piece, axis=1, keepdims=True) for piece in pieces]
        )
        weights = [jnp.exp2((piece - top) * factor) for piece in pieces]
        total = sum(jnp.sum(weight, axis=1, keepdims=True) for weight in weights)
        value_parts = [own_value_ref[0:end, :]] + far_values
        product = sum(
            jnp.dot(weight.astype(jnp.bfloat16), value, preferred_element_type=jnp.float32)
            for weight, value in zip(weights, value_parts)
        )
        out_ref[begin:end, :] = (product / total).astype(out_ref.dtype)


def attend(live, queries, own_keys, own_values, far):
    rows, columns = queries.shape
    whole = lambda shape: pl.BlockSpec(shape, lambda h: (0,) * len(shape))
    return pl.pallas_call(
        attend_kernel,
        grid=(columns // HD,),
        out_shape=jax.ShapeDtypeStruct(queries.shape, queries.dtype),
        in_specs=[
            pl.BlockSpec(memory_space=pltpu.SMEM),
            pl.BlockSpec((rows, HD), lambda h: (0, h)),
            whole(own_keys.shape),
            whole(own_values.shape),
            whole(far.shape),
        ],
        out_specs=pl.BlockSpec((rows, HD), lambda h: (0, h)),
        compiler_params=pltpu.CompilerParams(vmem_limit_bytes=48 * 1024 * 1024),
    )(live, queries, own_keys, own_values, far)


def on_device(heads, ranks, queries, keys, values, selected):
    lists = selected[0]
    picks = lists.shape[1] - 1
    head_rank = lax.axis_index("head")
    ctx_rank = lax.axis_index("ctx")
    held = keys.shape[0]
    share = held // ranks

    local = jnp.stack([keys, values]).reshape(2, held, heads, HD)

    by_head = local.transpose(2, 0, 1, 3)
    if heads == 2:
        mine = lax.dynamic_index_in_dim(by_head, head_rank, 0, keepdims=False)
        other = lax.dynamic_index_in_dim(by_head, 1 - head_rank, 0, keepdims=False)
        came = lax.ppermute(other, "head", [(0, 1), (1, 0)])
        own = jnp.where(
            head_rank == 0,
            jnp.concatenate([mine, came], axis=1),
            jnp.concatenate([came, mine], axis=1),
        )
    else:
        own = lax.all_to_all(by_head, "head", split_axis=0, concat_axis=0, tiled=True)
        own = own.transpose(1, 0, 2, 3).reshape(2, BLK, HD)

    spread = local.reshape(2, ranks, share, heads, HD).transpose(3, 1, 0, 2, 4)
    spread = spread.reshape(heads * ranks, 2, share, HD)
    spread = lax.all_to_all(spread, ("head", "ctx"), split_axis=0, concat_axis=0, tiled=True)
    spread = spread.reshape(heads, ranks, 2, share, HD)
    if share % 16:
        spread = spread.transpose(1, 2, 0, 3, 4).reshape(1, ranks, 2, heads * share, HD)

    far = pick_pieces(lists, spread, ranks, picks)
    far = lax.all_to_all(far, "ctx", split_axis=0, concat_axis=0, tiled=True)
    far = far.reshape(ranks, 2, picks, -1, HD)

    chosen = lax.dynamic_index_in_dim(lists, ctx_rank, 0, keepdims=False)[1:]
    live = (chosen != ctx_rank).astype(jnp.int32)
    return attend(live, queries, own[0], own[1], far)


def solution(mesh):
    return jax.shard_map(
        functools.partial(on_device, mesh.shape["head"], mesh.shape["ctx"]),
        mesh=mesh,
        in_specs=(
            P("ctx", "head"),
            P(("ctx", "head"), None),
            P(("ctx", "head"), None),
            P("head", None, None),
        ),
        out_specs=P("ctx", "head"),
        check_vma=False,
    )
```

time: 120 us -> 47.7 us (0.40)
  waiting for transfers between devices: 71.3 us -> 22 us
  blocking collectives: 15.3 us -> 0 us
  between operations: 13.5 us -> 0.1 us
  starting transfers between devices: 0.04 us -> 11.7 us
  Pallas kernels: 0 us -> 8.87 us
  local copies, waits for them, and re-layouts: 10.6 us -> 4 us
  matrix products: 6.15 us -> 0 us
  other arithmetic: 2.95 us -> 0.64 us
    all_gather x2 -> x0, waiting for transfers between devices: 71.3 us -> none  [the longest x1 40.2 us: on_device(): lax.all_gather(value_local, 'ctx', axis=0, tiled=True)]
    all_to_all x0 -> x2, waiting for transfers between devices: none -> 17.2 us  [the longest x1 8.82 us: on_device(): lax.all_to_all(spread, ('head', 'ctx'), split_axis=0, concat_axis=0, tile...]
    all_to_all x2 -> x0, blocking collectives: 15.3 us -> none  [the longest x1 8.48 us: on_device(): lax.all_to_all(keys, 'head', split_axis=1, concat_axis=0, tiled=True)]
    all_to_all x0 -> x2, starting transfers between devices: none -> 10.9 us  [the longest x1 7.3 us: on_device(): lax.all_to_all(spread, ('head', 'ctx'), split_axis=0, concat_axis=0, tile...]
    pallas_call x0 -> x2, Pallas kernels: none -> 8.87 us  [the longest x1 7.06 us: attend(): pl.pallas_call(attend_kernel, grid=(columns // HD,), out_shape=jax.ShapeD...]
    dot_general x8 -> x0, matrix products: 6.15 us -> none  [the longest x4 3.31 us: per_head(): jnp.einsum('qd,kd->qk', query_head, key_rows, preferred_element_type=jnp....]
    ppermute x0 -> x1, waiting for transfers between devices: none -> 4.84 us  [on_device(): came = lax.ppermute(other, 'head', [(0, 1), (1, 0)])]
    gather x2 -> x0, local copies, waits for them, and re-layouts: 4.37 us -> none  [the longest x1 2.19 us: on_device(): tile_values = full_values[own_lists[:, 1:]]]
  transfers between devices with their start and end apart: 2 -> 3, of which waited for: 2 -> 3; matrix products, arithmetic and copies ran while one was open for 5% -> 2% of each run, Pallas kernels for 0% -> 0%
where the time goes in v1:
time: 47.7 us; the launch traced here: 47.3 us
  waiting for transfers between devices  22 us (46%)
  starting transfers between devices  11.7 us (25%)
  Pallas kernels  8.87 us (19%)
  local copies, waits for them, and re-layouts  4 us (8%)
  other arithmetic  0.64 us (1%)
    all_to_all x1, waiting for transfers between devices, on_device(): lax.all_to_all(spread, ('head', 'ctx'), split_axis=0, concat_axis=0, tile...  8.82 us
    all_to_all x1, waiting for transfers between devices, on_device(): far = lax.all_to_all(far, 'ctx', split_axis=0, concat_axis=0, tiled=True)  8.38 us
    all_to_all x1, starting transfers between devices, on_device(): lax.all_to_all(spread, ('head', 'ctx'), split_axis=0, concat_axis=0, tile...  7.3 us
    pallas_call x1, Pallas kernels, attend(): pl.pallas_call(attend_kernel, grid=(columns // HD,), out_shape=jax.ShapeD...  7.06 us
    ppermute x1, waiting for transfers between devices, on_device(): came = lax.ppermute(other, 'head', [(0, 1), (1, 0)])  4.84 us
    all_to_all x1, starting transfers between devices, on_device(): far = lax.all_to_all(far, 'ctx', split_axis=0, concat_axis=0, tiled=True)  3.58 us
    pallas_call x1, Pallas kernels, pick_pieces(): pl.pallas_call(pick_kernel, out_shape=jax.ShapeDtypeStruct((receivers, 2,...  1.81 us
    unnamed x11, local copies, waits for them, and re-layouts  1.4 us
  transfers between devices with their start and end apart: 3, of which 3 were waited for; matrix products, arithmetic and copies ran while one was open for 2% of the time, Pallas kernels for 0%

profile of v1, /device:TPU:0, one launch (start us, length us, event | category | flops | bytes accessed | tf_op | source)
XLA Modules:
  0.0 47.3 jit_solution(1109159248656479969)
XLA Ops:
  0.0 0.0 copy-start.3
  0.0 1.0 %stack.18 = bf16[1,16,16,2,128]{4,3,2,1,0:T(2,128)(2,1)S(1)} reshape(bf16[256,256]{1,0:T(8,128)(2,1)} %param.5) | data formatting | bytes 262144 | tf_op jit(solution)/shard_map/stack | solution.py:107
  1.0 0.0 copy-done.3
  1.0 0.4 maximum_bitcast_fusion
  1.4 0.7 %copy.11 = bf16[2,16,2,16,128]{4,3,2,1,0:T(8,128)(2,1)} copy(bf16[2,16,2,16,128]{4,0,3,1,2:T(2,128)(2,1)S(1)} %maximum_bitcast_fusion) | data formatting | bytes 524288 | tf_op jit(solution)/shard_map/transpose | solution.py:123
  2.1 0.0 copy-start.2
  2.2 7.3 %all-to-all-start = ((bf16[32,2,16,128]{3,2,1,0:T(8,128)(2,1)}), bf16[32,2,16,128]{3,2,1,0:T(8,128)(2,1)S(1)}, u32[]{:S(2)}, u32[]{:S(2)}) async-start(bf16[32,2,16,128]{3,2,1,0:T(8,128)(2,1)} %bitcast.6), calls=%async_computation | async-start | bytes 524288 | tf_op jit(solution)/shard_map/all_to_all | solution.py:125
  9.5 0.0 copy-done.2
  9.6 0.0 copy-start.4
  9.6 0.7 %copy-done.4 = s32[1,16,3]{1,0,2:T(1,128)S(1)} copy-done((s32[1,16,3]{1,0,2:T(1,128)S(1)}, s32[1,16,3]{1,0,2:T(1,128)}, u32[]{:S(2)}) %copy-start.4) | copy-done | bytes 216
  10.2 0.7 %copy.13 = s32[1,16,3]{2,1,0:T(8,128)} copy(s32[1,16,3]{1,0,2:T(1,128)S(1)} %copy-done.4) | data formatting | bytes 384 | tf_op jit(solution)/shard_map/squeeze | solution.py:100
  10.9 8.8 %all-to-all-done = bf16[32,2,16,128]{3,2,1,0:T(8,128)(2,1)S(1)} async-done(((bf16[32,2,16,128]{3,2,1,0:T(8,128)(2,1)}), bf16[32,2,16,128]{3,2,1,0:T(8,128)(2,1)S(1)}, u32[]{:S(2)}, u32[]{:S(2)}) %all-to-all-start) | async-done | bytes 262176 | tf_op jit(solution)/shard_map/all_to_all | solution.py:125
  19.7 0.0 copy-start.1
  19.7 0.7 %copy-done.1 = bf16[32,2,16,128]{3,2,1,0:T(8,128)(2,1)} copy-done((bf16[32,2,16,128]{3,2,1,0:T(8,128)(2,1)}, bf16[32,2,16,128]{3,2,1,0:T(8,128)(2,1)S(1)}, u32[]{:S(2)}) %copy-start.1) | copy-done | bytes 262168
  20.4 1.8 %shard_map.46 = bf16[16,2,2,2,16,128]{5,4,3,2,1,0:T(8,128)(2,1)} custom-call(s32[16,3]{1,0:T(8,128)} %bitcast.16, bf16[2,16,2,16,128]{4,3,2,1,0:T(8,128)(2,1)} %bitcast.15), custom_call_target="tpu_custom_call" | custom-call | tf_op jit(solution)/shard_map/pallas_call | solution.py:33
  22.3 3.6 %all-to-all-start.1 = ((bf16[16,2,2,2,16,128]{5,4,3,2,1,0:T(8,128)(2,1)}), bf16[16,2,2,2,16,128]{5,4,3,2,1,0:T(8,128)(2,1)S(1)}, u32[]{:S(2)}, u32[]{:S(2)}) async-start(bf16[16,2,2,2,16,128]{5,4,3,2,1,0:T(8,128)(2,1)} %shard_map.46), calls=%async_computation.1 | async-start | bytes 1048576 | tf_op jit(solution)/shard_map/all_to_all | solution.py:131
  25.9 0.8 %collective-permute-start = (bf16[2,256,128]{2,1,0:T(8,128)(2,1)S(1)}, bf16[2,256,128]{2,1,0:T(8,128)(2,1)S(1)}, u32[]{:S(2)}, u32[]{:S(2)}) collective-permute-start(bf16[2,256,128]{2,1,0:T(8,128)(2,1)S(1)} %get-tuple-element.8), channel_id=1, source_target_pairs={{0,16},{16,0},{1,17},{17,1},{2,18},{18,2},{3,19},{19,3},{4,20},{20... | collective-permute-start | bytes 393224 | tf_op jit(solution)/shard_map/ppermute | solution.py:113
  26.8 0.2 fusion.live_ref
  26.9 4.8 %collective-permute-done = bf16[2,256,128]{2,1,0:T(8,128)(2,1)S(1)} collective-permute-done((bf16[2,256,128]{2,1,0:T(8,128)(2,1)S(1)}, bf16[2,256,128]{2,1,0:T(8,128)(2,1)S(1)}, u32[]{:S(2)}, u32[]{:S(2)}) %collective-permute-start) | collective-permute-done | bytes 131104 | tf_op jit(solution)/shard_map/ppermute | solution.py:113
  31.8 0.0 copy-start
  31.8 0.1 maximum_select_fusion
  31.9 8.4 %all-to-all-done.1 = bf16[16,2,2,2,16,128]{5,4,3,2,1,0:T(8,128)(2,1)S(1)} async-done(((bf16[16,2,2,2,16,128]{5,4,3,2,1,0:T(8,128)(2,1)}), bf16[16,2,2,2,16,128]{5,4,3,2,1,0:T(8,128)(2,1)S(1)}, u32[]{:S(2)}, u32[]{:S(2)}) %all-to-all-start.1) | async-done | bytes 524320 | tf_op jit(solution)/shard_map/all_to_all | solution.py:131
  40.3 0.0 copy-done
  40.3 7.1 %shard_map.47 = bf16[512,512]{1,0:T(8,128)(2,1)} custom-call(s32[2]{0:T(128)S(1)} %fusion.live_ref, bf16[512,512]{1,0:T(8,128)(2,1)S(1)} %copy-done, bf16[512,128]{1,0:T(8,128)(2,1)S(1)} %get-tuple-element.6.own_key_ref, bf16[512,128]{1,0:T(8,128)(2,1)S(1)} %get-tuple-element.5.own_value_ref, bf16[16,2,2,32,128]{4,3,2,1,0:T(8,128)(2,1)S(1)} %bitcast.14), custom_call_target="tpu_custom_call" | custom-call | tf_op jit(solution)/shard_map/pallas_call | solution.py:83
  (7 shorter events, 0.2 us)
Async XLA Ops:
  0.0 1.0 %copy-start.3 = (bf16[256,256]{1,0:T(8,128)(2,1)S(1)}, bf16[256,256]{1,0:T(8,128)(2,1)}, u32[]{:S(2)}) copy-start(bf16[256,256]{1,0:T(8,128)(2,1)} %param.6) | copy-start | bytes 393220
  2.1 7.3 %copy-start.2 = (bf16[256,256]{1,0:T(8,128)(2,1)S(1)}, bf16[256,256]{1,0:T(8,128)(2,1)}, u32[]{:S(2)}) copy-start(bf16[256,256]{1,0:T(8,128)(2,1)} %param.5) | copy-start | bytes 393220
  2.2 17.6 %all-to-all-start = ((bf16[32,2,16,128]{3,2,1,0:T(8,128)(2,1)}), bf16[32,2,16,128]{3,2,1,0:T(8,128)(2,1)S(1)}, u32[]{:S(2)}, u32[]{:S(2)}) async-start(bf16[32,2,16,128]{3,2,1,0:T(8,128)(2,1)} %bitcast.6), calls=%async_computation | async-start | bytes 524288 | tf_op jit(solution)/shard_map/all_to_all | solution.py:125
  9.6 0.7 %copy-start.4 = (s32[1,16,3]{1,0,2:T(1,128)S(1)}, s32[1,16,3]{1,0,2:T(1,128)}, u32[]{:S(2)}) copy-start(s32[1,16,3]{1,0,2:T(1,128)} %param.7) | copy-start | bytes 580
  19.7 0.7 %copy-start.1 = (bf16[32,2,16,128]{3,2,1,0:T(8,128)(2,1)}, bf16[32,2,16,128]{3,2,1,0:T(8,128)(2,1)S(1)}, u32[]{:S(2)}) copy-start(bf16[32,2,16,128]{3,2,1,0:T(8,128)(2,1)S(1)} %all-to-all-done) | copy-start | bytes 786436
  22.3 18.0 %all-to-all-start.1 = ((bf16[16,2,2,2,16,128]{5,4,3,2,1,0:T(8,128)(2,1)}), bf16[16,2,2,2,16,128]{5,4,3,2,1,0:T(8,128)(2,1)S(1)}, u32[]{:S(2)}, u32[]{:S(2)}) async-start(bf16[16,2,2,2,16,128]{5,4,3,2,1,0:T(8,128)(2,1)} %shard_map.46), calls=%async_computation.1 | async-start | bytes 1048576 | tf_op jit(solution)/shard_map/all_to_all | solution.py:131
  25.9 5.8 %collective-permute-start = (bf16[2,256,128]{2,1,0:T(8,128)(2,1)S(1)}, bf16[2,256,128]{2,1,0:T(8,128)(2,1)S(1)}, u32[]{:S(2)}, u32[]{:S(2)}) collective-permute-start(bf16[2,256,128]{2,1,0:T(8,128)(2,1)S(1)} %get-tuple-element.8), channel_id=1, source_target_pairs={{0,16},{16,0},{1,17},{17,1},{2,18},{18,2},{3,19},{19,3},{4,20},{20... | collective-permute-start | bytes 393224 | tf_op jit(solution)/shard_map/ppermute | solution.py:113
  31.8 8.5 %copy-start = (bf16[512,512]{1,0:T(8,128)(2,1)S(1)}, bf16[512,512]{1,0:T(8,128)(2,1)}, u32[]{:S(2)}) copy-start(bf16[512,512]{1,0:T(8,128)(2,1)} %query_ref.1) | copy-start | bytes 1572868

commit v2 on v1

v2 whole, which is shorter than its diff:
```python
import functools
import math

import jax
import jax.numpy as jnp
from jax import lax
from jax.experimental import pallas as pl
from jax.experimental.pallas import tpu as pltpu
from jax.sharding import PartitionSpec as P

HD = 128
BLK = 512
CHUNK = 256
FACTOR = math.log2(math.e) / math.sqrt(HD)
SMALL = pltpu.CompilerParams(vmem_limit_bytes=4 * 1024 * 1024)
LARGE = pltpu.CompilerParams(vmem_limit_bytes=24 * 1024 * 1024)
VMEM = pl.BlockSpec(memory_space=pltpu.VMEM)
SMEM = pl.BlockSpec(memory_space=pltpu.SMEM)


def spread_kernel(key_ref, value_ref, out_ref):
    peers, _, share, _ = out_ref.shape
    ranks = key_ref.shape[0] // share
    for kv, ref in enumerate((key_ref, value_ref)):
        for h in range(peers // ranks):
            columns = ref[:, h * HD : (h + 1) * HD]
            out_ref[h * ranks : (h + 1) * ranks, kv] = columns.reshape(ranks, share, HD)


def spread_rows(keys, values, heads, ranks):
    held = keys.shape[0]
    share = held // ranks
    if share % 16 == 0:
        return pl.pallas_call(
            spread_kernel,
            out_shape=jax.ShapeDtypeStruct((heads * ranks, 2, share, HD), keys.dtype),
            in_specs=[VMEM, VMEM],
            out_specs=VMEM,
            compiler_params=SMALL,
        )(keys, values)
    both = jnp.stack([keys, values]).reshape(2, ranks, share, heads, HD)
    return both.transpose(3, 1, 0, 2, 4).reshape(heads * ranks, 2, share, HD)


def pick_kernel(lists_ref, pieces_ref, out_ref):
    receivers, _, picks, parts, _, _ = out_ref.shape

    def one(receiver, carry):
        for s in range(picks):
            block = lists_ref[receiver, s + 1]
            for part in range(parts):
                for kv in range(2):
                    out_ref[receiver, kv, s, part] = pieces_ref[part, block, kv]
        return carry

    lax.fori_loop(0, receivers, one, 0, unroll=4)


def pick_pieces(lists, pieces, receivers, picks):
    parts, _, _, rows, _ = pieces.shape
    return pl.pallas_call(
        pick_kernel,
        out_shape=jax.ShapeDtypeStruct((receivers, 2, picks, parts, rows, HD), pieces.dtype),
        in_specs=[SMEM, VMEM],
        out_specs=VMEM,
        compiler_params=SMALL,
    )(lists, pieces)


def split_queries(query_rows):
    scaled = query_rows.astype(jnp.float32) * FACTOR
    high = scaled.astype(jnp.bfloat16)
    low = (scaled - high.astype(jnp.float32)).astype(jnp.bfloat16)
    return jnp.concatenate([high, low], axis=1)


def units_of(columns):
    return [(h, begin) for h in range(columns // HD) for begin in range(0, BLK, CHUNK)]


def in_turn(units, score, finish):
    held = score(*units[0])
    for i, unit in enumerate(units):
        later = score(*units[i + 1]) if i + 1 < len(units) else None
        finish(*unit, held)
        held = later


def near_kernel(query_ref, key_ref, value_ref, top_ref, sum_ref, acc_ref, turned):
    turned[:HD] = key_ref[...].T
    turned[HD:] = turned[:HD]
    values = jnp.concatenate([value_ref[...], jnp.ones(value_ref.shape, jnp.bfloat16)], axis=1)

    def score(h, begin):
        query_rows = split_queries(query_ref[begin : begin + CHUNK, h * HD : (h + 1) * HD])
        end = begin + CHUNK
        scores = jnp.dot(query_rows, turned[:, :end], preferred_element_type=jnp.float32)
        row_ids = lax.broadcasted_iota(jnp.int32, scores.shape, 0) + begin
        col_ids = lax.broadcasted_iota(jnp.int32, scores.shape, 1)
        return jnp.where(row_ids >= col_ids, scores, -jnp.inf)

    def finish(h, begin, scores):
        rows = slice(begin, begin + CHUNK)
        top = jnp.max(scores, axis=1, keepdims=True)
        weights = jnp.exp2(scores - top).astype(jnp.bfloat16)
        product = jnp.dot(weights, values[: begin + CHUNK], preferred_element_type=jnp.float32)
        top_ref[h, rows] = jnp.broadcast_to(top, (CHUNK, HD))
        sum_ref[h, rows] = product[:, HD:]
        acc_ref[h, rows] = product[:, :HD]

    in_turn(units_of(query_ref.shape[1]), score, finish)


def attend_near(queries, own_keys, own_values):
    rows, columns = queries.shape
    part = jax.ShapeDtypeStruct((columns // HD, rows, HD), jnp.float32)
    return pl.pallas_call(
        near_kernel,
        out_shape=[part, part, part],
        in_specs=[VMEM] * 3,
        out_specs=[VMEM] * 3,
        scratch_shapes=[pltpu.VMEM((2 * HD, BLK), jnp.bfloat16)],
        compiler_params=LARGE,
        cost_estimate=pl.CostEstimate(
            flops=4 * columns * rows * BLK, bytes_accessed=4 << 20, transcendentals=0
        ),
    )(queries, own_keys, own_values)


def far_kernel(
    live_ref, query_ref, key_ref, far_ref, top_ref, sum_ref, acc_ref, out_ref, turned, valued
):
    picks = far_ref.shape[2]
    spare = jnp.broadcast_to(key_ref[0:1, :], (BLK, HD))
    for s in range(picks):
        rows = slice(s * BLK, (s + 1) * BLK)
        live = live_ref[s] > 0
        key_rows = jnp.where(live, far_ref[:, 0, s].reshape(BLK, HD), spare)
        value_rows = far_ref[:, 1, s].reshape(BLK, HD)
        turned[:HD, rows] = key_rows.T
        valued[rows, :HD] = jnp.where(live, value_rows, jnp.zeros_like(value_rows))
        valued[rows, HD:] = jnp.where(
            live, jnp.ones_like(value_rows), jnp.zeros_like(value_rows)
        )
    turned[HD:] = turned[:HD]

    def score(h, begin):
        query_rows = split_queries(query_ref[begin : begin + CHUNK, h * HD : (h + 1) * HD])
        return jnp.dot(query_rows, turned[...], preferred_element_type=jnp.float32)

    def finish(h, begin, scores):
        rows = slice(begin, begin + CHUNK)
        near_top = top_ref[h, rows]
        top = jnp.maximum(jnp.max(scores, axis=1, keepdims=True), near_top[:, :1])
        weights = jnp.exp2(scores - top).astype(jnp.bfloat16)
        product = jnp.dot(weights, valued[...], preferred_element_type=jnp.float32)
        scale = jnp.exp2(near_top - top)
        total = product[:, HD:] + sum_ref[h, rows] * scale
        product = product[:, :HD] + acc_ref[h, rows] * scale
        out_ref[rows, h * HD : (h + 1) * HD] = (product / total).astype(out_ref.dtype)

    in_turn(units_of(query_ref.shape[1]), score, finish)


def attend_far(live, queries, own_keys, far, near):
    keys_here = far.shape[2] * BLK
    return pl.pallas_call(
        far_kernel,
        out_shape=jax.ShapeDtypeStruct(queries.shape, queries.dtype),
        in_specs=[SMEM] + [VMEM] * 6,
        out_specs=VMEM,
        scratch_shapes=[
            pltpu.VMEM((2 * HD, keys_here), jnp.bfloat16),
            pltpu.VMEM((keys_here, 2 * HD), jnp.bfloat16),
        ],
        compiler_params=LARGE,
    )(live, queries, own_keys, far, *near)


def own_block(keys, values, heads, head_rank):
    if heads == 2:
        columns = lambda rank: jnp.stack(
            [lax.dynamic_slice_in_dim(x, rank * HD, HD, 1) for x in (keys, values)]
        )
        mine = columns(head_rank)
        came = lax.ppermute(columns(1 - head_rank), "head", [(0, 1), (1, 0)])
        return jnp.where(
            head_rank == 0,
            jnp.concatenate([mine, came], axis=1),
            jnp.concatenate([came, mine], axis=1),
        )
    by_head = jnp.stack([keys, values]).reshape(2, -1, heads, HD).transpose(2, 0, 1, 3)
    own = lax.all_to_all(by_head, "head", split_axis=0, concat_axis=0, tiled=True)
    return own.transpose(1, 0, 2, 3).reshape(2, BLK, HD)


def on_device(heads, ranks, queries, keys, values, selected):
    lists = selected[0]
    picks = lists.shape[1] - 1
    head_rank = lax.axis_index("head")
    ctx_rank = lax.axis_index("ctx")
    share = keys.shape[0] // ranks

    spread = spread_rows(keys, values, heads, ranks)
    spread = lax.all_to_all(spread, ("head", "ctx"), split_axis=0, concat_axis=0, tiled=True)
    spread = spread.reshape(heads, ranks, 2, share, HD)
    if share % 16:
        spread = spread.transpose(1, 2, 0, 3, 4).reshape(1, ranks, 2, heads * share, HD)

    far = pick_pieces(lists, spread, ranks, picks)
    far = lax.all_to_all(far, "ctx", split_axis=0, concat_axis=0, tiled=True)
    far = far.reshape(ranks, 2, picks, -1, HD)

    own = own_block(keys, values, heads, head_rank)
    near = attend_near(queries, own[0], own[1])

    chosen = lax.dynamic_index_in_dim(lists, ctx_rank, 0, keepdims=False)[1:]
    live = (chosen != ctx_rank).astype(jnp.int32)
    return attend_far(live, queries, own[0], far, near)


def solution(mesh):
    return jax.shard_map(
        functools.partial(on_device, mesh.shape["head"], mesh.shape["ctx"]),
        mesh=mesh,
        in_specs=(
            P("ctx", "head"),
            P(("ctx", "head"), None),
            P(("ctx", "head"), None),
            P("head", None, None),
        ),
        out_specs=P("ctx", "head"),
        check_vma=False,
    )
```

time: 47.7 us -> 45.8 us (0.960)
  waiting for transfers between devices: 22 us -> 20.3 us
  local copies, waits for them, and re-layouts: 4 us -> 5.09 us
  Pallas kernels: 8.87 us -> 7.84 us
    unnamed x11 -> x16, local copies, waits for them, and re-layouts: 1.4 us -> 4.94 us
    all_to_all x1, waiting for transfers between devices: 8.38 us -> 5.26 us  [on_device(): far = lax.all_to_all(far, 'ctx', split_axis=0, concat_axis=0, tiled=True)]
    all_to_all x1, waiting for transfers between devices: 8.82 us -> 10.2 us  [on_device(): lax.all_to_all(spread, ('head', 'ctx'), split_axis=0, concat_axis=0, tile...]
    another operation x5 -> x1, local copies, waits for them, and re-layouts: 1.13 us -> 0.05 us  [own_block(): jnp.stack([lax.dynamic_slice_in_dim(x, rank * HD, HD, 1) for x in (keys,...]
    transpose x1 -> x0, local copies, waits for them, and re-layouts: 0.74 us -> none  [on_device(): spread = local.reshape(2, ranks, share, heads, HD).transpose(3, 1, 0, 2, 4)]
    pallas_call x1 -> x3, Pallas kernels: 7.06 us -> 6.32 us  [the longest x1 4.37 us: attend_far(): pl.pallas_call(far_kernel, out_shape=jax.ShapeDtypeStruct(queries.shape,...]
    squeeze x1, local copies, waits for them, and re-layouts: 0.68 us -> 0.08 us  [on_device(): lists = selected[0]]
  transfers between devices with their start and end apart: 3 -> 3, of which waited for: 3 -> 3; matrix products, arithmetic and copies ran while one was open for 2% -> 1% of each run, Pallas kernels for 0% -> 3%
where the time goes in v2:
time: 45.8 us; the launch traced here: 45.4 us
  waiting for transfers between devices  20.3 us (44%)
  starting transfers between devices  11.8 us (26%)
  Pallas kernels  7.84 us (17%)
  local copies, waits for them, and re-layouts  5.09 us (11%)
    all_to_all x1, waiting for transfers between devices, on_device(): lax.all_to_all(spread, ('head', 'ctx'), split_axis=0, concat_axis=0, tile...  10.2 us
    all_to_all x1, starting transfers between devices, on_device(): lax.all_to_all(spread, ('head', 'ctx'), split_axis=0, concat_axis=0, tile...  7.3 us
    all_to_all x1, waiting for transfers between devices, on_device(): far = lax.all_to_all(far, 'ctx', split_axis=0, concat_axis=0, tiled=True)  5.26 us
    unnamed x16, local copies, waits for them, and re-layouts  4.94 us
    ppermute x1, waiting for transfers between devices, own_block(): came = lax.ppermute(columns(1 - head_rank), 'head', [(0, 1), (1, 0)])  4.84 us
    pallas_call x1, Pallas kernels, attend_far(): pl.pallas_call(far_kernel, out_shape=jax.ShapeDtypeStruct(queries.shape,...  4.37 us
    all_to_all x1, starting transfers between devices, on_device(): far = lax.all_to_all(far, 'ctx', split_axis=0, concat_axis=0, tiled=True)  3.71 us
    pallas_call x1, Pallas kernels, pick_pieces(): pl.pallas_call(pick_kernel, out_shape=jax.ShapeDtypeStruct((receivers, 2,...  1.52 us
  transfers between devices with their start and end apart: 3, of which 3 were waited for; matrix products, arithmetic and copies ran while one was open for 1% of the time, Pallas kernels for 3%

profile of v2, /device:TPU:0, one launch (start us, length us, event | category | flops | bytes accessed | tf_op | source)
XLA Modules:
  0.0 45.4 jit_solution(8988486273140057254)
XLA Ops:
  0.0 0.0 copy-start.3
  0.0 0.9 %copy-done.3 = bf16[256,256]{1,0:T(8,128)(2,1)S(1)} copy-done((bf16[256,256]{1,0:T(8,128)(2,1)S(1)}, bf16[256,256]{1,0:T(8,128)(2,1)}, u32[]{:S(2)}) %copy-start.3) | copy-done | bytes 131096
  0.9 0.9 %copy-done.5 = bf16[256,256]{1,0:T(8,128)(2,1)S(1)} copy-done((bf16[256,256]{1,0:T(8,128)(2,1)S(1)}, bf16[256,256]{1,0:T(8,128)(2,1)}, u32[]{:S(2)}) %copy-start.5) | copy-done | bytes 131096
  1.8 0.7 %shard_map.46 = bf16[32,2,16,128]{3,2,1,0:T(8,128)(2,1)} custom-call(bf16[256,256]{1,0:T(8,128)(2,1)S(1)} %copy-done.5, bf16[256,256]{1,0:T(8,128)(2,1)S(1)} %copy-done.3), custom_call_target="tpu_custom_call" | custom-call | tf_op jit(solution)/shard_map/pallas_call | solution.py:34
  2.6 7.3 %all-to-all-start = ((bf16[32,2,16,128]{3,2,1,0:T(8,128)(2,1)}), bf16[32,2,16,128]{3,2,1,0:T(8,128)(2,1)S(1)}, u32[]{:S(2)}, u32[]{:S(2)}) async-start(bf16[32,2,16,128]{3,2,1,0:T(8,128)(2,1)} %shard_map.46), calls=%async_computation | async-start | bytes 524288 | tf_op jit(solution)/shard_map/all_to_all | solution.py:205
  9.9 0.0 copy-done.7
  9.9 0.1 copy.7
  10.0 10.2 %all-to-all-done = bf16[32,2,16,128]{3,2,1,0:T(8,128)(2,1)S(1)} async-done(((bf16[32,2,16,128]{3,2,1,0:T(8,128)(2,1)}), bf16[32,2,16,128]{3,2,1,0:T(8,128)(2,1)S(1)}, u32[]{:S(2)}, u32[]{:S(2)}) %all-to-all-start) | async-done | bytes 262176 | tf_op jit(solution)/shard_map/all_to_all | solution.py:205
  20.1 1.5 %shard_map.47 = bf16[16,2,2,2,16,128]{5,4,3,2,1,0:T(8,128)(2,1)} custom-call(s32[16,3]{1,0:T(8,128)S(1)} %bitcast.17, bf16[2,16,2,16,128]{4,3,2,1,0:T(8,128)(2,1)S(1)} %bitcast.16), custom_call_target="tpu_custom_call" | custom-call | tf_op jit(solution)/shard_map/pallas_call | solution.py:61
  21.7 3.7 %all-to-all-start.1 = ((bf16[16,2,2,2,16,128]{5,4,3,2,1,0:T(8,128)(2,1)}), bf16[16,2,2,2,16,128]{5,4,3,2,1,0:T(8,128)(2,1)S(1)}, u32[]{:S(2)}, u32[]{:S(2)}) async-start(bf16[16,2,2,2,16,128]{5,4,3,2,1,0:T(8,128)(2,1)} %shard_map.47), calls=%async_computation.1 | async-start | bytes 1048576 | tf_op jit(solution)/shard_map/all_to_all | solution.py:211
  25.4 0.0 copy-done.4
  25.4 0.0 copy-done.6
  25.4 0.1 dynamic-slice_bitcast_fusion.2
  25.5 0.8 %collective-permute-start = (bf16[2,256,128]{2,1,0:T(8,128)(2,1)S(1)}, bf16[2,256,128]{2,1,0:T(8,128)(2,1)S(1)}, u32[]{:S(2)}, u32[]{:S(2)}) collective-permute-start(bf16[2,256,128]{2,1,0:T(8,128)(2,1)S(1)} %pad_maximum_fusion), channel_id=1, source_target_pairs={{0,16},{16,0},{1,17},{17,1},{2,18},{18,2},{3,19},{19,3},{4,20},{20... | collective-permute-start | bytes 393224 | tf_op jit(solution)/shard_map/ppermute | solution.py:186
  26.3 0.2 fusion.live_ref
  26.5 4.8 %collective-permute-done = bf16[2,256,128]{2,1,0:T(8,128)(2,1)S(1)} collective-permute-done((bf16[2,256,128]{2,1,0:T(8,128)(2,1)S(1)}, bf16[2,256,128]{2,1,0:T(8,128)(2,1)S(1)}, u32[]{:S(2)}, u32[]{:S(2)}) %collective-permute-start) | collective-permute-done | bytes 131104 | tf_op jit(solution)/shard_map/ppermute | solution.py:186
  31.3 0.1 maximum_select_fusion
  31.5 0.9 %copy-done.2 = bf16[512,512]{1,0:T(8,128)(2,1)S(1)} copy-done((bf16[512,512]{1,0:T(8,128)(2,1)S(1)}, bf16[512,512]{1,0:T(8,128)(2,1)}, u32[]{:S(2)}) %copy-start.2) | copy-done | bytes 524312
  32.4 1.2 %shard_map.48 = (f32[4,512,128]{2,1,0:T(8,128)S(1)}, f32[4,512,128]{2,1,0:T(8,128)S(1)}, f32[4,512,128]{2,1,0:T(8,128)S(1)}) custom-call(bf16[512,512]{1,0:T(8,128)(2,1)S(1)} %copy-done.2, bf16[512,128]{1,0:T(8,128)(2,1)S(1)} %get-tuple-element.12.key_ref, bf16[512,128]{1,0:T(8,128)(2,1)S(1)} %get-tuple-element.11.value_ref), custom_call_target="tpu_custom_call" | custom-call | flops 536870912 | bytes 4194304 | tf_op jit(solution)/shard_map/pallas_call | solution.py:117
  33.6 0.0 copy-start
  33.6 1.0 %copy-done = f32[4,512,128]{2,1,0:T(8,128)} copy-done((f32[4,512,128]{2,1,0:T(8,128)}, f32[4,512,128]{2,1,0:T(8,128)S(1)}, u32[]{:S(2)}) %copy-start) | copy-done | bytes 1048600
  34.6 5.3 %all-to-all-done.1 = bf16[16,2,2,2,16,128]{5,4,3,2,1,0:T(8,128)(2,1)S(1)} async-done(((bf16[16,2,2,2,16,128]{5,4,3,2,1,0:T(8,128)(2,1)}), bf16[16,2,2,2,16,128]{5,4,3,2,1,0:T(8,128)(2,1)S(1)}, u32[]{:S(2)}, u32[]{:S(2)}) %all-to-all-start.1) | async-done | bytes 524320 | tf_op jit(solution)/shard_map/all_to_all | solution.py:211
  39.8 1.2 %copy-done.1 = f32[4,512,128]{2,1,0:T(8,128)S(1)} copy-done((f32[4,512,128]{2,1,0:T(8,128)S(1)}, f32[4,512,128]{2,1,0:T(8,128)}, u32[]{:S(2)}) %copy-start.1) | copy-done | bytes 1048600
  41.1 4.4 %shard_map.49 = bf16[512,512]{1,0:T(8,128)(2,1)} custom-call(s32[2]{0:T(128)S(1)} %fusion.live_ref, bf16[512,512]{1,0:T(8,128)(2,1)S(1)} %copy-done.2, bf16[512,128]{1,0:T(8,128)(2,1)S(1)} %get-tuple-element.12.key_ref, bf16[16,2,2,32,128]{4,3,2,1,0:T(8,128)(2,1)S(1)} %bitcast.15, f32[4,512,128]{2,1,0:T(8,128)S(1)} %get-tuple-element.8.top_ref, ...), custom_call_target="tpu_custom_call" | custom-call | tf_op jit(solution)/shard_map/pallas_call | solution.py:167
  (8 shorter events, 0.0 us)
Async XLA Ops:
  0.0 0.9 %copy-start.3 = (bf16[256,256]{1,0:T(8,128)(2,1)S(1)}, bf16[256,256]{1,0:T(8,128)(2,1)}, u32[]{:S(2)}) copy-start(bf16[256,256]{1,0:T(8,128)(2,1)} %value_ref.1) | copy-start | bytes 393220
  0.9 0.9 %copy-start.5 = (bf16[256,256]{1,0:T(8,128)(2,1)S(1)}, bf16[256,256]{1,0:T(8,128)(2,1)}, u32[]{:S(2)}) copy-start(bf16[256,256]{1,0:T(8,128)(2,1)} %key_ref.1) | copy-start | bytes 393220
  2.6 7.3 %copy-start.7 = (s32[1,16,3]{1,0,2:T(1,128)S(1)}, s32[1,16,3]{1,0,2:T(1,128)}, u32[]{:S(2)}) copy-start(s32[1,16,3]{1,0,2:T(1,128)} %param.7) | copy-start | bytes 580
  2.6 17.6 %all-to-all-start = ((bf16[32,2,16,128]{3,2,1,0:T(8,128)(2,1)}), bf16[32,2,16,128]{3,2,1,0:T(8,128)(2,1)S(1)}, u32[]{:S(2)}, u32[]{:S(2)}) async-start(bf16[32,2,16,128]{3,2,1,0:T(8,128)(2,1)} %shard_map.46), calls=%async_computation | async-start | bytes 524288 | tf_op jit(solution)/shard_map/all_to_all | solution.py:205
  21.7 3.7 %copy-start.4 = (bf16[256,256]{1,0:T(8,128)(2,1)S(1)}, bf16[256,256]{1,0:T(8,128)(2,1)}, u32[]{:S(2)}) copy-start(bf16[256,256]{1,0:T(8,128)(2,1)} %value_ref.1) | copy-start | bytes 393220
  21.7 3.7 %copy-start.6 = (bf16[256,256]{1,0:T(8,128)(2,1)S(1)}, bf16[256,256]{1,0:T(8,128)(2,1)}, u32[]{:S(2)}) copy-start(bf16[256,256]{1,0:T(8,128)(2,1)} %key_ref.1) | copy-start | bytes 393220
  21.7 18.2 %all-to-all-start.1 = ((bf16[16,2,2,2,16,128]{5,4,3,2,1,0:T(8,128)(2,1)}), bf16[16,2,2,2,16,128]{5,4,3,2,1,0:T(8,128)(2,1)S(1)}, u32[]{:S(2)}, u32[]{:S(2)}) async-start(bf16[16,2,2,2,16,128]{5,4,3,2,1,0:T(8,128)(2,1)} %shard_map.47), calls=%async_computation.1 | async-start | bytes 1048576 | tf_op jit(solution)/shard_map/all_to_all | solution.py:211
  25.5 5.8 %collective-permute-start = (bf16[2,256,128]{2,1,0:T(8,128)(2,1)S(1)}, bf16[2,256,128]{2,1,0:T(8,128)(2,1)S(1)}, u32[]{:S(2)}, u32[]{:S(2)}) collective-permute-start(bf16[2,256,128]{2,1,0:T(8,128)(2,1)S(1)} %pad_maximum_fusion), channel_id=1, source_target_pairs={{0,16},{16,0},{1,17},{17,1},{2,18},{18,2},{3,19},{19,3},{4,20},{20... | collective-permute-start | bytes 393224 | tf_op jit(solution)/shard_map/ppermute | solution.py:186
  31.3 1.0 %copy-start.2 = (bf16[512,512]{1,0:T(8,128)(2,1)S(1)}, bf16[512,512]{1,0:T(8,128)(2,1)}, u32[]{:S(2)}) copy-start(bf16[512,512]{1,0:T(8,128)(2,1)} %query_ref.3) | copy-start | bytes 1572868
  33.6 1.0 %copy-start = (f32[4,512,128]{2,1,0:T(8,128)}, f32[4,512,128]{2,1,0:T(8,128)S(1)}, u32[]{:S(2)}) copy-start(f32[4,512,128]{2,1,0:T(8,128)S(1)} %get-tuple-element.10.acc_ref) | copy-start | bytes 3145732
  39.8 1.2 %copy-start.1 = (f32[4,512,128]{2,1,0:T(8,128)S(1)}, f32[4,512,128]{2,1,0:T(8,128)}, u32[]{:S(2)}) copy-start(f32[4,512,128]{2,1,0:T(8,128)} %copy-done) | copy-start | bytes 3145732

commit v3 on v2

--- a/solution.py
+++ b/solution.py
@@ -12,57 +12,65 @@
 BLK = 512
 CHUNK = 256
 FACTOR = math.log2(math.e) / math.sqrt(HD)
-SMALL = pltpu.CompilerParams(vmem_limit_bytes=4 * 1024 * 1024)
-LARGE = pltpu.CompilerParams(vmem_limit_bytes=24 * 1024 * 1024)
+SMALL = pltpu.CompilerParams(vmem_limit_bytes=2 * 1024 * 1024)
+LARGE = pltpu.CompilerParams(vmem_limit_bytes=12 * 1024 * 1024)
 VMEM = pl.BlockSpec(memory_space=pltpu.VMEM)
 SMEM = pl.BlockSpec(memory_space=pltpu.SMEM)
-
-
-def spread_kernel(key_ref, value_ref, out_ref):
-    peers, _, share, _ = out_ref.shape
-    ranks = key_ref.shape[0] // share
-    for kv, ref in enumerate((key_ref, value_ref)):
+ANY = pl.BlockSpec(memory_space=pl.ANY)
+
+
+def spread_kernel(key_ref, value_ref, key_out, value_out, sems):
+    peers = key_out.shape[0]
+    ranks = key_ref.shape[0]
+    copies = []
+    for kv, (ref, out) in enumerate(((key_ref, key_out), (value_ref, value_out))):
         for h in range(peers // ranks):
-            columns = ref[:, h * HD : (h + 1) * HD]
-            out_ref[h * ranks : (h + 1) * ranks, kv] = columns.reshape(ranks, share, HD)
+            copies.append(
+                pltpu.make_async_copy(
+                    ref.at[:, :, h * HD : (h + 1) * HD],
+                    out.at[h * ranks : (h + 1) * ranks],
+                    sems.at[kv, h],
+                )
+            )
+    for copy in copies:
+        copy.start()
+    for copy in copies:
+        copy.wait()
 
 
 def spread_rows(keys, values, heads, ranks):
-    held = keys.shape[0]
-    share = held // ranks
+    share = keys.shape[0] // ranks
     if share % 16 == 0:
+        part = jax.ShapeDtypeStruct((heads * ranks, share, HD), keys.dtype)
         return pl.pallas_call(
             spread_kernel,
-            out_shape=jax.ShapeDtypeStruct((heads * ranks, 2, share, HD), keys.dtype),
-            in_specs=[VMEM, VMEM],
-            out_specs=VMEM,
+            out_shape=[part, part],
+            in_specs=[ANY, ANY],
+            out_specs=[ANY, ANY],
+            scratch_shapes=[pltpu.SemaphoreType.DMA((2, heads))],
             compiler_params=SMALL,
-        )(keys, values)
-    both = jnp.stack([keys, values]).reshape(2, ranks, share, heads, HD)
-    return both.transpose(3, 1, 0, 2, 4).reshape(heads * ranks, 2, share, HD)
-
-
-def pick_kernel(lists_ref, pieces_ref, out_ref):
-    receivers, _, picks, parts, _, _ = out_ref.shape
-
-    def one(receiver, carry):
+        )(keys.reshape(ranks, share, heads * HD), values.reshape(ranks, share, heads * HD))
+    split = lambda x: x.reshape(ranks, share, heads, HD).transpose(2, 0, 1, 3)
+    return [split(x).reshape(heads * ranks, share, HD) for x in (keys, values)]
+
+
+def pick_kernel(lists_ref, pieces_ref, out_ref, sem):
+    receivers, picks = out_ref.shape[:2]
+    for receiver in range(receivers):
         for s in range(picks):
             block = lists_ref[receiver, s + 1]
-            for part in range(parts):
-                for kv in range(2):
-                    out_ref[receiver, kv, s, part] = pieces_ref[part, block, kv]
-        return carry
-
-    lax.fori_loop(0, receivers, one, 0, unroll=4)
+            pltpu.make_async_copy(pieces_ref.at[:, block], out_ref.at[receiver, s], sem).start()
+    pltpu.make_async_copy(out_ref, out_ref, sem).wait()
 
 
 def pick_pieces(lists, pieces, receivers, picks):
-    parts, _, _, rows, _ = pieces.shape
+    parts, _, rows, _ = pieces.shape
     return pl.pallas_call(
         pick_kernel,
-        out_shape=jax.ShapeDtypeStruct((receivers, 2, picks, parts, rows, HD), pieces.dtype),
-        in_specs=[SMEM, VMEM],
-        out_specs=VMEM,
+        out_shape=jax.ShapeDtypeStruct((receivers, picks, parts, rows, HD), pieces.dtype),
+        in_specs=[SMEM, ANY],
+        out_specs=ANY,
+        scratch_shapes=[pltpu.SemaphoreType.DMA],
         compiler_params=SMALL,
     )(lists, pieces)
 
@@ -127,21 +135,12 @@
     )(queries, own_keys, own_values)
 
 
-def far_kernel(
-    live_ref, query_ref, key_ref, far_ref, top_ref, sum_ref, acc_ref, out_ref, turned, valued
-):
-    picks = far_ref.shape[2]
+def weigh_kernel(live_ref, query_ref, key_ref, far_ref, top_ref, weight_ref, scale_ref, turned):
+    picks = far_ref.shape[1]
     spare = jnp.broadcast_to(key_ref[0:1, :], (BLK, HD))
     for s in range(picks):
-        rows = slice(s * BLK, (s + 1) * BLK)
-        live = live_ref[s] > 0
-        key_rows = jnp.where(live, far_ref[:, 0, s].reshape(BLK, HD), spare)
-        value_rows = far_ref[:, 1, s].reshape(BLK, HD)
-        turned[:HD, rows] = key_rows.T
-        valued[rows, :HD] = jnp.where(live, value_rows, jnp.zeros_like(value_rows))
-        valued[rows, HD:] = jnp.where(
-            live, jnp.ones_like(value_rows), jnp.zeros_like(value_rows)
-        )
+        key_rows = jnp.where(live_ref[s] > 0, far_ref[:, s].reshape(BLK, HD), spare)
+        turned[:HD, s * BLK : (s + 1) * BLK] = key_rows.T
     turned[HD:] = turned[:HD]
 
     def score(h, begin):
@@ -152,29 +151,70 @@
         rows = slice(begin, begin + CHUNK)
         near_top = top_ref[h, rows]
         top = jnp.maximum(jnp.max(scores, axis=1, keepdims=True), near_top[:, :1])
-        weights = jnp.exp2(scores - top).astype(jnp.bfloat16)
-        product = jnp.dot(weights, valued[...], preferred_element_type=jnp.float32)
-        scale = jnp.exp2(near_top - top)
-        total = product[:, HD:] + sum_ref[h, rows] * scale
-        product = product[:, :HD] + acc_ref[h, rows] * scale
-        out_ref[rows, h * HD : (h + 1) * HD] = (product / total).astype(out_ref.dtype)
+        weight_ref[h, rows] = jnp.exp2(scores - top).astype(jnp.bfloat16)
+        scale_ref[h, rows] = jnp.exp2(near_top - top)
 
     in_turn(units_of(query_ref.shape[1]), score, finish)
 
 
-def attend_far(live, queries, own_keys, far, near):
-    keys_here = far.shape[2] * BLK
-    return pl.pallas_call(
-        far_kernel,
-        out_shape=jax.ShapeDtypeStruct(queries.shape, queries.dtype),
-        in_specs=[SMEM] + [VMEM] * 6,
-        out_specs=VMEM,
+def weigh_far(live, queries, own_keys, far_keys, near_top):
+    rows, columns = queries.shape
+    keys_here = far_keys.shape[1] * BLK
+    heads_here = columns // HD
+    return pl.pallas_call(
+        weigh_kernel,
+        out_shape=[
+            jax.ShapeDtypeStruct((heads_here, rows, keys_here), jnp.bfloat16),
+            jax.ShapeDtypeStruct((heads_here, rows, HD), jnp.float32),
+        ],
+        in_specs=[SMEM] + [VMEM] * 4,
+        out_specs=[VMEM] * 2,
+        scratch_shapes=[pltpu.VMEM((2 * HD, keys_here), jnp.bfloat16)],
+        compiler_params=LARGE,
+        cost_estimate=pl.CostEstimate(
+            flops=8 * columns * rows * keys_here, bytes_accessed=8 << 20, transcendentals=0
+        ),
+    )(live, queries, own_keys, far_keys, near_top)
+
+
+def gather_kernel(
+    live_ref, weight_ref, far_ref, scale_ref, sum_ref, acc_ref, out_ref, valued, ready, sems
+):
+    picks = far_ref.shape[1]
+    for s in range(picks):
+        rows = slice(s * BLK, (s + 1) * BLK)
+        live = live_ref[s] > 0
+        value_rows = far_ref[:, s].reshape(BLK, HD)
+        none = jnp.zeros_like(value_rows)
+        valued[rows, :HD] = jnp.where(live, value_rows, none)
+        valued[rows, HD:] = jnp.where(live, jnp.ones_like(value_rows), none)
+    copies = []
+    for h in range(weight_ref.shape[0]):
+        product = jnp.dot(weight_ref[h], valued[...], preferred_element_type=jnp.float32)
+        scale = scale_ref[h]
+        total = product[:, HD:] + sum_ref[h] * scale
+        ready[h] = ((product[:, :HD] + acc_ref[h] * scale) / total).astype(ready.dtype)
+        columns = slice(h * HD, (h + 1) * HD)
+        copies.append(pltpu.make_async_copy(ready.at[h], out_ref.at[:, columns], sems.at[h]))
+        copies[-1].start()
+    for copy in copies:
+        copy.wait()
+
+
+def gather_far(live, weights, far_values, scale, near_sum, near_acc):
+    heads_here, rows, keys_here = weights.shape
+    return pl.pallas_call(
+        gather_kernel,
+        out_shape=jax.ShapeDtypeStruct((rows, heads_here * HD), jnp.bfloat16),
+        in_specs=[SMEM] + [VMEM] * 5,
+        out_specs=ANY,
         scratch_shapes=[
-            pltpu.VMEM((2 * HD, keys_here), jnp.bfloat16),
             pltpu.VMEM((keys_here, 2 * HD), jnp.bfloat16),
+            pltpu.VMEM((heads_here, rows, HD), jnp.bfloat16),
+            pltpu.SemaphoreType.DMA((heads_here,)),
         ],
         compiler_params=LARGE,
-    )(live, queries, own_keys, far, *near)
+    )(live, weights, far_values, scale, near_sum, near_acc)
 
 
 def own_block(keys, values, heads, head_rank):
@@ -201,22 +241,31 @@
     ctx_rank = lax.axis_index("ctx")
     share = keys.shape[0] // ranks
 
-    spread = spread_rows(keys, values, heads, ranks)
-    spread = lax.all_to_all(spread, ("head", "ctx"), split_axis=0, concat_axis=0, tiled=True)
-    spread = spread.reshape(heads, ranks, 2, share, HD)
-    if share % 16:
-        spread = spread.transpose(1, 2, 0, 3, 4).reshape(1, ranks, 2, heads * share, HD)
-
-    far = pick_pieces(lists, spread, ranks, picks)
-    far = lax.all_to_all(far, "ctx", split_axis=0, concat_axis=0, tiled=True)
-    far = far.reshape(ranks, 2, picks, -1, HD)
+    def spread_to_ranks(part):
+        part = lax.all_to_all(part, ("head", "ctx"), split_axis=0, concat_axis=0, tiled=True)
+        part = part.reshape(heads, ranks, share, HD)
+        if share % 16:
+            part = part.transpose(1, 0, 2, 3).reshape(1, ranks, heads * share, HD)
+        return part
+
+    def send_picked(pieces):
+        far = pick_pieces(lists, pieces, ranks, picks)
+        far = lax.all_to_all(far, "ctx", split_axis=0, concat_axis=0, tiled=True)
+        return far.reshape(ranks, picks, -1, HD)
+
+    key_part, value_part = spread_rows(keys, values, heads, ranks)
+    key_part = spread_to_ranks(key_part)
+    value_part = spread_to_ranks(value_part)
+    far_keys = send_picked(key_part)
+    far_values = send_picked(value_part)
 
     own = own_block(keys, values, heads, head_rank)
-    near = attend_near(queries, own[0], own[1])
+    near_top, near_sum, near_acc = attend_near(queries, own[0], own[1])
 
     chosen = lax.dynamic_index_in_dim(lists, ctx_rank, 0, keepdims=False)[1:]
     live = (chosen != ctx_rank).astype(jnp.int32)
-    return attend_far(live, queries, own[0], far, near)
+    weights, scale = weigh_far(live, queries, own[0], far_keys, near_top)
+    return gather_far(live, weights, far_values, scale, near_sum, near_acc)
 
 
 def solution(mesh):

time: 45.8 us -> 61.1 us (1.33)
  blocking collectives: 0 us -> 15.3 us
  waiting for transfers between devices: 20.3 us -> 13.7 us
  local copies, waits for them, and re-layouts: 5.09 us -> 9.68 us
  Pallas kernels: 7.84 us -> 10.3 us
  starting transfers between devices: 11.8 us -> 10.5 us
  other arithmetic: 0.29 us -> 0.97 us
    all_to_all x0 -> x1, blocking collectives: none -> 15.3 us  [spread_to_ranks(): lax.all_to_all(part, ('head', 'ctx'), split_axis=0, concat_axis=0, tiled=...]
    ppermute x1, waiting for transfers between devices: 4.84 us -> 0.01 us  [own_block(): came = lax.ppermute(columns(1 - head_rank), 'head', [(0, 1), (1, 0)])]
    unnamed x16, local copies, waits for them, and re-layouts: 4.94 us -> 7.94 us
    pallas_call x3 -> x5, Pallas kernels: 6.63 us -> 9.06 us  [the longest x1 2.96 us: weigh_far(): pl.pallas_call(weigh_kernel, out_shape=[jax.ShapeDtypeStruct((heads_here,...]
    all_to_all x2 -> x3, waiting for transfers between devices: 15.5 us -> 13.7 us  [the longest x2 7.6 us: send_picked(): far = lax.all_to_all(far, 'ctx', split_axis=0, concat_axis=0, tiled=True)]
    all_to_all x2 -> x3, starting transfers between devices: 11 us -> 9.63 us  [the longest x2 7.06 us: send_picked(): far = lax.all_to_all(far, 'ctx', split_axis=0, concat_axis=0, tiled=True)]
    another operation x1, local copies, waits for them, and re-layouts: 0.05 us -> 0.96 us  [own_block(): jnp.stack([lax.dynamic_slice_in_dim(x, rank * HD, HD, 1) for x in (keys,...]
    convert_element_type x1, other arithmetic: 0.19 us -> 0.87 us  [on_device(): live = (chosen != ctx_rank).astype(jnp.int32)]
  transfers between devices with their start and end apart: 3 -> 4, of which waited for: 3 -> 3; matrix products, arithmetic and copies ran while one was open for 1% -> 4% of each run, Pallas kernels for 3% -> 12%
where the time goes in v3:
time: 61.1 us; the launch traced here: 60.5 us
  blocking collectives  15.3 us (25%)
  waiting for transfers between devices  13.7 us (22%)
  starting transfers between devices  10.5 us (17%)
  Pallas kernels  10.3 us (17%)
  local copies, waits for them, and re-layouts  9.68 us (16%)
  other arithmetic  0.97 us (2%)
    all_to_all x1, blocking collectives, spread_to_ranks(): lax.all_to_all(part, ('head', 'ctx'), split_axis=0, concat_axis=0, tiled=...  15.3 us
    unnamed x16, local copies, waits for them, and re-layouts  7.94 us
    all_to_all x2, waiting for transfers between devices, send_picked(): far = lax.all_to_all(far, 'ctx', split_axis=0, concat_axis=0, tiled=True)  7.6 us
    all_to_all x2, starting transfers between devices, send_picked(): far = lax.all_to_all(far, 'ctx', split_axis=0, concat_axis=0, tiled=True)  7.06 us
    all_to_all x1, waiting for transfers between devices, spread_to_ranks(): lax.all_to_all(part, ('head', 'ctx'), split_axis=0, concat_axis=0, tiled=...  6.07 us
    pallas_call x1, Pallas kernels, weigh_far(): pl.pallas_call(weigh_kernel, out_shape=[jax.ShapeDtypeStruct((heads_here,...  2.96 us
    pallas_call x2, Pallas kernels, pick_pieces(): pl.pallas_call(pick_kernel, out_shape=jax.ShapeDtypeStruct((receivers, pi...  2.8 us
    pallas_call x1, Pallas kernels, gather_far(): pl.pallas_call(gather_kernel, out_shape=jax.ShapeDtypeStruct((rows, heads...  2.59 us
  transfers between devices with their start and end apart: 4, of which 3 were waited for; matrix products, arithmetic and copies ran while one was open for 4% of the time, Pallas kernels for 12%

profile of v3, /device:TPU:0, one launch (start us, length us, event | category | flops | bytes accessed | tf_op | source)
XLA Modules:
  0.0 60.5 jit_solution(2936158261523114111)
XLA Ops:
  0.0 0.9 %copy-done.2 = bf16[256,256]{1,0:T(8,128)(2,1)S(1)} copy-done((bf16[256,256]{1,0:T(8,128)(2,1)S(1)}, bf16[256,256]{1,0:T(8,128)(2,1)}, u32[]{:S(2)}) %copy-start.2) | copy-done | bytes 131096
  0.9 0.9 %copy-done.3 = bf16[256,256]{1,0:T(8,128)(2,1)S(1)} copy-done((bf16[256,256]{1,0:T(8,128)(2,1)S(1)}, bf16[256,256]{1,0:T(8,128)(2,1)}, u32[]{:S(2)}) %copy-start.3) | copy-done | bytes 131096
  1.8 0.7 %shard_map.46 = (bf16[32,16,128]{2,1,0:T(8,128)(2,1)S(1)}, bf16[32,16,128]{2,1,0:T(8,128)(2,1)}) custom-call(bf16[16,16,256]{2,1,0:T(8,128)(2,1)S(1)} %bitcast.23, bf16[16,16,256]{2,1,0:T(8,128)(2,1)S(1)} %bitcast.22), custom_call_target="tpu_custom_call" | custom-call | tf_op jit(solution)/shard_map/pallas_call | solution.py:45
  2.5 15.3 %all_to_all.20 = bf16[32,16,128]{2,1,0:T(8,128)(2,1)S(1)} all-to-all(bf16[32,16,128]{2,1,0:T(8,128)(2,1)S(1)} %get-tuple-element.12), channel_id=1, replica_groups=mesh['head'=2,'ctx'=16] {'head','ctx'}, dimensions={0} | all-to-all | bytes 262144 | tf_op jit(solution)/shard_map/all_to_all | solution.py:245
  17.9 2.6 %all-to-all-start.2 = ((bf16[32,16,128]{2,1,0:T(8,128)(2,1)}), bf16[32,16,128]{2,1,0:T(8,128)(2,1)S(1)}, u32[]{:S(2)}, u32[]{:S(2)}) async-start(bf16[32,16,128]{2,1,0:T(8,128)(2,1)} %get-tuple-element.15), calls=%async_computation.2 | async-start | bytes 262144 | tf_op jit(solution)/shard_map/all_to_all | solution.py:245
  20.4 0.8 %copy.9 = s32[1,16,3]{2,1,0:T(8,128)S(1)} copy(s32[1,16,3]{1,0,2:T(1,128)} %param.7) | data formatting | bytes 384 | tf_op jit(solution)/shard_map/squeeze | solution.py:238
  21.2 1.4 %shard_map.47 = bf16[16,2,2,16,128]{4,3,2,1,0:T(8,128)(2,1)} custom-call(s32[16,3]{1,0:T(8,128)S(1)} %bitcast.25, bf16[2,16,16,128]{3,2,1,0:T(8,128)(2,1)S(1)} %bitcast.21), custom_call_target="tpu_custom_call" | custom-call | tf_op jit(solution)/shard_map/pallas_call | solution.py:68
  22.6 6.1 %all-to-all-done.2 = bf16[32,16,128]{2,1,0:T(8,128)(2,1)S(1)} async-done(((bf16[32,16,128]{2,1,0:T(8,128)(2,1)}), bf16[32,16,128]{2,1,0:T(8,128)(2,1)S(1)}, u32[]{:S(2)}, u32[]{:S(2)}) %all-to-all-start.2) | async-done | bytes 131104 | tf_op jit(solution)/shard_map/all_to_all | solution.py:245
  28.7 3.5 %all-to-all-start.1 = ((bf16[16,2,2,16,128]{4,3,2,1,0:T(8,128)(2,1)}), bf16[16,2,2,16,128]{4,3,2,1,0:T(8,128)(2,1)S(1)}, u32[]{:S(2)}, u32[]{:S(2)}) async-start(bf16[16,2,2,16,128]{4,3,2,1,0:T(8,128)(2,1)} %shard_map.47), calls=%async_computation.1 | async-start | bytes 524288 | tf_op jit(solution)/shard_map/all_to_all | solution.py:253
  32.2 1.0 %dynamic-slice_bitcast_fusion.2 = (bf16[1,256,128]{2,1,0:T(8,128)(2,1)S(1)}, bf16[1,256,128]{2,1,0:T(8,128)(2,1)S(1)}, bf16[1,256,128]{2,1,0:T(8,128)(2,1)S(1)}, bf16[1,256,128]{2,1,0:T(8,128)(2,1)S(1)}) fusion(bf16[256,256]{1,0:T(8,128)(2,1)} %param.6, s32[]{:T(128)S(6)} %select_n.22, s32[]{:T(128)S(6)} %select_n.23, bf16[256,256]{1,0:T(8,128)(2,1)} %param.5), kind=kLoop, calls=%fused_computation.6 | loop fusion | bytes 524296 | tf_op jit(solution)/shard_map/stack | solution.py:222
  33.2 0.8 %collective-permute-start = (bf16[2,256,128]{2,1,0:T(8,128)(2,1)S(1)}, bf16[2,256,128]{2,1,0:T(8,128)(2,1)S(1)}, u32[]{:S(2)}, u32[]{:S(2)}) collective-permute-start(bf16[2,256,128]{2,1,0:T(8,128)(2,1)S(1)} %pad_maximum_fusion), channel_id=1, source_target_pairs={{0,16},{16,0},{1,17},{17,1},{2,18},{18,2},{3,19},{19,3},{4,20},{20... | collective-permute-start | bytes 393224 | tf_op jit(solution)/shard_map/ppermute | solution.py:226
  34.1 0.9 %fusion.live_ref = s32[2]{0:T(128)S(1)} fusion(s32[1,16,3]{1,0,2:T(1,128)} %param.7, s32[]{:T(128)S(6)} %select_n.20, s32[]{:T(128)S(6)} %add.16, s32[]{:T(128)S(6)} %axis_index.22), kind=kLoop, calls=%fused_computation.10 | loop fusion | flops 4 | bytes 28 | tf_op jit(solution)/shard_map/convert_element_type | solution.py:266
  34.9 1.4 %shard_map.50 = bf16[16,2,2,16,128]{4,3,2,1,0:T(8,128)(2,1)} custom-call(s32[16,3]{1,0:T(8,128)S(1)} %bitcast.26, bf16[2,16,16,128]{3,2,1,0:T(8,128)(2,1)S(1)} %bitcast.20), custom_call_target="tpu_custom_call" | custom-call | tf_op jit(solution)/shard_map/pallas_call | solution.py:68
  36.3 5.9 %all-to-all-done.1 = bf16[16,2,2,16,128]{4,3,2,1,0:T(8,128)(2,1)S(1)} async-done(((bf16[16,2,2,16,128]{4,3,2,1,0:T(8,128)(2,1)}), bf16[16,2,2,16,128]{4,3,2,1,0:T(8,128)(2,1)S(1)}, u32[]{:S(2)}, u32[]{:S(2)}) %all-to-all-start.1) | async-done | bytes 262176 | tf_op jit(solution)/shard_map/all_to_all | solution.py:253
  42.2 3.5 %all-to-all-start.3 = ((bf16[16,2,2,16,128]{4,3,2,1,0:T(8,128)(2,1)}), bf16[16,2,2,16,128]{4,3,2,1,0:T(8,128)(2,1)S(1)}, u32[]{:S(2)}, u32[]{:S(2)}) async-start(bf16[16,2,2,16,128]{4,3,2,1,0:T(8,128)(2,1)} %shard_map.50), calls=%async_computation.3 | async-start | bytes 524288 | tf_op jit(solution)/shard_map/all_to_all | solution.py:253
  45.8 0.1 maximum_select_fusion
  45.9 1.2 %shard_map.48 = (f32[4,512,128]{2,1,0:T(8,128)S(1)}, f32[4,512,128]{2,1,0:T(8,128)S(1)}, f32[4,512,128]{2,1,0:T(8,128)S(1)}) custom-call(bf16[512,512]{1,0:T(8,128)(2,1)S(1)} %copy-done.6, bf16[512,128]{1,0:T(8,128)(2,1)S(1)} %get-tuple-element.20.key_ref, bf16[512,128]{1,0:T(8,128)(2,1)S(1)} %get-tuple-element.19.value_ref), custom_call_target="tpu_custom_call" | custom-call | flops 536870912 | bytes 4194304 | tf_op jit(solution)/shard_map/pallas_call | solution.py:125
  47.1 0.9 %copy-done.5 = bf16[16,2,2,16,128]{4,3,2,1,0:T(8,128)(2,1)S(1)} copy-done((bf16[16,2,2,16,128]{4,3,2,1,0:T(8,128)(2,1)S(1)}, bf16[16,2,2,16,128]{4,3,2,1,0:T(8,128)(2,1)}, u32[]{:S(2)}) %copy-start.5) | copy-done | bytes 262168
  48.1 1.0 %copy-done.7 = bf16[512,512]{1,0:T(8,128)(2,1)S(1)} copy-done((bf16[512,512]{1,0:T(8,128)(2,1)S(1)}, bf16[512,512]{1,0:T(8,128)(2,1)}, u32[]{:S(2)}) %copy-start.7) | copy-done | bytes 524312
  49.1 3.0 %shard_map.49 = (bf16[4,512,1024]{2,1,0:T(8,128)(2,1)S(1)}, f32[4,512,128]{2,1,0:T(8,128)S(1)}) custom-call(s32[2]{0:T(128)S(1)} %fusion.live_ref, bf16[512,512]{1,0:T(8,128)(2,1)S(1)} %copy-done.7, bf16[512,128]{1,0:T(8,128)(2,1)S(1)} %get-tuple-element.20.key_ref, bf16[16,2,32,128]{3,2,1,0:T(8,128)(2,1)S(1)} %bitcast.24, ...), custom_call_target="tpu_custom_call" | custom-call | flops 2147483648 | bytes 8388608 | tf_op jit(solution)/shard_map/pallas_call | solution.py:164
  52.1 2.0 %copy-done = bf16[4,512,1024]{2,1,0:T(8,128)(2,1)} copy-done((bf16[4,512,1024]{2,1,0:T(8,128)(2,1)}, bf16[4,512,1024]{2,1,0:T(8,128)(2,1)S(1)}, u32[]{:S(2)}) %copy-start) | copy-done | bytes 4194328
  54.0 1.7 %all-to-all-done.3 = bf16[16,2,2,16,128]{4,3,2,1,0:T(8,128)(2,1)S(1)} async-done(((bf16[16,2,2,16,128]{4,3,2,1,0:T(8,128)(2,1)}), bf16[16,2,2,16,128]{4,3,2,1,0:T(8,128)(2,1)S(1)}, u32[]{:S(2)}, u32[]{:S(2)}) %all-to-all-start.3) | async-done | bytes 262176 | tf_op jit(solution)/shard_map/all_to_all | solution.py:253
  55.8 2.2 %copy-done.1 = bf16[4,512,1024]{2,1,0:T(8,128)(2,1)S(1)} copy-done((bf16[4,512,1024]{2,1,0:T(8,128)(2,1)S(1)}, bf16[4,512,1024]{2,1,0:T(8,128)(2,1)}, u32[]{:S(2)}) %copy-start.1) | copy-done | bytes 4194328
  58.0 2.6 %shard_map.51 = bf16[512,512]{1,0:T(8,128)(2,1)} custom-call(s32[2]{0:T(128)S(1)} %fusion.live_ref, bf16[4,512,1024]{2,1,0:T(8,128)(2,1)S(1)} %copy-done.1, bf16[16,2,32,128]{3,2,1,0:T(8,128)(2,1)S(1)} %bitcast.19, f32[4,512,128]{2,1,0:T(8,128)S(1)} %get-tuple-element.16.scale_ref, f32[4,512,128]{2,1,0:T(8,128)S(1)} %get-tuple-element.17.sum_ref, ...), custom_call_target="tpu_custom_call" | custom-call | tf_op jit(solution)/shard_map/pallas_call | solution.py:206
  (13 shorter events, 0.1 us)
Async XLA Ops:
  0.0 0.9 %copy-start.2 = (bf16[256,256]{1,0:T(8,128)(2,1)S(1)}, bf16[256,256]{1,0:T(8,128)(2,1)}, u32[]{:S(2)}) copy-start(bf16[256,256]{1,0:T(8,128)(2,1)} %param.6) | copy-start | bytes 393220
  0.9 0.9 %copy-start.3 = (bf16[256,256]{1,0:T(8,128)(2,1)S(1)}, bf16[256,256]{1,0:T(8,128)(2,1)}, u32[]{:S(2)}) copy-start(bf16[256,256]{1,0:T(8,128)(2,1)} %param.5) | copy-start | bytes 393220
  1.8 44.1 %copy-start.6 = (bf16[512,512]{1,0:T(8,128)(2,1)S(1)}, bf16[512,512]{1,0:T(8,128)(2,1)}, u32[]{:S(2)}) copy-start(bf16[512,512]{1,0:T(8,128)(2,1)} %query_ref.3) | copy-start | bytes 1572868
  17.9 10.8 %all-to-all-start.2 = ((bf16[32,16,128]{2,1,0:T(8,128)(2,1)}), bf16[32,16,128]{2,1,0:T(8,128)(2,1)S(1)}, u32[]{:S(2)}, u32[]{:S(2)}) async-start(bf16[32,16,128]{2,1,0:T(8,128)(2,1)} %get-tuple-element.15), calls=%async_computation.2 | async-start | bytes 262144 | tf_op jit(solution)/shard_map/all_to_all | solution.py:245
  28.7 13.5 %all-to-all-start.1 = ((bf16[16,2,2,16,128]{4,3,2,1,0:T(8,128)(2,1)}), bf16[16,2,2,16,128]{4,3,2,1,0:T(8,128)(2,1)S(1)}, u32[]{:S(2)}, u32[]{:S(2)}) async-start(bf16[16,2,2,16,128]{4,3,2,1,0:T(8,128)(2,1)} %shard_map.47), calls=%async_computation.1 | async-start | bytes 524288 | tf_op jit(solution)/shard_map/all_to_all | solution.py:253
  33.2 12.6 %collective-permute-start = (bf16[2,256,128]{2,1,0:T(8,128)(2,1)S(1)}, bf16[2,256,128]{2,1,0:T(8,128)(2,1)S(1)}, u32[]{:S(2)}, u32[]{:S(2)}) collective-permute-start(bf16[2,256,128]{2,1,0:T(8,128)(2,1)S(1)} %pad_maximum_fusion), channel_id=1, source_target_pairs={{0,16},{16,0},{1,17},{17,1},{2,18},{18,2},{3,19},{19,3},{4,20},{20... | collective-permute-start | bytes 393224 | tf_op jit(solution)/shard_map/ppermute | solution.py:226
  42.2 4.9 %copy-start.4 = (bf16[16,2,2,16,128]{4,3,2,1,0:T(8,128)(2,1)}, bf16[16,2,2,16,128]{4,3,2,1,0:T(8,128)(2,1)S(1)}, u32[]{:S(2)}) copy-start(bf16[16,2,2,16,128]{4,3,2,1,0:T(8,128)(2,1)S(1)} %all-to-all-done.1) | copy-start | bytes 786436
  42.2 13.5 %all-to-all-start.3 = ((bf16[16,2,2,16,128]{4,3,2,1,0:T(8,128)(2,1)}), bf16[16,2,2,16,128]{4,3,2,1,0:T(8,128)(2,1)S(1)}, u32[]{:S(2)}, u32[]{:S(2)}) async-start(bf16[16,2,2,16,128]{4,3,2,1,0:T(8,128)(2,1)} %shard_map.50), calls=%async_computation.3 | async-start | bytes 524288 | tf_op jit(solution)/shard_map/all_to_all | solution.py:253
  47.1 1.0 %copy-start.5 = (bf16[16,2,2,16,128]{4,3,2,1,0:T(8,128)(2,1)S(1)}, bf16[16,2,2,16,128]{4,3,2,1,0:T(8,128)(2,1)}, u32[]{:S(2)}) copy-start(bf16[16,2,2,16,128]{4,3,2,1,0:T(8,128)(2,1)} %copy-done.4) | copy-start | bytes 786436
  48.1 1.0 %copy-start.7 = (bf16[512,512]{1,0:T(8,128)(2,1)S(1)}, bf16[512,512]{1,0:T(8,128)(2,1)}, u32[]{:S(2)}) copy-start(bf16[512,512]{1,0:T(8,128)(2,1)} %query_ref.3) | copy-start | bytes 1572868
  52.1 2.0 %copy-start = (bf16[4,512,1024]{2,1,0:T(8,128)(2,1)}, bf16[4,512,1024]{2,1,0:T(8,128)(2,1)S(1)}, u32[]{:S(2)}) copy-start(bf16[4,512,1024]{2,1,0:T(8,128)(2,1)S(1)} %get-tuple-element.14.weight_ref) | copy-start | bytes 12582916
  55.8 2.2 %copy-start.1 = (bf16[4,512,1024]{2,1,0:T(8,128)(2,1)S(1)}, bf16[4,512,1024]{2,1,0:T(8,128)(2,1)}, u32[]{:S(2)}) copy-start(bf16[4,512,1024]{2,1,0:T(8,128)(2,1)} %copy-done) | copy-start | bytes 12582916

commit v4 on v2

v4 whole, which is shorter than its diff:
```python
import functools
import math

import jax
import jax.numpy as jnp
from jax import lax
from jax.experimental import pallas as pl
from jax.experimental.pallas import tpu as pltpu
from jax.sharding import PartitionSpec as P

HD = 128
BLK = 512
CHUNK = 128
AHEAD = 2
FACTOR = math.log2(math.e) / math.sqrt(HD)
SMALL = pltpu.CompilerParams(vmem_limit_bytes=2 * 1024 * 1024)
LARGE = pltpu.CompilerParams(vmem_limit_bytes=12 * 1024 * 1024)
VMEM = pl.BlockSpec(memory_space=pltpu.VMEM)
ANY = pl.BlockSpec(memory_space=pl.ANY)


def in_vmem(*arrays):
    return [pltpu.with_memory_space_constraint(x, pltpu.VMEM) for x in arrays]


def pack_kernel(key_ref, value_ref, out_ref, sems):
    copies = [
        pltpu.make_async_copy(ref, out_ref.at[:, kv], sems.at[kv])
        for kv, ref in enumerate((key_ref, value_ref))
    ]
    for copy in copies:
        copy.start()
    for copy in copies:
        copy.wait()


def pack_rows(keys, values, ranks):
    held, columns = keys.shape
    share = held // ranks
    keys = keys.reshape(ranks, share, columns)
    values = values.reshape(ranks, share, columns)
    if share % 16:
        return jnp.stack([keys, values], axis=1)
    return pl.pallas_call(
        pack_kernel,
        out_shape=pltpu.VMEM((ranks, 2, share, columns), keys.dtype),
        in_specs=[ANY, ANY],
        out_specs=VMEM,
        scratch_shapes=[pltpu.SemaphoreType.DMA((2,))],
        compiler_params=SMALL,
    )(*[pltpu.with_memory_space_constraint(x, pltpu.HBM) for x in (keys, values)])


def pick_kernel(lists_ref, pieces_ref, out_ref):
    heads, receivers, picks = out_ref.shape[:3]
    lists = lists_ref[...]
    for h in range(heads):
        for receiver in range(receivers):
            for s in range(picks):
                block = lists[h, receiver, s + 1]
                out_ref[h, receiver, s] = pieces_ref[block, :, :, h * HD : (h + 1) * HD]


def pick_pieces(lists, pieces):
    heads, ranks, slots = lists.shape
    share = pieces.shape[2]
    if share % 16:
        by_head = pieces.reshape(ranks, 2, share, heads, HD).transpose(3, 0, 1, 2, 4)
        return jax.vmap(lambda list_, part: part[list_[:, 1:]])(lists, by_head)
    return pl.pallas_call(
        pick_kernel,
        out_shape=pltpu.VMEM((heads, ranks, slots - 1, 2, share, HD), pieces.dtype),
        in_specs=[VMEM, VMEM],
        out_specs=VMEM,
        compiler_params=SMALL,
    )(*in_vmem(lists, pieces))


def units_of(heads_here):
    return [(h, begin) for h in range(heads_here) for begin in range(0, BLK, CHUNK)]


def in_turn(units, score, finish):
    held = [score(*unit) for unit in units[: AHEAD - 1]]
    for i, unit in enumerate(units):
        if i + AHEAD - 1 < len(units):
            held.append(score(*units[i + AHEAD - 1]))
        finish(*unit, held.pop(0))


def near_kernel(
    query_ref, key_ref, value_ref, split_ref, top_ref, sum_ref, acc_ref, turned, valued
):
    turned[:HD] = key_ref[...].T
    turned[HD:] = turned[:HD]
    valued[:, :HD] = value_ref[...]
    valued[:, HD:] = jnp.ones(value_ref.shape, valued.dtype)
    heads_here = query_ref.shape[1] // HD

    for h in range(heads_here):
        scaled = query_ref[:, h * HD : (h + 1) * HD].astype(jnp.float32) * FACTOR
        high = scaled.astype(jnp.bfloat16)
        split_ref[h, :, :HD] = high
        split_ref[h, :, HD:] = (scaled - high.astype(jnp.float32)).astype(jnp.bfloat16)

    def score(h, begin):
        end = begin + CHUNK
        scores = jnp.dot(
            split_ref[h, begin:end], turned[:, :end], preferred_element_type=jnp.float32
        )
        row_ids = lax.broadcasted_iota(jnp.int32, scores.shape, 0) + begin
        col_ids = lax.broadcasted_iota(jnp.int32, scores.shape, 1)
        return jnp.where(row_ids >= col_ids, scores, -jnp.inf)

    def finish(h, begin, scores):
        rows = slice(begin, begin + CHUNK)
        top = jnp.max(scores, axis=1, keepdims=True)
        weights = jnp.exp2(scores - top).astype(jnp.bfloat16)
        product = jnp.dot(
            weights, valued[: begin + CHUNK], preferred_element_type=jnp.float32
        )
        top_ref[h, rows] = jnp.broadcast_to(top, (CHUNK, HD))
        sum_ref[h, rows] = product[:, HD:]
        acc_ref[h, rows] = product[:, :HD]

    in_turn(units_of(heads_here), score, finish)


def attend_near(queries, own_keys, own_values):
    rows, columns = queries.shape
    heads_here = columns // HD
    part = pltpu.VMEM((heads_here, rows, HD), jnp.float32)
    return pl.pallas_call(
        near_kernel,
        out_shape=[pltpu.VMEM((heads_here, rows, 2 * HD), jnp.bfloat16), part, part, part],
        in_specs=[VMEM] * 3,
        out_specs=[VMEM] * 4,
        scratch_shapes=[
            pltpu.VMEM((2 * HD, BLK), jnp.bfloat16),
            pltpu.VMEM((BLK, 2 * HD), jnp.bfloat16),
        ],
        compiler_params=LARGE,
        cost_estimate=pl.CostEstimate(
            flops=4 * columns * rows * BLK, bytes_accessed=4 << 20, transcendentals=0
        ),
    )(queries, own_keys, own_values)


def far_kernel(
    live_ref, split_ref, key_ref, far_ref, top_ref, sum_ref, acc_ref, out_ref,
    turned, valued, ready, sems,
):
    heads_here = split_ref.shape[0]
    spare = jnp.broadcast_to(key_ref[0:1, :], (BLK, HD))
    none = jnp.zeros((BLK, HD), jnp.bfloat16)
    for s in range(far_ref.shape[1]):
        rows = slice(s * BLK, (s + 1) * BLK)
        live = jnp.broadcast_to(live_ref[s], (BLK, HD)) > 0
        turned[:HD, rows] = jnp.where(live, far_ref[:, s, 0].reshape(BLK, HD), spare).T
        valued[rows, :HD] = jnp.where(live, far_ref[:, s, 1].reshape(BLK, HD), none)
        valued[rows, HD:] = jnp.where(live, jnp.ones_like(none), none)
    turned[HD:] = turned[:HD]
    copies = []

    def score(h, begin):
        query_rows = split_ref[h, begin : begin + CHUNK]
        return jnp.dot(query_rows, turned[...], preferred_element_type=jnp.float32)

    def finish(h, begin, scores):
        rows = slice(begin, begin + CHUNK)
        near_top = top_ref[h, rows]
        top = jnp.maximum(jnp.max(scores, axis=1, keepdims=True), near_top[:, :1])
        weights = jnp.exp2(scores - top).astype(jnp.bfloat16)
        product = jnp.dot(weights, valued[...], preferred_element_type=jnp.float32)
        scale = jnp.exp2(near_top - top)
        total = product[:, HD:] + sum_ref[h, rows] * scale
        product = product[:, :HD] + acc_ref[h, rows] * scale
        ready[h, rows] = (product / total).astype(ready.dtype)
        if begin + CHUNK == BLK:
            columns = slice(h * HD, (h + 1) * HD)
            copies.append(pltpu.make_async_copy(ready.at[h], out_ref.at[:, columns], sems.at[h]))
            copies[-1].start()

    in_turn(units_of(heads_here), score, finish)
    for copy in copies:
        copy.wait()


def attend_far(live, own_keys, far, near):
    split, near_top, near_sum, near_acc = in_vmem(*near)
    heads_here, rows, _ = near_top.shape
    keys_here = far.shape[1] * BLK
    return pl.pallas_call(
        far_kernel,
        out_shape=jax.ShapeDtypeStruct((rows, heads_here * HD), jnp.bfloat16),
        in_specs=[VMEM] * 7,
        out_specs=ANY,
        scratch_shapes=[
            pltpu.VMEM((2 * HD, keys_here), jnp.bfloat16),
            pltpu.VMEM((keys_here, 2 * HD), jnp.bfloat16),
            pltpu.VMEM((heads_here, rows, HD), jnp.bfloat16),
            pltpu.SemaphoreType.DMA((heads_here,)),
        ],
        compiler_params=LARGE,
    )(*in_vmem(live), split, *in_vmem(own_keys, far), near_top, near_sum, near_acc)


def other_head(x):
    return lax.ppermute(x, "head", [(0, 1), (1, 0)])


def own_block(keys, values, heads, head_rank):
    if heads == 2:
        columns = lambda rank: jnp.stack(
            [lax.dynamic_slice_in_dim(x, rank * HD, HD, 1) for x in (keys, values)]
        )
        mine = columns(head_rank)
        came = other_head(columns(1 - head_rank))
        return jnp.where(
            head_rank == 0,
            jnp.concatenate([mine, came], axis=1),
            jnp.concatenate([came, mine], axis=1),
        )
    by_head = jnp.stack([keys, values]).reshape(2, -1, heads, HD).transpose(2, 0, 1, 3)
    own = lax.all_to_all(by_head, "head", split_axis=0, concat_axis=0, tiled=True)
    return own.transpose(1, 0, 2, 3).reshape(2, BLK, HD)


def lists_of_heads(lists, heads, head_rank):
    if heads == 2:
        came = other_head(lists)
        return jnp.where(head_rank == 0, jnp.stack([lists, came]), jnp.stack([came, lists]))
    copies = jnp.broadcast_to(lists[None], (heads, *lists.shape))
    return lax.all_to_all(copies, "head", split_axis=0, concat_axis=0, tiled=True)


def on_device(heads, ranks, queries, keys, values, selected):
    lists = selected[0]
    picks = lists.shape[1] - 1
    head_rank = lax.axis_index("head")
    ctx_rank = lax.axis_index("ctx")
    share = keys.shape[0] // ranks

    pieces = pack_rows(keys, values, ranks)
    pieces = lax.all_to_all(pieces, "ctx", split_axis=0, concat_axis=0, tiled=True)

    far = pick_pieces(lists_of_heads(lists, heads, head_rank), pieces)
    far = far.reshape(heads * ranks, picks, 2, share, HD)
    far = lax.all_to_all(far, ("head", "ctx"), split_axis=0, concat_axis=0, tiled=True)
    if share % 16:
        far = far.transpose(1, 2, 0, 3, 4).reshape(1, picks, 2, BLK, HD)

    own = own_block(keys, values, heads, head_rank)
    near = attend_near(queries, own[0], own[1])

    chosen = lax.dynamic_index_in_dim(lists, ctx_rank, 0, keepdims=False)[1:]
    live = (chosen != ctx_rank).astype(jnp.float32)
    live = jnp.broadcast_to(live[:, None, None], (picks, 1, HD))
    return attend_far(live, own[0], far, near)


def solution(mesh):
    return jax.shard_map(
        functools.partial(on_device, mesh.shape["head"], mesh.shape["ctx"]),
        mesh=mesh,
        in_specs=(
            P("ctx", "head"),
            P(("ctx", "head"), None),
            P(("ctx", "head"), None),
            P("head", None, None),
        ),
        out_specs=P("ctx", "head"),
        check_vma=False,
    )
```

time: 45.8 us -> 45.6 us (level)
  waiting for transfers between devices: 20.3 us -> 16.9 us
  starting transfers between devices: 11.8 us -> 13.7 us
  Pallas kernels: 7.84 us -> 8.49 us
  local copies, waits for them, and re-layouts: 5.09 us -> 5.68 us
    all_to_all x2, waiting for transfers between devices: 15.5 us -> 7.32 us  [the longest x1 6.28 us: on_device(): lax.all_to_all(pieces, 'ctx', split_axis=0, concat_axis=0, tiled=True)]
    ppermute x1 -> x2, waiting for transfers between devices: 4.84 us -> 9.61 us  [other_head(): return lax.ppermute(x, 'head', [(0, 1), (1, 0)])]
    ppermute x1 -> x2, starting transfers between devices: 0.82 us -> 3.39 us  [other_head(): return lax.ppermute(x, 'head', [(0, 1), (1, 0)])]
    all_to_all x2, starting transfers between devices: 11 us -> 10.3 us  [the longest x1 7.4 us: on_device(): lax.all_to_all(pieces, 'ctx', split_axis=0, concat_axis=0, tiled=True)]
    pallas_call x4, Pallas kernels: 7.84 us -> 8.49 us  [the longest x1 3.69 us: attend_far(): pl.pallas_call(far_kernel, out_shape=jax.ShapeDtypeStruct((rows, heads_he...]
    unnamed x16 -> x18, local copies, waits for them, and re-layouts: 4.94 us -> 5.45 us
  transfers between devices with their start and end apart: 3 -> 4, of which waited for: 3 -> 4; matrix products, arithmetic and copies ran while one was open for 1% -> 1% of each run, Pallas kernels for 3% -> 5%
where the time goes in v4:
time: 45.6 us; the launch traced here: 45.2 us
  waiting for transfers between devices  16.9 us (37%)
  starting transfers between devices  13.7 us (30%)
  Pallas kernels  8.49 us (19%)
  local copies, waits for them, and re-layouts  5.68 us (12%)
    ppermute x2, waiting for transfers between devices, other_head(): return lax.ppermute(x, 'head', [(0, 1), (1, 0)])  9.61 us
    all_to_all x1, starting transfers between devices, on_device(): lax.all_to_all(pieces, 'ctx', split_axis=0, concat_axis=0, tiled=True)  7.4 us
    all_to_all x1, waiting for transfers between devices, on_device(): lax.all_to_all(pieces, 'ctx', split_axis=0, concat_axis=0, tiled=True)  6.28 us
    unnamed x18, local copies, waits for them, and re-layouts  5.45 us
    pallas_call x1, Pallas kernels, attend_far(): pl.pallas_call(far_kernel, out_shape=jax.ShapeDtypeStruct((rows, heads_he...  3.69 us
    ppermute x2, starting transfers between devices, other_head(): return lax.ppermute(x, 'head', [(0, 1), (1, 0)])  3.39 us
    all_to_all x1, starting transfers between devices, on_device(): lax.all_to_all(far, ('head', 'ctx'), split_axis=0, concat_axis=0, tiled=T...  2.89 us
    pallas_call x1, Pallas kernels, attend_near(): pl.pallas_call(near_kernel, out_shape=[pltpu.VMEM((heads_here, rows, 2 *...  2.12 us
  transfers between devices with their start and end apart: 4, of which 4 were waited for; matrix products, arithmetic and copies ran while one was open for 1% of the time, Pallas kernels for 5%

profile of v4, /device:TPU:0, one launch (start us, length us, event | category | flops | bytes accessed | tf_op | source)
XLA Modules:
  0.0 45.2 jit_solution(3971389992514813838)
XLA Ops:
  0.0 1.7 %shard_map.47 = bf16[16,2,16,256]{3,2,1,0:T(8,128)(2,1)} custom-call(bf16[16,16,256]{2,1,0:T(8,128)(2,1)} %bitcast.20, bf16[16,16,256]{2,1,0:T(8,128)(2,1)} %bitcast.19), custom_call_target="tpu_custom_call" | custom-call | tf_op jit(solution)/shard_map/pallas_call | solution.py:44
  1.7 0.0 copy-start.7
  1.7 7.4 %all-to-all-start = ((bf16[16,2,16,256]{3,2,1,0:T(8,128)(2,1)}), bf16[16,2,16,256]{3,2,1,0:T(8,128)(2,1)S(1)}, u32[]{:S(2)}, u32[]{:S(2)}) async-start(bf16[16,2,16,256]{3,2,1,0:T(8,128)(2,1)} %shard_map.47), calls=%async_computation | async-start | bytes 524288 | tf_op jit(solution)/shard_map/all_to_all | solution.py:245
  9.1 1.6 %collective-permute-start.1 = (s32[16,3]{0,1:T(4,128)S(1)}, s32[16,3]{0,1:T(4,128)S(1)}, u32[]{:S(2)}, u32[]{:S(2)}) collective-permute-start(s32[16,3]{0,1:T(4,128)S(1)} %bitcast.22), channel_id=1, source_target_pairs={{0,16},{16,0},{1,17},{17,1},{2,18},{18,2},{3,19},{19,3},{4,20},{20... | collective-permute-start | bytes 584 | tf_op jit(solution)/shard_map/ppermute | solution.py:209
  10.7 0.1 copy.17
  10.8 2.0 %collective-permute-done.1 = s32[16,3]{0,1:T(4,128)S(1)} collective-permute-done((s32[16,3]{0,1:T(4,128)S(1)}, s32[16,3]{0,1:T(4,128)S(1)}, u32[]{:S(2)}, u32[]{:S(2)}) %collective-permute-start.1) | collective-permute-done | bytes 224 | tf_op jit(solution)/shard_map/ppermute | solution.py:209
  12.8 0.1 copy.18
  12.9 6.3 %all-to-all-done.pieces_ref = bf16[16,2,16,256]{3,2,1,0:T(8,128)(2,1)S(1)} async-done(((bf16[16,2,16,256]{3,2,1,0:T(8,128)(2,1)}), bf16[16,2,16,256]{3,2,1,0:T(8,128)(2,1)S(1)}, u32[]{:S(2)}, u32[]{:S(2)}) %all-to-all-start) | async-done | bytes 262176 | tf_op jit(solution)/shard_map/all_to_all | solution.py:245
  19.2 1.0 %shard_map.48 = bf16[2,16,2,2,16,128]{5,4,3,2,1,0:T(8,128)(2,1)} custom-call(s32[2,16,3]{2,1,0:T(8,128)S(1)} %add_select_fusion.lists_ref, bf16[16,2,16,256]{3,2,1,0:T(8,128)(2,1)S(1)} %all-to-all-done.pieces_ref), custom_call_target="tpu_custom_call" | custom-call | tf_op jit(solution)/shard_map/pallas_call | solution.py:70
  20.2 2.9 %all-to-all-start.1 = ((bf16[32,2,2,16,128]{4,3,2,1,0:T(8,128)(2,1)}), bf16[32,2,2,16,128]{4,3,2,1,0:T(8,128)(2,1)S(1)}, u32[]{:S(2)}, u32[]{:S(2)}) async-start(bf16[32,2,2,16,128]{4,3,2,1,0:T(8,128)(2,1)} %bitcast.9), calls=%async_computation.1 | async-start | bytes 1048576 | tf_op jit(solution)/shard_map/all_to_all | solution.py:249
  23.1 0.1 dynamic-slice_bitcast_fusion.2
  23.2 1.8 %collective-permute-start = (bf16[2,256,128]{2,1,0:T(8,128)(2,1)S(1)}, bf16[2,256,128]{2,1,0:T(8,128)(2,1)S(1)}, u32[]{:S(2)}, u32[]{:S(2)}) collective-permute-start(bf16[2,256,128]{2,1,0:T(8,128)(2,1)S(1)} %pad_maximum_fusion), channel_id=1, source_target_pairs={{0,16},{16,0},{1,17},{17,1},{2,18},{18,2},{3,19},{19,3},{4,20},{20... | collective-permute-start | bytes 393224 | tf_op jit(solution)/shard_map/ppermute | solution.py:209
  25.0 0.2 fusion
  25.2 7.6 %collective-permute-done = bf16[2,256,128]{2,1,0:T(8,128)(2,1)S(1)} collective-permute-done((bf16[2,256,128]{2,1,0:T(8,128)(2,1)S(1)}, bf16[2,256,128]{2,1,0:T(8,128)(2,1)S(1)}, u32[]{:S(2)}, u32[]{:S(2)}) %collective-permute-start) | collective-permute-done | bytes 131104 | tf_op jit(solution)/shard_map/ppermute | solution.py:209
  32.8 0.1 maximum_select_fusion
  32.9 0.9 %copy-done.4 = bf16[512,512]{1,0:T(8,128)(2,1)S(1)} copy-done((bf16[512,512]{1,0:T(8,128)(2,1)S(1)}, bf16[512,512]{1,0:T(8,128)(2,1)}, u32[]{:S(2)}) %copy-start.4) | copy-done | bytes 524312
  33.8 2.1 %shard_map.46 = (bf16[4,512,256]{2,1,0:T(8,128)(2,1)S(1)}, f32[4,512,128]{2,1,0:T(8,128)S(1)}, f32[4,512,128]{2,1,0:T(8,128)S(1)}, f32[4,512,128]{2,1,0:T(8,128)S(1)}) custom-call(bf16[512,512]{1,0:T(8,128)(2,1)S(1)} %copy-done.4, bf16[512,128]{1,0:T(8,128)(2,1)S(1)} %get-tuple-element.14.key_ref, bf16[512,128]{1,0:T(8,128)(2,1)S(1)} %get-tuple-element.13.value_ref), custom_call_target="tpu_custom_call" | custom-call | flops 536870912 | bytes 4194304 | tf_op jit(solution)/shard_map/pallas_call | solution.py:133
  35.9 1.0 %copy-done = f32[4,512,128]{2,1,0:T(8,128)} copy-done((f32[4,512,128]{2,1,0:T(8,128)}, f32[4,512,128]{2,1,0:T(8,128)S(1)}, u32[]{:S(2)}) %copy-start) | copy-done | bytes 1048600
  36.9 1.0 %copy-done.2 = f32[4,512,128]{2,1,0:T(8,128)} copy-done((f32[4,512,128]{2,1,0:T(8,128)}, f32[4,512,128]{2,1,0:T(8,128)S(1)}, u32[]{:S(2)}) %copy-start.2) | copy-done | bytes 1048600
  37.9 1.0 %all-to-all-done.1.far_ref = bf16[32,2,2,16,128]{4,3,2,1,0:T(8,128)(2,1)S(1)} async-done(((bf16[32,2,2,16,128]{4,3,2,1,0:T(8,128)(2,1)}), bf16[32,2,2,16,128]{4,3,2,1,0:T(8,128)(2,1)S(1)}, u32[]{:S(2)}, u32[]{:S(2)}) %all-to-all-start.1) | async-done | bytes 524320 | tf_op jit(solution)/shard_map/all_to_all | solution.py:249
  39.0 0.1 broadcast_in_dim.2.live_ref
  39.0 1.2 %copy-done.1 = f32[4,512,128]{2,1,0:T(8,128)S(1)} copy-done((f32[4,512,128]{2,1,0:T(8,128)S(1)}, f32[4,512,128]{2,1,0:T(8,128)}, u32[]{:S(2)}) %copy-start.1) | copy-done | bytes 1048600
  40.3 1.2 %copy-done.3 = f32[4,512,128]{2,1,0:T(8,128)S(1)} copy-done((f32[4,512,128]{2,1,0:T(8,128)S(1)}, f32[4,512,128]{2,1,0:T(8,128)}, u32[]{:S(2)}) %copy-start.3) | copy-done | bytes 1048600
  41.5 3.7 %shard_map.49 = bf16[512,512]{1,0:T(8,128)(2,1)} custom-call(f32[2,1,128]{2,1,0:T(1,128)S(1)} %broadcast_in_dim.2.live_ref, bf16[4,512,256]{2,1,0:T(8,128)(2,1)S(1)} %get-tuple-element.9.split_ref, bf16[512,128]{1,0:T(8,128)(2,1)S(1)} %get-tuple-element.14.key_ref, bf16[32,2,2,16,128]{4,3,2,1,0:T(8,128)(2,1)S(1)} %all-to-all-done.1.far_ref, ...), custom_call_target="tpu_custom_call" | custom-call | tf_op jit(solution)/shard_map/pallas_call | solution.py:193
  (14 shorter events, 0.1 us)
Async XLA Ops:
  1.7 7.4 %copy-start.7 = (s32[1,16,3]{1,0,2:T(1,128)S(1)}, s32[1,16,3]{1,0,2:T(1,128)}, u32[]{:S(2)}) copy-start(s32[1,16,3]{1,0,2:T(1,128)} %param.7) | copy-start | bytes 580
  1.7 17.5 %all-to-all-start = ((bf16[16,2,16,256]{3,2,1,0:T(8,128)(2,1)}), bf16[16,2,16,256]{3,2,1,0:T(8,128)(2,1)S(1)}, u32[]{:S(2)}, u32[]{:S(2)}) async-start(bf16[16,2,16,256]{3,2,1,0:T(8,128)(2,1)} %shard_map.47), calls=%async_computation | async-start | bytes 524288 | tf_op jit(solution)/shard_map/all_to_all | solution.py:245
  9.1 3.7 %collective-permute-start.1 = (s32[16,3]{0,1:T(4,128)S(1)}, s32[16,3]{0,1:T(4,128)S(1)}, u32[]{:S(2)}, u32[]{:S(2)}) collective-permute-start(s32[16,3]{0,1:T(4,128)S(1)} %bitcast.22), channel_id=1, source_target_pairs={{0,16},{16,0},{1,17},{17,1},{2,18},{18,2},{3,19},{19,3},{4,20},{20... | collective-permute-start | bytes 584 | tf_op jit(solution)/shard_map/ppermute | solution.py:209
  20.2 2.9 %copy-start.5 = (bf16[256,256]{1,0:T(8,128)(2,1)S(1)}, bf16[256,256]{1,0:T(8,128)(2,1)}, u32[]{:S(2)}) copy-start(bf16[256,256]{1,0:T(8,128)(2,1)} %param.6) | copy-start | bytes 393220
  20.2 2.9 %copy-start.6 = (bf16[256,256]{1,0:T(8,128)(2,1)S(1)}, bf16[256,256]{1,0:T(8,128)(2,1)}, u32[]{:S(2)}) copy-start(bf16[256,256]{1,0:T(8,128)(2,1)} %param.5) | copy-start | bytes 393220
  20.2 18.8 %all-to-all-start.1 = ((bf16[32,2,2,16,128]{4,3,2,1,0:T(8,128)(2,1)}), bf16[32,2,2,16,128]{4,3,2,1,0:T(8,128)(2,1)S(1)}, u32[]{:S(2)}, u32[]{:S(2)}) async-start(bf16[32,2,2,16,128]{4,3,2,1,0:T(8,128)(2,1)} %bitcast.9), calls=%async_computation.1 | async-start | bytes 1048576 | tf_op jit(solution)/shard_map/all_to_all | solution.py:249
  23.2 9.6 %collective-permute-start = (bf16[2,256,128]{2,1,0:T(8,128)(2,1)S(1)}, bf16[2,256,128]{2,1,0:T(8,128)(2,1)S(1)}, u32[]{:S(2)}, u32[]{:S(2)}) collective-permute-start(bf16[2,256,128]{2,1,0:T(8,128)(2,1)S(1)} %pad_maximum_fusion), channel_id=1, source_target_pairs={{0,16},{16,0},{1,17},{17,1},{2,18},{18,2},{3,19},{19,3},{4,20},{20... | collective-permute-start | bytes 393224 | tf_op jit(solution)/shard_map/ppermute | solution.py:209
  32.8 1.0 %copy-start.4 = (bf16[512,512]{1,0:T(8,128)(2,1)S(1)}, bf16[512,512]{1,0:T(8,128)(2,1)}, u32[]{:S(2)}) copy-start(bf16[512,512]{1,0:T(8,128)(2,1)} %query_ref.1) | copy-start | bytes 1572868
  35.9 1.0 %copy-start = (f32[4,512,128]{2,1,0:T(8,128)}, f32[4,512,128]{2,1,0:T(8,128)S(1)}, u32[]{:S(2)}) copy-start(f32[4,512,128]{2,1,0:T(8,128)S(1)} %get-tuple-element.11.sum_ref) | copy-start | bytes 3145732
  36.9 1.0 %copy-start.2 = (f32[4,512,128]{2,1,0:T(8,128)}, f32[4,512,128]{2,1,0:T(8,128)S(1)}, u32[]{:S(2)}) copy-start(f32[4,512,128]{2,1,0:T(8,128)S(1)} %get-tuple-element.12.acc_ref) | copy-start | bytes 3145732
  39.0 1.2 %copy-start.1 = (f32[4,512,128]{2,1,0:T(8,128)S(1)}, f32[4,512,128]{2,1,0:T(8,128)}, u32[]{:S(2)}) copy-start(f32[4,512,128]{2,1,0:T(8,128)} %copy-done) | copy-start | bytes 3145732
  40.3 1.2 %copy-start.3 = (f32[4,512,128]{2,1,0:T(8,128)S(1)}, f32[4,512,128]{2,1,0:T(8,128)}, u32[]{:S(2)}) copy-start(f32[4,512,128]{2,1,0:T(8,128)} %copy-done.2) | copy-start | bytes 3145732

commit v5 on v4

--- a/solution.py
+++ b/solution.py
@@ -12,6 +12,7 @@
 BLK = 512
 CHUNK = 128
 AHEAD = 2
+PARTS = 4
 FACTOR = math.log2(math.e) / math.sqrt(HD)
 SMALL = pltpu.CompilerParams(vmem_limit_bytes=2 * 1024 * 1024)
 LARGE = pltpu.CompilerParams(vmem_limit_bytes=12 * 1024 * 1024)
@@ -23,14 +24,24 @@
     return [pltpu.with_memory_space_constraint(x, pltpu.VMEM) for x in arrays]
 
 
-def pack_kernel(key_ref, value_ref, out_ref, sems):
-    copies = [
-        pltpu.make_async_copy(ref, out_ref.at[:, kv], sems.at[kv])
-        for kv, ref in enumerate((key_ref, value_ref))
-    ]
-    for copy in copies:
+def pack_kernel(key_ref, value_ref, out_ref, held, sems):
+    ranks = key_ref.shape[0]
+    step = ranks // PARTS
+    arrive, leave = [], []
+    for part in range(PARTS):
+        rows = slice(part * step, (part + 1) * step)
+        for kv, ref in enumerate((key_ref, value_ref)):
+            place = held.at[rows, kv]
+            arrive.append(pltpu.make_async_copy(ref.at[rows], place, sems.at[0, part, kv]))
+            leave.append(
+                pltpu.make_async_copy(place, out_ref.at[rows, kv], sems.at[1, part, kv])
+            )
+    for copy in arrive:
         copy.start()
-    for copy in copies:
+    for copy, after in zip(arrive, leave):
+        copy.wait()
+        after.start()
+    for copy in leave:
         copy.wait()
 
 
@@ -39,14 +50,18 @@
     share = held // ranks
     keys = keys.reshape(ranks, share, columns)
     values = values.reshape(ranks, share, columns)
-    if share % 16:
+    if share % 16 or ranks % PARTS:
         return jnp.stack([keys, values], axis=1)
+    shape = (ranks, 2, share, columns)
     return pl.pallas_call(
         pack_kernel,
-        out_shape=pltpu.VMEM((ranks, 2, share, columns), keys.dtype),
+        out_shape=jax.ShapeDtypeStruct(shape, keys.dtype),
         in_specs=[ANY, ANY],
-        out_specs=VMEM,
-        scratch_shapes=[pltpu.SemaphoreType.DMA((2,))],
+        out_specs=ANY,
+        scratch_shapes=[
+            pltpu.VMEM(shape, keys.dtype),
+            pltpu.SemaphoreType.DMA((2, PARTS, 2)),
+        ],
         compiler_params=SMALL,
     )(*[pltpu.with_memory_space_constraint(x, pltpu.HBM) for x in (keys, values)])
 
@@ -88,26 +103,25 @@
         finish(*unit, held.pop(0))
 
 
+def split_queries(query_rows):
+    scaled = query_rows.astype(jnp.float32) * FACTOR
+    high = scaled.astype(jnp.bfloat16)
+    low = (scaled - high.astype(jnp.float32)).astype(jnp.bfloat16)
+    return jnp.concatenate([high, low], axis=1)
+
+
 def near_kernel(
-    query_ref, key_ref, value_ref, split_ref, top_ref, sum_ref, acc_ref, turned, valued
+    query_ref, key_ref, value_ref, level_ref, mean_ref, turned, valued
 ):
     turned[:HD] = key_ref[...].T
     turned[HD:] = turned[:HD]
     valued[:, :HD] = value_ref[...]
     valued[:, HD:] = jnp.ones(value_ref.shape, valued.dtype)
-    heads_here = query_ref.shape[1] // HD
-
-    for h in range(heads_here):
-        scaled = query_ref[:, h * HD : (h + 1) * HD].astype(jnp.float32) * FACTOR
-        high = scaled.astype(jnp.bfloat16)
-        split_ref[h, :, :HD] = high
-        split_ref[h, :, HD:] = (scaled - high.astype(jnp.float32)).astype(jnp.bfloat16)
 
     def score(h, begin):
         end = begin + CHUNK
-        scores = jnp.dot(
-            split_ref[h, begin:end], turned[:, :end], preferred_element_type=jnp.float32
-        )
+        query_rows = split_queries(query_ref[begin:end, h * HD : (h + 1) * HD])
+        scores = jnp.dot(query_rows, turned[:, :end], preferred_element_type=jnp.float32)
         row_ids = lax.broadcasted_iota(jnp.int32, scores.shape, 0) + begin
         col_ids = lax.broadcasted_iota(jnp.int32, scores.shape, 1)
         return jnp.where(row_ids >= col_ids, scores, -jnp.inf)
@@ -119,22 +133,19 @@
         product = jnp.dot(
             weights, valued[: begin + CHUNK], preferred_element_type=jnp.float32
         )
-        top_ref[h, rows] = jnp.broadcast_to(top, (CHUNK, HD))
-        sum_ref[h, rows] = product[:, HD:]
-        acc_ref[h, rows] = product[:, :HD]
-
-    in_turn(units_of(heads_here), score, finish)
+        level_ref[h, rows] = top + jnp.log2(product[:, HD:])
+        mean_ref[h, rows] = product[:, :HD] / product[:, HD:]
+
+    in_turn(units_of(query_ref.shape[1] // HD), score, finish)
 
 
 def attend_near(queries, own_keys, own_values):
     rows, columns = queries.shape
-    heads_here = columns // HD
-    part = pltpu.VMEM((heads_here, rows, HD), jnp.float32)
     return pl.pallas_call(
         near_kernel,
-        out_shape=[pltpu.VMEM((heads_here, rows, 2 * HD), jnp.bfloat16), part, part, part],
+        out_shape=[pltpu.VMEM((columns // HD, rows, HD), jnp.float32)] * 2,
         in_specs=[VMEM] * 3,
-        out_specs=[VMEM] * 4,
+        out_specs=[VMEM] * 2,
         scratch_shapes=[
             pltpu.VMEM((2 * HD, BLK), jnp.bfloat16),
             pltpu.VMEM((BLK, 2 * HD), jnp.bfloat16),
@@ -147,11 +158,9 @@
 
 
 def far_kernel(
-    live_ref, split_ref, key_ref, far_ref, top_ref, sum_ref, acc_ref, out_ref,
-    turned, valued, ready, sems,
+    live_ref, query_ref, key_ref, far_ref, level_ref, mean_ref, out_ref, turned, valued, ready, sems
 ):
-    heads_here = split_ref.shape[0]
-    spare = jnp.broadcast_to(key_ref[0:1, :], (BLK, HD))
+    spare = jnp.broadcast_to(key_ref[...], (BLK, HD))
     none = jnp.zeros((BLK, HD), jnp.bfloat16)
     for s in range(far_ref.shape[1]):
         rows = slice(s * BLK, (s + 1) * BLK)
@@ -163,46 +172,45 @@
     copies = []
 
     def score(h, begin):
-        query_rows = split_ref[h, begin : begin + CHUNK]
+        query_rows = split_queries(query_ref[begin : begin + CHUNK, h * HD : (h + 1) * HD])
         return jnp.dot(query_rows, turned[...], preferred_element_type=jnp.float32)
 
     def finish(h, begin, scores):
         rows = slice(begin, begin + CHUNK)
-        near_top = top_ref[h, rows]
-        top = jnp.maximum(jnp.max(scores, axis=1, keepdims=True), near_top[:, :1])
+        level = level_ref[h, rows]
+        top = jnp.maximum(jnp.max(scores, axis=1, keepdims=True), level[:, :1])
         weights = jnp.exp2(scores - top).astype(jnp.bfloat16)
         product = jnp.dot(weights, valued[...], preferred_element_type=jnp.float32)
-        scale = jnp.exp2(near_top - top)
-        total = product[:, HD:] + sum_ref[h, rows] * scale
-        product = product[:, :HD] + acc_ref[h, rows] * scale
+        scale = jnp.exp2(level - top)
+        total = product[:, HD:] + scale
+        product = product[:, :HD] + mean_ref[h, rows] * scale
         ready[h, rows] = (product / total).astype(ready.dtype)
         if begin + CHUNK == BLK:
             columns = slice(h * HD, (h + 1) * HD)
             copies.append(pltpu.make_async_copy(ready.at[h], out_ref.at[:, columns], sems.at[h]))
             copies[-1].start()
 
-    in_turn(units_of(heads_here), score, finish)
+    in_turn(units_of(query_ref.shape[1] // HD), score, finish)
     for copy in copies:
         copy.wait()
 
 
-def attend_far(live, own_keys, far, near):
-    split, near_top, near_sum, near_acc = in_vmem(*near)
-    heads_here, rows, _ = near_top.shape
+def attend_far(live, queries, first_key, far, near):
+    rows, columns = queries.shape
     keys_here = far.shape[1] * BLK
     return pl.pallas_call(
         far_kernel,
-        out_shape=jax.ShapeDtypeStruct((rows, heads_here * HD), jnp.bfloat16),
-        in_specs=[VMEM] * 7,
+        out_shape=jax.ShapeDtypeStruct(queries.shape, queries.dtype),
+        in_specs=[VMEM] * 6,
         out_specs=ANY,
         scratch_shapes=[
             pltpu.VMEM((2 * HD, keys_here), jnp.bfloat16),
             pltpu.VMEM((keys_here, 2 * HD), jnp.bfloat16),
-            pltpu.VMEM((heads_here, rows, HD), jnp.bfloat16),
-            pltpu.SemaphoreType.DMA((heads_here,)),
+            pltpu.VMEM((columns // HD, rows, HD), jnp.bfloat16),
+            pltpu.SemaphoreType.DMA((columns // HD,)),
         ],
         compiler_params=LARGE,
-    )(*in_vmem(live), split, *in_vmem(own_keys, far), near_top, near_sum, near_acc)
+    )(*in_vmem(live, queries, first_key, far, *near))
 
 
 def other_head(x):
@@ -244,19 +252,22 @@
     pieces = pack_rows(keys, values, ranks)
     pieces = lax.all_to_all(pieces, "ctx", split_axis=0, concat_axis=0, tiled=True)
 
-    far = pick_pieces(lists_of_heads(lists, heads, head_rank), pieces)
+    own = own_block(keys, values, heads, head_rank)
+    every_list = lists_of_heads(lists, heads, head_rank)
+    pieces, own, every_list = lax.optimization_barrier((pieces, own, every_list))
+
+    far = pick_pieces(every_list, pieces)
     far = far.reshape(heads * ranks, picks, 2, share, HD)
     far = lax.all_to_all(far, ("head", "ctx"), split_axis=0, concat_axis=0, tiled=True)
     if share % 16:
         far = far.transpose(1, 2, 0, 3, 4).reshape(1, picks, 2, BLK, HD)
 
-    own = own_block(keys, values, heads, head_rank)
     near = attend_near(queries, own[0], own[1])
 
     chosen = lax.dynamic_index_in_dim(lists, ctx_rank, 0, keepdims=False)[1:]
     live = (chosen != ctx_rank).astype(jnp.float32)
     live = jnp.broadcast_to(live[:, None, None], (picks, 1, HD))
-    return attend_far(live, own[0], far, near)
+    return attend_far(live, queries, own[0, :1], far, near)
 
 
 def solution(mesh):

time: 45.6 us -> 43.2 us (0.947)
  local copies, waits for them, and re-layouts: 5.68 us -> 1.17 us
  waiting for transfers between devices: 16.9 us -> 20.3 us
  starting transfers between devices: 13.7 us -> 12.6 us
    all_to_all x1, waiting for transfers between devices: 1.04 us -> 12.7 us  [on_device(): lax.all_to_all(far, ('head', 'ctx'), split_axis=0, concat_axis=0, tiled=T...]
    ppermute x2, waiting for transfers between devices: 9.61 us -> 3.72 us  [other_head(): return lax.ppermute(x, 'head', [(0, 1), (1, 0)])]
    unnamed x18 -> x10, local copies, waits for them, and re-layouts: 5.45 us -> 0.94 us
    all_to_all x1, waiting for transfers between devices: 6.28 us -> 3.8 us  [on_device(): lax.all_to_all(pieces, 'ctx', split_axis=0, concat_axis=0, tiled=True)]
    ppermute x2, starting transfers between devices: 3.39 us -> 2.14 us  [other_head(): return lax.ppermute(x, 'head', [(0, 1), (1, 0)])]
  transfers between devices with their start and end apart: 4 -> 4, of which waited for: 4 -> 3; matrix products, arithmetic and copies ran while one was open for 1% -> 1% of each run, Pallas kernels for 5% -> 5%
where the time goes in v5:
time: 43.2 us; the launch traced here: 42.8 us
  waiting for transfers between devices  20.3 us (47%)
  starting transfers between devices  12.6 us (29%)
  Pallas kernels  8.4 us (19%)
  local copies, waits for them, and re-layouts  1.17 us (3%)
    all_to_all x1, waiting for transfers between devices, on_device(): lax.all_to_all(far, ('head', 'ctx'), split_axis=0, concat_axis=0, tiled=T...  12.7 us
    all_to_all x1, starting transfers between devices, on_device(): lax.all_to_all(pieces, 'ctx', split_axis=0, concat_axis=0, tiled=True)  7.53 us
    all_to_all x1, waiting for transfers between devices, on_device(): lax.all_to_all(pieces, 'ctx', split_axis=0, concat_axis=0, tiled=True)  3.8 us
    ppermute x2, waiting for transfers between devices, other_head(): return lax.ppermute(x, 'head', [(0, 1), (1, 0)])  3.72 us
    pallas_call x1, Pallas kernels, attend_far(): pl.pallas_call(far_kernel, out_shape=jax.ShapeDtypeStruct(queries.shape,...  3.68 us
    all_to_all x1, starting transfers between devices, on_device(): lax.all_to_all(far, ('head', 'ctx'), split_axis=0, concat_axis=0, tiled=T...  2.89 us
    ppermute x2, starting transfers between devices, other_head(): return lax.ppermute(x, 'head', [(0, 1), (1, 0)])  2.14 us
    pallas_call x1, Pallas kernels, attend_near(): pl.pallas_call(near_kernel, out_shape=[pltpu.VMEM((columns // HD, rows, H...  2.1 us
  transfers between devices with their start and end apart: 4, of which 3 were waited for; matrix products, arithmetic and copies ran while one was open for 1% of the time, Pallas kernels for 5%

profile of v5, /device:TPU:0, one launch (start us, length us, event | category | flops | bytes accessed | tf_op | source)
XLA Modules:
  0.0 42.8 jit_solution(4710121194368030691)
XLA Ops:
  0.0 1.6 %shard_map.46 = bf16[16,2,16,256]{3,2,1,0:T(8,128)(2,1)} custom-call(bf16[16,16,256]{2,1,0:T(8,128)(2,1)} %bitcast.22, bf16[16,16,256]{2,1,0:T(8,128)(2,1)} %bitcast.21), custom_call_target="tpu_custom_call" | custom-call | tf_op jit(solution)/shard_map/pallas_call | solution.py:56
  1.6 0.0 copy-start.1
  1.6 0.0 copy-start.2
  1.7 7.5 %all-to-all-start = ((bf16[16,2,16,256]{3,2,1,0:T(8,128)(2,1)}), bf16[16,2,16,256]{3,2,1,0:T(8,128)(2,1)S(1)}, u32[]{:S(2)}, u32[]{:S(2)}) async-start(bf16[16,2,16,256]{3,2,1,0:T(8,128)(2,1)} %shard_map.46), calls=%async_computation | async-start | bytes 524288 | tf_op jit(solution)/shard_map/all_to_all | solution.py:253
  9.2 0.1 dynamic-slice_bitcast_fusion.2
  9.3 0.0 copy-start.3
  9.3 1.6 %collective-permute-start = (bf16[2,256,128]{2,1,0:T(8,128)(2,1)S(1)}, bf16[2,256,128]{2,1,0:T(8,128)(2,1)S(1)}, u32[]{:S(2)}, u32[]{:S(2)}) collective-permute-start(bf16[2,256,128]{2,1,0:T(8,128)(2,1)S(1)} %pad_maximum_fusion), channel_id=1, source_target_pairs={{0,16},{16,0},{1,17},{17,1},{2,18},{18,2},{3,19},{19,3},{4,20},{20... | collective-permute-start | bytes 393224 | tf_op jit(solution)/shard_map/ppermute | solution.py:217
  10.9 0.0 copy-done.3
  10.9 0.6 %collective-permute-start.1 = (s32[16,3]{0,1:T(4,128)S(1)}, s32[16,3]{0,1:T(4,128)S(1)}, u32[]{:S(2)}, u32[]{:S(2)}) collective-permute-start(s32[16,3]{0,1:T(4,128)S(1)} %bitcast.24), channel_id=1, source_target_pairs={{0,16},{16,0},{1,17},{17,1},{2,18},{18,2},{3,19},{19,3},{4,20},{20... | collective-permute-start | bytes 584 | tf_op jit(solution)/shard_map/ppermute | solution.py:217
  11.5 0.1 copy.17
  11.5 3.7 %collective-permute-done.1 = s32[16,3]{0,1:T(4,128)S(1)} collective-permute-done((s32[16,3]{0,1:T(4,128)S(1)}, s32[16,3]{0,1:T(4,128)S(1)}, u32[]{:S(2)}, u32[]{:S(2)}) %collective-permute-start.1) | collective-permute-done | bytes 224 | tf_op jit(solution)/shard_map/ppermute | solution.py:217
  15.3 0.1 copy.18
  15.3 0.0 collective-permute-done
  15.4 0.1 maximum_select_fusion
  15.4 3.8 %all-to-all-done.pieces_ref = bf16[16,2,16,256]{3,2,1,0:T(8,128)(2,1)S(1)} async-done(((bf16[16,2,16,256]{3,2,1,0:T(8,128)(2,1)}), bf16[16,2,16,256]{3,2,1,0:T(8,128)(2,1)S(1)}, u32[]{:S(2)}, u32[]{:S(2)}) %all-to-all-start) | async-done | bytes 262176 | tf_op jit(solution)/shard_map/all_to_all | solution.py:253
  19.2 1.0 %shard_map.47 = bf16[2,16,2,2,16,128]{5,4,3,2,1,0:T(8,128)(2,1)} custom-call(s32[2,16,3]{2,1,0:T(8,128)S(1)} %add_select_fusion.lists_ref, bf16[16,2,16,256]{3,2,1,0:T(8,128)(2,1)S(1)} %all-to-all-done.pieces_ref), custom_call_target="tpu_custom_call" | custom-call | tf_op jit(solution)/shard_map/pallas_call | solution.py:85
  20.2 2.9 %all-to-all-start.1 = ((bf16[32,2,2,16,128]{4,3,2,1,0:T(8,128)(2,1)}), bf16[32,2,2,16,128]{4,3,2,1,0:T(8,128)(2,1)S(1)}, u32[]{:S(2)}, u32[]{:S(2)}) async-start(bf16[32,2,2,16,128]{4,3,2,1,0:T(8,128)(2,1)} %bitcast.8), calls=%async_computation.1 | async-start | bytes 1048576 | tf_op jit(solution)/shard_map/all_to_all | solution.py:261
  23.1 0.0 copy-start
  23.1 0.2 fusion
  23.3 0.8 %copy-done = bf16[512,512]{1,0:T(8,128)(2,1)S(1)} copy-done((bf16[512,512]{1,0:T(8,128)(2,1)S(1)}, bf16[512,512]{1,0:T(8,128)(2,1)}, u32[]{:S(2)}) %copy-start) | copy-done | bytes 524312
  24.2 2.1 %shard_map.48 = (f32[4,512,128]{2,1,0:T(8,128)S(1)}, f32[4,512,128]{2,1,0:T(8,128)S(1)}) custom-call(bf16[512,512]{1,0:T(8,128)(2,1)S(1)} %copy-done, bf16[512,128]{1,0:T(8,128)(2,1)S(1)} %get-tuple-element.16.key_ref, bf16[512,128]{1,0:T(8,128)(2,1)S(1)} %get-tuple-element.15.value_ref), custom_call_target="tpu_custom_call" | custom-call | flops 536870912 | bytes 4194304 | tf_op jit(solution)/shard_map/pallas_call | solution.py:144
  26.3 12.7 %all-to-all-done.1.far_ref = bf16[32,2,2,16,128]{4,3,2,1,0:T(8,128)(2,1)S(1)} async-done(((bf16[32,2,2,16,128]{4,3,2,1,0:T(8,128)(2,1)}), bf16[32,2,2,16,128]{4,3,2,1,0:T(8,128)(2,1)S(1)}, u32[]{:S(2)}, u32[]{:S(2)}) %all-to-all-start.1) | async-done | bytes 524320 | tf_op jit(solution)/shard_map/all_to_all | solution.py:261
  39.0 0.1 broadcast_in_dim.2.live_ref
  39.1 3.7 %shard_map.49 = bf16[512,512]{1,0:T(8,128)(2,1)} custom-call(f32[2,1,128]{2,1,0:T(1,128)S(1)} %broadcast_in_dim.2.live_ref, bf16[512,512]{1,0:T(8,128)(2,1)S(1)} %copy-done, bf16[1,128]{1,0:T(2,128)(2,1)S(1)} %slice_bitcast_fusion.2.key_ref, bf16[32,2,2,16,128]{4,3,2,1,0:T(8,128)(2,1)S(1)} %all-to-all-done.1.far_ref, ...), custom_call_target="tpu_custom_call" | custom-call | tf_op jit(solution)/shard_map/pallas_call | solution.py:201
  (7 shorter events, 0.1 us)
Async XLA Ops:
  1.6 7.6 %copy-start.1 = (bf16[256,256]{1,0:T(8,128)(2,1)S(1)}, bf16[256,256]{1,0:T(8,128)(2,1)}, u32[]{:S(2)}) copy-start(bf16[256,256]{1,0:T(8,128)(2,1)} %param.6) | copy-start | bytes 393220
  1.6 7.6 %copy-start.2 = (bf16[256,256]{1,0:T(8,128)(2,1)S(1)}, bf16[256,256]{1,0:T(8,128)(2,1)}, u32[]{:S(2)}) copy-start(bf16[256,256]{1,0:T(8,128)(2,1)} %param.5) | copy-start | bytes 393220
  1.7 17.6 %all-to-all-start = ((bf16[16,2,16,256]{3,2,1,0:T(8,128)(2,1)}), bf16[16,2,16,256]{3,2,1,0:T(8,128)(2,1)S(1)}, u32[]{:S(2)}, u32[]{:S(2)}) async-start(bf16[16,2,16,256]{3,2,1,0:T(8,128)(2,1)} %shard_map.46), calls=%async_computation | async-start | bytes 524288 | tf_op jit(solution)/shard_map/all_to_all | solution.py:253
  9.3 1.6 %copy-start.3 = (s32[1,16,3]{1,0,2:T(1,128)S(1)}, s32[1,16,3]{1,0,2:T(1,128)}, u32[]{:S(2)}) copy-start(s32[1,16,3]{1,0,2:T(1,128)} %param.7) | copy-start | bytes 580
  9.3 6.0 %collective-permute-start = (bf16[2,256,128]{2,1,0:T(8,128)(2,1)S(1)}, bf16[2,256,128]{2,1,0:T(8,128)(2,1)S(1)}, u32[]{:S(2)}, u32[]{:S(2)}) collective-permute-start(bf16[2,256,128]{2,1,0:T(8,128)(2,1)S(1)} %pad_maximum_fusion), channel_id=1, source_target_pairs={{0,16},{16,0},{1,17},{17,1},{2,18},{18,2},{3,19},{19,3},{4,20},{20... | collective-permute-start | bytes 393224 | tf_op jit(solution)/shard_map/ppermute | solution.py:217
  10.9 4.4 %collective-permute-start.1 = (s32[16,3]{0,1:T(4,128)S(1)}, s32[16,3]{0,1:T(4,128)S(1)}, u32[]{:S(2)}, u32[]{:S(2)}) collective-permute-start(s32[16,3]{0,1:T(4,128)S(1)} %bitcast.24), channel_id=1, source_target_pairs={{0,16},{16,0},{1,17},{17,1},{2,18},{18,2},{3,19},{19,3},{4,20},{20... | collective-permute-start | bytes 584 | tf_op jit(solution)/shard_map/ppermute | solution.py:217
  20.2 18.8 %all-to-all-start.1 = ((bf16[32,2,2,16,128]{4,3,2,1,0:T(8,128)(2,1)}), bf16[32,2,2,16,128]{4,3,2,1,0:T(8,128)(2,1)S(1)}, u32[]{:S(2)}, u32[]{:S(2)}) async-start(bf16[32,2,2,16,128]{4,3,2,1,0:T(8,128)(2,1)} %bitcast.8), calls=%async_computation.1 | async-start | bytes 1048576 | tf_op jit(solution)/shard_map/all_to_all | solution.py:261
  23.1 1.0 %copy-start = (bf16[512,512]{1,0:T(8,128)(2,1)S(1)}, bf16[512,512]{1,0:T(8,128)(2,1)}, u32[]{:S(2)}) copy-start(bf16[512,512]{1,0:T(8,128)(2,1)} %query_ref.3) | copy-start | bytes 1572868

commit v6 on v5

--- a/solution.py
+++ b/solution.py
@@ -1,4 +1,5 @@
 import functools
+import itertools
 import math
 
 import jax
@@ -158,50 +159,73 @@
 
 
 def far_kernel(
-    live_ref, query_ref, key_ref, far_ref, level_ref, mean_ref, out_ref, turned, valued, ready, sems
+    live_ref, query_ref, far_ref, level_ref, mean_ref, out_ref, turned, valued, ready, sems
 ):
-    spare = jnp.broadcast_to(key_ref[...], (BLK, HD))
-    none = jnp.zeros((BLK, HD), jnp.bfloat16)
-    for s in range(far_ref.shape[1]):
-        rows = slice(s * BLK, (s + 1) * BLK)
-        live = jnp.broadcast_to(live_ref[s], (BLK, HD)) > 0
-        turned[:HD, rows] = jnp.where(live, far_ref[:, s, 0].reshape(BLK, HD), spare).T
-        valued[rows, :HD] = jnp.where(live, far_ref[:, s, 1].reshape(BLK, HD), none)
-        valued[rows, HD:] = jnp.where(live, jnp.ones_like(none), none)
-    turned[HD:] = turned[:HD]
-    copies = []
-
-    def score(h, begin):
-        query_rows = split_queries(query_ref[begin : begin + CHUNK, h * HD : (h + 1) * HD])
-        return jnp.dot(query_rows, turned[...], preferred_element_type=jnp.float32)
-
-    def finish(h, begin, scores):
-        rows = slice(begin, begin + CHUNK)
-        level = level_ref[h, rows]
-        top = jnp.maximum(jnp.max(scores, axis=1, keepdims=True), level[:, :1])
-        weights = jnp.exp2(scores - top).astype(jnp.bfloat16)
-        product = jnp.dot(weights, valued[...], preferred_element_type=jnp.float32)
-        scale = jnp.exp2(level - top)
-        total = product[:, HD:] + scale
-        product = product[:, :HD] + mean_ref[h, rows] * scale
-        ready[h, rows] = (product / total).astype(ready.dtype)
-        if begin + CHUNK == BLK:
-            columns = slice(h * HD, (h + 1) * HD)
-            copies.append(pltpu.make_async_copy(ready.at[h], out_ref.at[:, columns], sems.at[h]))
-            copies[-1].start()
-
-    in_turn(units_of(query_ref.shape[1] // HD), score, finish)
-    for copy in copies:
-        copy.wait()
-
-
-def attend_far(live, queries, first_key, far, near):
+    heads_here = query_ref.shape[1] // HD
+    picks = far_ref.shape[1]
+
+    def leave(h):
+        columns = slice(h * HD, (h + 1) * HD)
+        return pltpu.make_async_copy(ready.at[h], out_ref.at[:, columns], sems.at[h])
+
+    def attend(slots):
+        keys_here = len(slots) * BLK
+        for place, s in enumerate(slots):
+            rows = slice(place * BLK, (place + 1) * BLK)
+            turned[:HD, rows] = far_ref[:, s, 0].reshape(BLK, HD).T
+            valued[rows, :HD] = far_ref[:, s, 1].reshape(BLK, HD)
+        turned[HD:, :keys_here] = turned[:HD, :keys_here]
+        valued[:keys_here, HD:] = jnp.ones((keys_here, HD), valued.dtype)
+
+        def score(h, begin):
+            query_rows = split_queries(query_ref[begin : begin + CHUNK, h * HD : (h + 1) * HD])
+            return jnp.dot(
+                query_rows, turned[:, :keys_here], preferred_element_type=jnp.float32
+            )
+
+        def finish(h, begin, scores):
+            rows = slice(begin, begin + CHUNK)
+            level = level_ref[h, rows]
+            top = jnp.maximum(jnp.max(scores, axis=1, keepdims=True), level[:, :1])
+            weights = jnp.exp2(scores - top).astype(jnp.bfloat16)
+            product = jnp.dot(weights, valued[:keys_here], preferred_element_type=jnp.float32)
+            scale = jnp.exp2(level - top)
+            total = product[:, HD:] + scale
+            product = product[:, :HD] + mean_ref[h, rows] * scale
+            ready[h, rows] = (product / total).astype(ready.dtype)
+            if begin + CHUNK == BLK:
+                leave(h).start()
+
+        in_turn(units_of(heads_here), score, finish)
+
+    flags = live_ref[...]
+    live = [flags[0, s] > 0 for s in range(picks)]
+    for which in itertools.product((False, True), repeat=picks):
+        slots = [s for s in range(picks) if which[s]]
+        met = functools.reduce(
+            jnp.logical_and, [flag if on else ~flag for flag, on in zip(live, which)]
+        )
+
+        @pl.when(met)
+        def _():
+            if slots:
+                attend(slots)
+            else:
+                for h in range(heads_here):
+                    ready[h] = mean_ref[h].astype(ready.dtype)
+                    leave(h).start()
+
+    for h in range(heads_here):
+        leave(h).wait()
+
+
+def attend_far(live, queries, far, near):
     rows, columns = queries.shape
     keys_here = far.shape[1] * BLK
     return pl.pallas_call(
         far_kernel,
         out_shape=jax.ShapeDtypeStruct(queries.shape, queries.dtype),
-        in_specs=[VMEM] * 6,
+        in_specs=[VMEM] * 5,
         out_specs=ANY,
         scratch_shapes=[
             pltpu.VMEM((2 * HD, keys_here), jnp.bfloat16),
@@ -210,7 +234,7 @@
             pltpu.SemaphoreType.DMA((columns // HD,)),
         ],
         compiler_params=LARGE,
-    )(*in_vmem(live, queries, first_key, far, *near))
+    )(*in_vmem(live, queries, far, *near))
 
 
 def other_head(x):
@@ -265,9 +289,8 @@
     near = attend_near(queries, own[0], own[1])
 
     chosen = lax.dynamic_index_in_dim(lists, ctx_rank, 0, keepdims=False)[1:]
-    live = (chosen != ctx_rank).astype(jnp.float32)
-    live = jnp.broadcast_to(live[:, None, None], (picks, 1, HD))
-    return attend_far(live, queries, own[0, :1], far, near)
+    live = (chosen != ctx_rank).astype(jnp.int32)[None]
+    return attend_far(live, queries, far, near)
 
 
 def solution(mesh):

time: 43.2 us -> 42.6 us (0.986)
  the two profiles are of different devices: /device:TPU:0 before, /device:TPU:1 now
where the time goes in v6:
time: 42.6 us; the launch traced here: 42.2 us
  waiting for transfers between devices  19.4 us (46%)
  starting transfers between devices  12.7 us (30%)
  Pallas kernels  8.73 us (20%)
  local copies, waits for them, and re-layouts  1.07 us (3%)
    all_to_all x1, waiting for transfers between devices, on_device(): lax.all_to_all(far, ('head', 'ctx'), split_axis=0, concat_axis=0, tiled=T...  12.1 us
    all_to_all x1, starting transfers between devices, on_device(): lax.all_to_all(pieces, 'ctx', split_axis=0, concat_axis=0, tiled=True)  7.49 us
    all_to_all x1, waiting for transfers between devices, on_device(): lax.all_to_all(pieces, 'ctx', split_axis=0, concat_axis=0, tiled=True)  4.02 us
    pallas_call x1, Pallas kernels, attend_far(): pl.pallas_call(far_kernel, out_shape=jax.ShapeDtypeStruct(queries.shape,...  4.01 us
    all_to_all x1, starting transfers between devices, on_device(): lax.all_to_all(far, ('head', 'ctx'), split_axis=0, concat_axis=0, tiled=T...  3.28 us
    ppermute x2, waiting for transfers between devices, other_head(): return lax.ppermute(x, 'head', [(0, 1), (1, 0)])  3.21 us
    pallas_call x1, Pallas kernels, attend_near(): pl.pallas_call(near_kernel, out_shape=[pltpu.VMEM((columns // HD, rows, H...  2.1 us
    ppermute x2, starting transfers between devices, other_head(): return lax.ppermute(x, 'head', [(0, 1), (1, 0)])  1.89 us
  transfers between devices with their start and end apart: 4, of which 3 were waited for; matrix products, arithmetic and copies ran while one was open for 1% of the time, Pallas kernels for 5%

profile of v6, /device:TPU:1, one launch (start us, length us, event | category | flops | bytes accessed | tf_op | source)
XLA Modules:
  0.0 42.2 jit_solution(8442190855395499275)
XLA Ops:
  0.0 1.6 %shard_map.46 = bf16[16,2,16,256]{3,2,1,0:T(8,128)(2,1)} custom-call(bf16[16,16,256]{2,1,0:T(8,128)(2,1)} %bitcast.21, bf16[16,16,256]{2,1,0:T(8,128)(2,1)} %bitcast.22), custom_call_target="tpu_custom_call" | custom-call | tf_op jit(solution)/shard_map/pallas_call | solution.py:57
  1.6 0.0 copy-start.1
  1.6 0.0 copy-start.2
  1.7 7.5 %all-to-all-start = ((bf16[16,2,16,256]{3,2,1,0:T(8,128)(2,1)}), bf16[16,2,16,256]{3,2,1,0:T(8,128)(2,1)S(1)}, u32[]{:S(2)}, u32[]{:S(2)}) async-start(bf16[16,2,16,256]{3,2,1,0:T(8,128)(2,1)} %shard_map.46), calls=%async_computation | async-start | bytes 524288 | tf_op jit(solution)/shard_map/all_to_all | solution.py:277
  9.2 0.0 copy-done.1
  9.2 0.0 copy-done.2
  9.2 0.1 dynamic-slice_bitcast_fusion.2
  9.2 0.0 copy-start.3
  9.3 1.3 %collective-permute-start = (bf16[2,256,128]{2,1,0:T(8,128)(2,1)S(1)}, bf16[2,256,128]{2,1,0:T(8,128)(2,1)S(1)}, u32[]{:S(2)}, u32[]{:S(2)}) collective-permute-start(bf16[2,256,128]{2,1,0:T(8,128)(2,1)S(1)} %pad_maximum_fusion), channel_id=1, source_target_pairs={{0,16},{16,0},{1,17},{17,1},{2,18},{18,2},{3,19},{19,3},{4,20},{20... | collective-permute-start | bytes 393224 | tf_op jit(solution)/shard_map/ppermute | solution.py:241
  10.6 0.6 %collective-permute-start.1 = (s32[16,3]{0,1:T(4,128)S(1)}, s32[16,3]{0,1:T(4,128)S(1)}, u32[]{:S(2)}, u32[]{:S(2)}) collective-permute-start(s32[16,3]{0,1:T(4,128)S(1)} %bitcast.24), channel_id=1, source_target_pairs={{0,16},{16,0},{1,17},{17,1},{2,18},{18,2},{3,19},{19,3},{4,20},{20... | collective-permute-start | bytes 584 | tf_op jit(solution)/shard_map/ppermute | solution.py:241
  11.2 0.1 copy.17
  11.2 3.2 %collective-permute-done.1 = s32[16,3]{0,1:T(4,128)S(1)} collective-permute-done((s32[16,3]{0,1:T(4,128)S(1)}, s32[16,3]{0,1:T(4,128)S(1)}, u32[]{:S(2)}, u32[]{:S(2)}) %collective-permute-start.1) | collective-permute-done | bytes 224 | tf_op jit(solution)/shard_map/ppermute | solution.py:241
  14.4 0.1 copy.18
  14.5 0.0 collective-permute-done
  14.5 0.1 maximum_select_fusion
  14.6 4.0 %all-to-all-done.pieces_ref = bf16[16,2,16,256]{3,2,1,0:T(8,128)(2,1)S(1)} async-done(((bf16[16,2,16,256]{3,2,1,0:T(8,128)(2,1)}), bf16[16,2,16,256]{3,2,1,0:T(8,128)(2,1)S(1)}, u32[]{:S(2)}, u32[]{:S(2)}) %all-to-all-start) | async-done | bytes 262176 | tf_op jit(solution)/shard_map/all_to_all | solution.py:277
  18.6 1.0 %shard_map.47 = bf16[2,16,2,2,16,128]{5,4,3,2,1,0:T(8,128)(2,1)} custom-call(s32[2,16,3]{2,1,0:T(8,128)S(1)} %add_select_fusion.lists_ref, bf16[16,2,16,256]{3,2,1,0:T(8,128)(2,1)S(1)} %all-to-all-done.pieces_ref), custom_call_target="tpu_custom_call" | custom-call | tf_op jit(solution)/shard_map/pallas_call | solution.py:86
  19.6 3.3 %all-to-all-start.1 = ((bf16[32,2,2,16,128]{4,3,2,1,0:T(8,128)(2,1)}), bf16[32,2,2,16,128]{4,3,2,1,0:T(8,128)(2,1)S(1)}, u32[]{:S(2)}, u32[]{:S(2)}) async-start(bf16[32,2,2,16,128]{4,3,2,1,0:T(8,128)(2,1)} %bitcast.7), calls=%async_computation.1 | async-start | bytes 1048576 | tf_op jit(solution)/shard_map/all_to_all | solution.py:285
  22.9 0.0 copy-start
  22.9 0.2 fusion
  23.2 0.8 %copy-done = bf16[512,512]{1,0:T(8,128)(2,1)S(1)} copy-done((bf16[512,512]{1,0:T(8,128)(2,1)S(1)}, bf16[512,512]{1,0:T(8,128)(2,1)}, u32[]{:S(2)}) %copy-start) | copy-done | bytes 524312
  24.0 2.1 %shard_map.48 = (f32[4,512,128]{2,1,0:T(8,128)S(1)}, f32[4,512,128]{2,1,0:T(8,128)S(1)}) custom-call(bf16[512,512]{1,0:T(8,128)(2,1)S(1)} %copy-done, bf16[512,128]{1,0:T(8,128)(2,1)S(1)} %get-tuple-element.16.key_ref, bf16[512,128]{1,0:T(8,128)(2,1)S(1)} %get-tuple-element.15.value_ref), custom_call_target="tpu_custom_call" | custom-call | flops 536870912 | bytes 4194304 | tf_op jit(solution)/shard_map/pallas_call | solution.py:145
  26.1 12.1 %all-to-all-done.1.far_ref = bf16[32,2,2,16,128]{4,3,2,1,0:T(8,128)(2,1)S(1)} async-done(((bf16[32,2,2,16,128]{4,3,2,1,0:T(8,128)(2,1)}), bf16[32,2,2,16,128]{4,3,2,1,0:T(8,128)(2,1)S(1)}, u32[]{:S(2)}, u32[]{:S(2)}) %all-to-all-start.1) | async-done | bytes 524320 | tf_op jit(solution)/shard_map/all_to_all | solution.py:285
  38.2 4.0 %shard_map.49 = bf16[512,512]{1,0:T(8,128)(2,1)} custom-call(s32[1,2]{1,0:T(1,128)S(1)} %bitcast.20, bf16[512,512]{1,0:T(8,128)(2,1)S(1)} %copy-done, bf16[32,2,2,16,128]{4,3,2,1,0:T(8,128)(2,1)S(1)} %all-to-all-done.1.far_ref, f32[4,512,128]{2,1,0:T(8,128)S(1)} %get-tuple-element.13.level_ref, f32[4,512,128]{2,1,0:T(8,128)S(1)} %get-tuple-element.14.mean_ref), custom_call_target="tpu_custom_call" | custom-call | tf_op jit(solution)/shard_map/pallas_call | solution.py:225
  (5 shorter events, 0.1 us)
Async XLA Ops:
  1.6 7.5 %copy-start.1 = (bf16[256,256]{1,0:T(8,128)(2,1)S(1)}, bf16[256,256]{1,0:T(8,128)(2,1)}, u32[]{:S(2)}) copy-start(bf16[256,256]{1,0:T(8,128)(2,1)} %param.5) | copy-start | bytes 393220
  1.6 7.5 %copy-start.2 = (bf16[256,256]{1,0:T(8,128)(2,1)S(1)}, bf16[256,256]{1,0:T(8,128)(2,1)}, u32[]{:S(2)}) copy-start(bf16[256,256]{1,0:T(8,128)(2,1)} %param.6) | copy-start | bytes 393220
  1.7 17.0 %all-to-all-start = ((bf16[16,2,16,256]{3,2,1,0:T(8,128)(2,1)}), bf16[16,2,16,256]{3,2,1,0:T(8,128)(2,1)S(1)}, u32[]{:S(2)}, u32[]{:S(2)}) async-start(bf16[16,2,16,256]{3,2,1,0:T(8,128)(2,1)} %shard_map.46), calls=%async_computation | async-start | bytes 524288 | tf_op jit(solution)/shard_map/all_to_all | solution.py:277
  9.2 1.3 %copy-start.3 = (s32[1,16,3]{1,0,2:T(1,128)S(1)}, s32[1,16,3]{1,0,2:T(1,128)}, u32[]{:S(2)}) copy-start(s32[1,16,3]{1,0,2:T(1,128)} %param.7) | copy-start | bytes 580
  9.3 5.3 %collective-permute-start = (bf16[2,256,128]{2,1,0:T(8,128)(2,1)S(1)}, bf16[2,256,128]{2,1,0:T(8,128)(2,1)S(1)}, u32[]{:S(2)}, u32[]{:S(2)}) collective-permute-start(bf16[2,256,128]{2,1,0:T(8,128)(2,1)S(1)} %pad_maximum_fusion), channel_id=1, source_target_pairs={{0,16},{16,0},{1,17},{17,1},{2,18},{18,2},{3,19},{19,3},{4,20},{20... | collective-permute-start | bytes 393224 | tf_op jit(solution)/shard_map/ppermute | solution.py:241
  10.6 3.9 %collective-permute-start.1 = (s32[16,3]{0,1:T(4,128)S(1)}, s32[16,3]{0,1:T(4,128)S(1)}, u32[]{:S(2)}, u32[]{:S(2)}) collective-permute-start(s32[16,3]{0,1:T(4,128)S(1)} %bitcast.24), channel_id=1, source_target_pairs={{0,16},{16,0},{1,17},{17,1},{2,18},{18,2},{3,19},{19,3},{4,20},{20... | collective-permute-start | bytes 584 | tf_op jit(solution)/shard_map/ppermute | solution.py:241
  19.6 18.6 %all-to-all-start.1 = ((bf16[32,2,2,16,128]{4,3,2,1,0:T(8,128)(2,1)}), bf16[32,2,2,16,128]{4,3,2,1,0:T(8,128)(2,1)S(1)}, u32[]{:S(2)}, u32[]{:S(2)}) async-start(bf16[32,2,2,16,128]{4,3,2,1,0:T(8,128)(2,1)} %bitcast.7), calls=%async_computation.1 | async-start | bytes 1048576 | tf_op jit(solution)/shard_map/all_to_all | solution.py:285
  22.9 1.0 %copy-start = (bf16[512,512]{1,0:T(8,128)(2,1)S(1)}, bf16[512,512]{1,0:T(8,128)(2,1)}, u32[]{:S(2)}) copy-start(bf16[512,512]{1,0:T(8,128)(2,1)} %query_ref.3) | copy-start | bytes 1572868

commit v7 on v6

--- a/solution.py
+++ b/solution.py
@@ -92,8 +92,8 @@
     )(*in_vmem(lists, pieces))
 
 
-def units_of(heads_here):
-    return [(h, begin) for h in range(heads_here) for begin in range(0, BLK, CHUNK)]
+def units_of(heads_here, size):
+    return [(h, begin, begin + size) for h in range(heads_here) for begin in range(0, BLK, size)]
 
 
 def in_turn(units, score, finish):
@@ -119,25 +119,22 @@
     valued[:, :HD] = value_ref[...]
     valued[:, HD:] = jnp.ones(value_ref.shape, valued.dtype)
 
-    def score(h, begin):
-        end = begin + CHUNK
+    def score(h, begin, end):
         query_rows = split_queries(query_ref[begin:end, h * HD : (h + 1) * HD])
         scores = jnp.dot(query_rows, turned[:, :end], preferred_element_type=jnp.float32)
         row_ids = lax.broadcasted_iota(jnp.int32, scores.shape, 0) + begin
         col_ids = lax.broadcasted_iota(jnp.int32, scores.shape, 1)
         return jnp.where(row_ids >= col_ids, scores, -jnp.inf)
 
-    def finish(h, begin, scores):
-        rows = slice(begin, begin + CHUNK)
+    def finish(h, begin, end, scores):
+        rows = slice(begin, end)
         top = jnp.max(scores, axis=1, keepdims=True)
         weights = jnp.exp2(scores - top).astype(jnp.bfloat16)
-        product = jnp.dot(
-            weights, valued[: begin + CHUNK], preferred_element_type=jnp.float32
-        )
+        product = jnp.dot(weights, valued[:end], preferred_element_type=jnp.float32)
         level_ref[h, rows] = top + jnp.log2(product[:, HD:])
         mean_ref[h, rows] = product[:, :HD] / product[:, HD:]
 
-    in_turn(units_of(query_ref.shape[1] // HD), score, finish)
+    in_turn(units_of(query_ref.shape[1] // HD, CHUNK), score, finish)
 
 
 def attend_near(queries, own_keys, own_values):
@@ -177,14 +174,14 @@
         turned[HD:, :keys_here] = turned[:HD, :keys_here]
         valued[:keys_here, HD:] = jnp.ones((keys_here, HD), valued.dtype)
 
-        def score(h, begin):
-            query_rows = split_queries(query_ref[begin : begin + CHUNK, h * HD : (h + 1) * HD])
+        def score(h, begin, end):
+            query_rows = split_queries(query_ref[begin:end, h * HD : (h + 1) * HD])
             return jnp.dot(
                 query_rows, turned[:, :keys_here], preferred_element_type=jnp.float32
             )
 
-        def finish(h, begin, scores):
-            rows = slice(begin, begin + CHUNK)
+        def finish(h, begin, end, scores):
+            rows = slice(begin, end)
             level = level_ref[h, rows]
             top = jnp.maximum(jnp.max(scores, axis=1, keepdims=True), level[:, :1])
             weights = jnp.exp2(scores - top).astype(jnp.bfloat16)
@@ -193,10 +190,11 @@
             total = product[:, HD:] + scale
             product = product[:, :HD] + mean_ref[h, rows] * scale
             ready[h, rows] = (product / total).astype(ready.dtype)
-            if begin + CHUNK == BLK:
+            if end == BLK:
                 leave(h).start()
 
-        in_turn(units_of(heads_here), score, finish)
+        size = CHUNK if len(slots) == picks else 2 * CHUNK
+        in_turn(units_of(heads_here, size), score, finish)
 
     flags = live_ref[...]
     live = [flags[0, s] > 0 for s in range(picks)]
@@ -274,10 +272,13 @@
     share = keys.shape[0] // ranks
 
     pieces = pack_rows(keys, values, ranks)
-    pieces = lax.all_to_all(pieces, "ctx", split_axis=0, concat_axis=0, tiled=True)
+    backwards = [list(range(ranks))[::-1]]
+    pieces = lax.all_to_all(
+        pieces, "ctx", split_axis=0, concat_axis=0, axis_index_groups=backwards, tiled=True
+    )
 
     own = own_block(keys, values, heads, head_rank)
-    every_list = lists_of_heads(lists, heads, head_rank)
+    every_list = ranks - 1 - lists_of_heads(lists, heads, head_rank)
     pieces, own, every_list = lax.optimization_barrier((pieces, own, every_list))
 
     far = pick_pieces(every_list, pieces)

time: 42.6 us -> 41.8 us (0.981)
  the two profiles are of different devices: /device:TPU:1 before, /device:TPU:4 now
where the time goes in v7:
time: 41.8 us; the launch traced here: 41.4 us
  waiting for transfers between devices  17.2 us (41%)
  starting transfers between devices  14.1 us (34%)
  Pallas kernels  8.65 us (21%)
  local copies, waits for them, and re-layouts  1.07 us (3%)
    all_to_all x1, waiting for transfers between devices, on_device(): lax.all_to_all(far, ('head', 'ctx'), split_axis=0, concat_axis=0, tiled=T...  12.5 us
    all_to_all x1, starting transfers between devices, on_device(): lax.all_to_all(pieces, 'ctx', split_axis=0, concat_axis=0, axis_index_gro...  6.61 us
    all_to_all x1, starting transfers between devices, on_device(): lax.all_to_all(far, ('head', 'ctx'), split_axis=0, concat_axis=0, tiled=T...  5.36 us
    pallas_call x1, Pallas kernels, attend_far(): pl.pallas_call(far_kernel, out_shape=jax.ShapeDtypeStruct(queries.shape,...  3.93 us
    ppermute x2, waiting for transfers between devices, other_head(): return lax.ppermute(x, 'head', [(0, 1), (1, 0)])  3.37 us
    ppermute x2, starting transfers between devices, other_head(): return lax.ppermute(x, 'head', [(0, 1), (1, 0)])  2.14 us
    pallas_call x1, Pallas kernels, attend_near(): pl.pallas_call(near_kernel, out_shape=[pltpu.VMEM((columns // HD, rows, H...  2.1 us
    pallas_call x1, Pallas kernels, pack_rows(): pl.pallas_call(pack_kernel, out_shape=jax.ShapeDtypeStruct(shape, keys.dt...  1.62 us
  transfers between devices with their start and end apart: 4, of which 3 were waited for; matrix products, arithmetic and copies ran while one was open for 1% of the time, Pallas kernels for 5%

profile of v7, /device:TPU:4, one launch (start us, length us, event | category | flops | bytes accessed | tf_op | source)
XLA Modules:
  0.0 41.4 jit_solution(15108855829976745606)
XLA Ops:
  0.0 1.6 %shard_map.46 = bf16[16,2,16,256]{3,2,1,0:T(8,128)(2,1)} custom-call(bf16[16,16,256]{2,1,0:T(8,128)(2,1)} %bitcast.21, bf16[16,16,256]{2,1,0:T(8,128)(2,1)} %bitcast.22), custom_call_target="tpu_custom_call" | custom-call | tf_op jit(solution)/shard_map/pallas_call | solution.py:57
  1.6 0.0 copy-start.1
  1.6 0.0 copy-start.2
  1.7 6.6 %all-to-all-start = ((bf16[16,2,16,256]{3,2,1,0:T(8,128)(2,1)}), bf16[16,2,16,256]{3,2,1,0:T(8,128)(2,1)S(1)}, u32[]{:S(2)}, u32[]{:S(2)}) async-start(bf16[16,2,16,256]{3,2,1,0:T(8,128)(2,1)} %shard_map.46), calls=%async_computation | async-start | bytes 524288 | tf_op jit(solution)/shard_map/all_to_all | solution.py:276
  8.3 0.0 copy-done.1
  8.3 0.0 copy-done.2
  8.3 0.1 dynamic-slice_bitcast_fusion.2
  8.3 0.0 copy-start.3
  8.4 1.6 %collective-permute-start = (bf16[2,256,128]{2,1,0:T(8,128)(2,1)S(1)}, bf16[2,256,128]{2,1,0:T(8,128)(2,1)S(1)}, u32[]{:S(2)}, u32[]{:S(2)}) collective-permute-start(bf16[2,256,128]{2,1,0:T(8,128)(2,1)S(1)} %pad_maximum_fusion), channel_id=1, source_target_pairs={{0,16},{16,0},{1,17},{17,1},{2,18},{18,2},{3,19},{19,3},{4,20},{20... | collective-permute-start | bytes 393224 | tf_op jit(solution)/shard_map/ppermute | solution.py:239
  9.9 0.6 %collective-permute-start.1 = (s32[16,3]{0,1:T(4,128)S(1)}, s32[16,3]{0,1:T(4,128)S(1)}, u32[]{:S(2)}, u32[]{:S(2)}) collective-permute-start(s32[16,3]{0,1:T(4,128)S(1)} %bitcast.24), channel_id=1, source_target_pairs={{0,16},{16,0},{1,17},{17,1},{2,18},{18,2},{3,19},{19,3},{4,20},{20... | collective-permute-start | bytes 584 | tf_op jit(solution)/shard_map/ppermute | solution.py:239
  10.5 0.1 copy.17
  10.6 3.4 %collective-permute-done.1 = s32[16,3]{0,1:T(4,128)S(1)} collective-permute-done((s32[16,3]{0,1:T(4,128)S(1)}, s32[16,3]{0,1:T(4,128)S(1)}, u32[]{:S(2)}, u32[]{:S(2)}) %collective-permute-start.1) | collective-permute-done | bytes 224 | tf_op jit(solution)/shard_map/ppermute | solution.py:239
  14.0 0.1 copy.18
  14.1 0.0 collective-permute-done
  14.1 0.1 maximum_select_fusion
  14.2 1.3 %all-to-all-done.pieces_ref = bf16[16,2,16,256]{3,2,1,0:T(8,128)(2,1)S(1)} async-done(((bf16[16,2,16,256]{3,2,1,0:T(8,128)(2,1)}), bf16[16,2,16,256]{3,2,1,0:T(8,128)(2,1)S(1)}, u32[]{:S(2)}, u32[]{:S(2)}) %all-to-all-start) | async-done | bytes 262176 | tf_op jit(solution)/shard_map/all_to_all | solution.py:276
  15.5 1.0 %shard_map.47 = bf16[2,16,2,2,16,128]{5,4,3,2,1,0:T(8,128)(2,1)} custom-call(s32[2,16,3]{2,1,0:T(8,128)S(1)} %fusion.lists_ref, bf16[16,2,16,256]{3,2,1,0:T(8,128)(2,1)S(1)} %all-to-all-done.pieces_ref), custom_call_target="tpu_custom_call" | custom-call | tf_op jit(solution)/shard_map/pallas_call | solution.py:86
  16.5 5.4 %all-to-all-start.1 = ((bf16[32,2,2,16,128]{4,3,2,1,0:T(8,128)(2,1)}), bf16[32,2,2,16,128]{4,3,2,1,0:T(8,128)(2,1)S(1)}, u32[]{:S(2)}, u32[]{:S(2)}) async-start(bf16[32,2,2,16,128]{4,3,2,1,0:T(8,128)(2,1)} %bitcast.7), calls=%async_computation.1 | async-start | bytes 1048576 | tf_op jit(solution)/shard_map/all_to_all | solution.py:286
  21.9 0.0 copy-start
  21.9 0.2 fusion.1
  22.1 0.8 %copy-done = bf16[512,512]{1,0:T(8,128)(2,1)S(1)} copy-done((bf16[512,512]{1,0:T(8,128)(2,1)S(1)}, bf16[512,512]{1,0:T(8,128)(2,1)}, u32[]{:S(2)}) %copy-start) | copy-done | bytes 524312
  22.9 2.1 %shard_map.48 = (f32[4,512,128]{2,1,0:T(8,128)S(1)}, f32[4,512,128]{2,1,0:T(8,128)S(1)}) custom-call(bf16[512,512]{1,0:T(8,128)(2,1)S(1)} %copy-done, bf16[512,128]{1,0:T(8,128)(2,1)S(1)} %get-tuple-element.16.key_ref, bf16[512,128]{1,0:T(8,128)(2,1)S(1)} %get-tuple-element.15.value_ref), custom_call_target="tpu_custom_call" | custom-call | flops 536870912 | bytes 4194304 | tf_op jit(solution)/shard_map/pallas_call | solution.py:142
  25.0 12.5 %all-to-all-done.1.far_ref = bf16[32,2,2,16,128]{4,3,2,1,0:T(8,128)(2,1)S(1)} async-done(((bf16[32,2,2,16,128]{4,3,2,1,0:T(8,128)(2,1)}), bf16[32,2,2,16,128]{4,3,2,1,0:T(8,128)(2,1)S(1)}, u32[]{:S(2)}, u32[]{:S(2)}) %all-to-all-start.1) | async-done | bytes 524320 | tf_op jit(solution)/shard_map/all_to_all | solution.py:286
  37.5 3.9 %shard_map.49 = bf16[512,512]{1,0:T(8,128)(2,1)} custom-call(s32[1,2]{1,0:T(1,128)S(1)} %bitcast.20, bf16[512,512]{1,0:T(8,128)(2,1)S(1)} %copy-done, bf16[32,2,2,16,128]{4,3,2,1,0:T(8,128)(2,1)S(1)} %all-to-all-done.1.far_ref, f32[4,512,128]{2,1,0:T(8,128)S(1)} %get-tuple-element.13.level_ref, f32[4,512,128]{2,1,0:T(8,128)S(1)} %get-tuple-element.14.mean_ref), custom_call_target="tpu_custom_call" | custom-call | tf_op jit(solution)/shard_map/pallas_call | solution.py:223
  (5 shorter events, 0.1 us)
Async XLA Ops:
  1.6 6.6 %copy-start.1 = (bf16[256,256]{1,0:T(8,128)(2,1)S(1)}, bf16[256,256]{1,0:T(8,128)(2,1)}, u32[]{:S(2)}) copy-start(bf16[256,256]{1,0:T(8,128)(2,1)} %param.5) | copy-start | bytes 393220
  1.6 6.6 %copy-start.2 = (bf16[256,256]{1,0:T(8,128)(2,1)S(1)}, bf16[256,256]{1,0:T(8,128)(2,1)}, u32[]{:S(2)}) copy-start(bf16[256,256]{1,0:T(8,128)(2,1)} %param.6) | copy-start | bytes 393220
  1.7 13.8 %all-to-all-start = ((bf16[16,2,16,256]{3,2,1,0:T(8,128)(2,1)}), bf16[16,2,16,256]{3,2,1,0:T(8,128)(2,1)S(1)}, u32[]{:S(2)}, u32[]{:S(2)}) async-start(bf16[16,2,16,256]{3,2,1,0:T(8,128)(2,1)} %shard_map.46), calls=%async_computation | async-start | bytes 524288 | tf_op jit(solution)/shard_map/all_to_all | solution.py:276
  8.3 1.6 %copy-start.3 = (s32[1,16,3]{1,0,2:T(1,128)S(1)}, s32[1,16,3]{1,0,2:T(1,128)}, u32[]{:S(2)}) copy-start(s32[1,16,3]{1,0,2:T(1,128)} %param.7) | copy-start | bytes 580
  8.4 5.7 %collective-permute-start = (bf16[2,256,128]{2,1,0:T(8,128)(2,1)S(1)}, bf16[2,256,128]{2,1,0:T(8,128)(2,1)S(1)}, u32[]{:S(2)}, u32[]{:S(2)}) collective-permute-start(bf16[2,256,128]{2,1,0:T(8,128)(2,1)S(1)} %pad_maximum_fusion), channel_id=1, source_target_pairs={{0,16},{16,0},{1,17},{17,1},{2,18},{18,2},{3,19},{19,3},{4,20},{20... | collective-permute-start | bytes 393224 | tf_op jit(solution)/shard_map/ppermute | solution.py:239
  9.9 4.0 %collective-permute-start.1 = (s32[16,3]{0,1:T(4,128)S(1)}, s32[16,3]{0,1:T(4,128)S(1)}, u32[]{:S(2)}, u32[]{:S(2)}) collective-permute-start(s32[16,3]{0,1:T(4,128)S(1)} %bitcast.24), channel_id=1, source_target_pairs={{0,16},{16,0},{1,17},{17,1},{2,18},{18,2},{3,19},{19,3},{4,20},{20... | collective-permute-start | bytes 584 | tf_op jit(solution)/shard_map/ppermute | solution.py:239
  16.5 21.0 %all-to-all-start.1 = ((bf16[32,2,2,16,128]{4,3,2,1,0:T(8,128)(2,1)}), bf16[32,2,2,16,128]{4,3,2,1,0:T(8,128)(2,1)S(1)}, u32[]{:S(2)}, u32[]{:S(2)}) async-start(bf16[32,2,2,16,128]{4,3,2,1,0:T(8,128)(2,1)} %bitcast.7), calls=%async_computation.1 | async-start | bytes 1048576 | tf_op jit(solution)/shard_map/all_to_all | solution.py:286
  21.9 1.0 %copy-start = (bf16[512,512]{1,0:T(8,128)(2,1)S(1)}, bf16[512,512]{1,0:T(8,128)(2,1)}, u32[]{:S(2)}) copy-start(bf16[512,512]{1,0:T(8,128)(2,1)} %query_ref.3) | copy-start | bytes 1572868

commit v8 on v7

v8 whole, which is shorter than its diff:
```python
import functools
import itertools
import math

import jax
import jax.numpy as jnp
from jax import lax
from jax.experimental import pallas as pl
from jax.experimental.pallas import tpu as pltpu
from jax.sharding import PartitionSpec as P

HD = 128
BLK = 512
CHUNK = 128
AHEAD = 2
FACTOR = math.log2(math.e) / math.sqrt(HD)
SMALL = pltpu.CompilerParams(vmem_limit_bytes=2 * 1024 * 1024)
LARGE = pltpu.CompilerParams(vmem_limit_bytes=12 * 1024 * 1024)
VMEM = pl.BlockSpec(memory_space=pltpu.VMEM)
ANY = pl.BlockSpec(memory_space=pl.ANY)


def in_vmem(*arrays):
    return [pltpu.with_memory_space_constraint(x, pltpu.VMEM) for x in arrays]


def pack_kernel(key_ref, value_ref, slots_ref, out_ref, slots_out, sems, slots_sem):
    heads = out_ref.shape[0]
    copies = [
        pltpu.make_async_copy(
            ref.at[:, :, h * HD : (h + 1) * HD], out_ref.at[h, :, kv], sems.at[kv, h]
        )
        for kv, ref in enumerate((key_ref, value_ref))
        for h in range(heads)
    ]
    copies.append(pltpu.make_async_copy(slots_ref, slots_out, slots_sem))
    for copy in copies:
        copy.start()
    for copy in copies:
        copy.wait()


def pack(keys, values, slots, heads, ranks):
    rows, columns = keys.shape
    share = rows // ranks
    if share % 16:
        both = jnp.stack([keys, values]).reshape(2, ranks, share, heads, HD)
        return both.transpose(3, 1, 0, 2, 4), slots
    operands = [keys.reshape(ranks, share, columns), values.reshape(ranks, share, columns), slots]
    return pl.pallas_call(
        pack_kernel,
        out_shape=[
            pltpu.VMEM((heads, ranks, 2, share, HD), keys.dtype),
            pltpu.VMEM(slots.shape, slots.dtype),
        ],
        in_specs=[ANY] * 3,
        out_specs=[VMEM] * 2,
        scratch_shapes=[pltpu.SemaphoreType.DMA((2, heads)), pltpu.SemaphoreType.DMA],
        compiler_params=SMALL,
    )(*[pltpu.with_memory_space_constraint(x, pltpu.HBM) for x in operands])


def pick_kernel(order, slots_ref, pieces_ref, out_ref):
    _, picks, parts = out_ref.shape[:3]
    slots = slots_ref[...]
    for place, receiver in enumerate(order):
        for s in range(picks):
            block = slots[s + 1, 0, receiver]
            for part in range(parts):
                out_ref[place, s, part] = pieces_ref[part, block]


def pick_pieces(slots, pieces, order):
    heads, ranks, _, share, _ = pieces.shape
    if share % 16:
        return pieces.swapaxes(0, 1)[slots[1:, 0].T[jnp.array(order)]]
    return pl.pallas_call(
        functools.partial(pick_kernel, order),
        out_shape=pltpu.VMEM((ranks, slots.shape[0] - 1, heads, 2, share, HD), pieces.dtype),
        in_specs=[VMEM, VMEM],
        out_specs=VMEM,
        compiler_params=SMALL,
    )(*in_vmem(slots, pieces))


def units_of(heads_here, size):
    return [(h, begin, begin + size) for h in range(heads_here) for begin in range(0, BLK, size)]


def in_turn(units, score, finish):
    held = [score(*unit) for unit in units[: AHEAD - 1]]
    for i, unit in enumerate(units):
        if i + AHEAD - 1 < len(units):
            held.append(score(*units[i + AHEAD - 1]))
        finish(*unit, held.pop(0))


def split_queries(query_rows):
    scaled = query_rows.astype(jnp.float32) * FACTOR
    high = scaled.astype(jnp.bfloat16)
    low = (scaled - high.astype(jnp.float32)).astype(jnp.bfloat16)
    return jnp.concatenate([high, low], axis=1)


def near_kernel(
    query_ref, key_ref, value_ref, level_ref, mean_ref, turned, valued
):
    turned[:HD] = key_ref[...].T
    turned[HD:] = turned[:HD]
    valued[:, :HD] = value_ref[...]
    valued[:, HD:] = jnp.ones(value_ref.shape, valued.dtype)

    def score(h, begin, end):
        query_rows = split_queries(query_ref[begin:end, h * HD : (h + 1) * HD])
        scores = jnp.dot(query_rows, turned[:, :end], preferred_element_type=jnp.float32)
        row_ids = lax.broadcasted_iota(jnp.int32, scores.shape, 0) + begin
        col_ids = lax.broadcasted_iota(jnp.int32, scores.shape, 1)
        return jnp.where(row_ids >= col_ids, scores, -jnp.inf)

    def finish(h, begin, end, scores):
        rows = slice(begin, end)
        top = jnp.max(scores, axis=1, keepdims=True)
        weights = jnp.exp2(scores - top).astype(jnp.bfloat16)
        product = jnp.dot(weights, valued[:end], preferred_element_type=jnp.float32)
        level_ref[h, rows] = top + jnp.log2(product[:, HD:])
        mean_ref[h, rows] = product[:, :HD] / product[:, HD:]

    in_turn(units_of(query_ref.shape[1] // HD, CHUNK), score, finish)


def attend_near(queries, own_keys, own_values):
    rows, columns = queries.shape
    return pl.pallas_call(
        near_kernel,
        out_shape=[pltpu.VMEM((columns // HD, rows, HD), jnp.float32)] * 2,
        in_specs=[VMEM] * 3,
        out_specs=[VMEM] * 2,
        scratch_shapes=[
            pltpu.VMEM((2 * HD, BLK), jnp.bfloat16),
            pltpu.VMEM((BLK, 2 * HD), jnp.bfloat16),
        ],
        compiler_params=LARGE,
        cost_estimate=pl.CostEstimate(
            flops=4 * columns * rows * BLK, bytes_accessed=4 << 20, transcendentals=0
        ),
    )(*in_vmem(queries, own_keys, own_values))


def far_kernel(
    live_ref, query_ref, far_ref, level_ref, mean_ref, out_ref, turned, valued, ready, sems
):
    heads_here = query_ref.shape[1] // HD
    picks = far_ref.shape[1]

    def leave(h):
        columns = slice(h * HD, (h + 1) * HD)
        return pltpu.make_async_copy(ready.at[h], out_ref.at[:, columns], sems.at[h])

    for s in range(picks):
        place = slice(s * BLK, (s + 1) * BLK)
        turned[:HD, place] = far_ref[:, s, :, 0].reshape(BLK, HD).T
        valued[place, :HD] = far_ref[:, s, :, 1].reshape(BLK, HD)
    turned[HD:] = turned[:HD]
    valued[:, HD:] = jnp.ones((picks * BLK, HD), valued.dtype)

    def attend(first, last):
        place = slice(first * BLK, (last + 1) * BLK)

        def score(h, begin, end):
            query_rows = split_queries(query_ref[begin:end, h * HD : (h + 1) * HD])
            return jnp.dot(query_rows, turned[:, place], preferred_element_type=jnp.float32)

        def finish(h, begin, end, scores):
            rows = slice(begin, end)
            level = level_ref[h, rows]
            top = jnp.maximum(jnp.max(scores, axis=1, keepdims=True), level[:, :1])
            weights = jnp.exp2(scores - top).astype(jnp.bfloat16)
            product = jnp.dot(weights, valued[place], preferred_element_type=jnp.float32)
            scale = jnp.exp2(level - top)
            total = product[:, HD:] + scale
            product = product[:, :HD] + mean_ref[h, rows] * scale
            ready[h, rows] = (product / total).astype(ready.dtype)
            if end == BLK:
                leave(h).start()

        size = CHUNK if last > first else 2 * CHUNK
        in_turn(units_of(heads_here, size), score, finish)

    rank = lax.axis_index("ctx")

    @pl.when(rank >= picks)
    def _():
        attend(0, picks - 1)

    @pl.when(rank < picks)
    def _():
        flags = live_ref[...]
        live = [flags[0, s] > 0 for s in range(picks)]
        for which in itertools.product((False, True), repeat=picks):
            slots = [s for s in range(picks) if which[s]]
            met = functools.reduce(
                jnp.logical_and, [flag if on else ~flag for flag, on in zip(live, which)]
            )
            if len(slots) == picks:
                continue

            @pl.when(met)
            def _():
                if slots:
                    attend(slots[0], slots[-1])
                else:
                    for h in range(heads_here):
                        ready[h] = mean_ref[h].astype(ready.dtype)
                        leave(h).start()

    for h in range(heads_here):
        leave(h).wait()


def attend_far(live, queries, far, near):
    rows, columns = queries.shape
    keys_here = far.shape[1] * BLK
    return pl.pallas_call(
        far_kernel,
        out_shape=jax.ShapeDtypeStruct(queries.shape, queries.dtype),
        in_specs=[VMEM] * 5,
        out_specs=ANY,
        scratch_shapes=[
            pltpu.VMEM((2 * HD, keys_here), jnp.bfloat16),
            pltpu.VMEM((keys_here, 2 * HD), jnp.bfloat16),
            pltpu.VMEM((columns // HD, rows, HD), jnp.bfloat16),
            pltpu.SemaphoreType.DMA((columns // HD,)),
        ],
        compiler_params=LARGE,
    )(*in_vmem(live, queries, far, *near))


def other_head(x):
    return lax.ppermute(x, "head", [(0, 1), (1, 0)])


def own_block(keys, values, heads, head_rank):
    if heads == 2:
        columns = lambda rank: jnp.stack(
            [lax.dynamic_slice_in_dim(x, rank * HD, HD, 1) for x in (keys, values)]
        )
        mine = columns(head_rank)
        came = lax.ppermute(columns(1 - head_rank), "head", [(0, 1), (1, 0)])
        return jnp.where(
            head_rank == 0,
            jnp.concatenate([mine, came], axis=1),
            jnp.concatenate([came, mine], axis=1),
        )
    by_head = jnp.stack([keys, values]).reshape(2, -1, heads, HD).transpose(2, 0, 1, 3)
    own = lax.all_to_all(by_head, "head", split_axis=0, concat_axis=0, tiled=True)
    return own.transpose(1, 0, 2, 3).reshape(2, BLK, HD)


def on_device(heads, ranks, queries, keys, values, selected):
    lists = selected[0]
    picks = lists.shape[1] - 1
    head_rank = lax.axis_index("head")
    ctx_rank = lax.axis_index("ctx")
    share = keys.shape[0] // ranks

    order = [(i + ranks // 2) % ranks for i in range(ranks)]

    pieces, slots = pack(keys, values, selected.transpose(2, 0, 1), heads, ranks)
    pieces = pieces.reshape(heads * ranks, 2, share, HD)
    pieces = lax.all_to_all(pieces, ("head", "ctx"), split_axis=0, concat_axis=0, tiled=True)
    pieces = pieces.reshape(heads, ranks, 2, share, HD)

    pieces, queries, keys, values = lax.optimization_barrier((pieces, queries, keys, values))

    far = pick_pieces(slots, pieces, order)
    far = lax.all_to_all(
        far, "ctx", split_axis=0, concat_axis=0, axis_index_groups=[order], tiled=True
    )
    if share % 16:
        far = far.transpose(1, 3, 0, 2, 4, 5).reshape(1, picks, 2, BLK, HD)[:, :, None]

    own = own_block(keys, values, heads, head_rank)
    near = attend_near(queries, own[0], own[1])
    chosen = lax.dynamic_index_in_dim(lists, ctx_rank, 0, keepdims=False)[1:]
    live = (chosen != ctx_rank).astype(jnp.int32)[None]
    return attend_far(live, queries, far, near)


def solution(mesh):
    return jax.shard_map(
        functools.partial(on_device, mesh.shape["head"], mesh.shape["ctx"]),
        mesh=mesh,
        in_specs=(
            P("ctx", "head"),
            P(("ctx", "head"), None),
            P(("ctx", "head"), None),
            P("head", None, None),
        ),
        out_specs=P("ctx", "head"),
        check_vma=False,
    )
```

time: 41.8 us -> 40.3 us (0.964)
  the two profiles are of different devices: /device:TPU:4 before, /device:TPU:16 now
where the time goes in v8:
time: 40.3 us; the launch traced here: 40 us
  blocking collectives  14.5 us (36%)
  waiting for transfers between devices  10.5 us (26%)
  Pallas kernels  8.05 us (20%)
  starting transfers between devices  4.88 us (12%)
  local copies, waits for them, and re-layouts  1.69 us (4%)
    all_to_all x1, blocking collectives, on_device(): lax.all_to_all(pieces, ('head', 'ctx'), split_axis=0, concat_axis=0, tile...  14.5 us
    all_to_all x1, waiting for transfers between devices, on_device(): lax.all_to_all(far, 'ctx', split_axis=0, concat_axis=0, axis_index_groups...  6.11 us
    ppermute x1, waiting for transfers between devices, own_block(): came = lax.ppermute(columns(1 - head_rank), 'head', [(0, 1), (1, 0)])  4.41 us
    all_to_all x1, starting transfers between devices, on_device(): lax.all_to_all(far, 'ctx', split_axis=0, concat_axis=0, axis_index_groups...  4.27 us
    pallas_call x1, Pallas kernels, attend_far(): pl.pallas_call(far_kernel, out_shape=jax.ShapeDtypeStruct(queries.shape,...  4.04 us
    pallas_call x1, Pallas kernels, attend_near(): pl.pallas_call(near_kernel, out_shape=[pltpu.VMEM((columns // HD, rows, H...  2.1 us
    unnamed x8, local copies, waits for them, and re-layouts  1.62 us
    pallas_call x1, Pallas kernels, pack(): pl.pallas_call(pack_kernel, out_shape=[pltpu.VMEM((heads, ranks, 2, share...  0.98 us
  transfers between devices with their start and end apart: 2, of which 2 were waited for; matrix products, arithmetic and copies ran while one was open for 1% of the time, Pallas kernels for 5%

profile of v8, /device:TPU:16, one launch (start us, length us, event | category | flops | bytes accessed | tf_op | source)
XLA Modules:
  0.0 40.0 jit_solution(10091376123012479544)
XLA Ops:
  0.0 1.0 %shard_map.46 = (bf16[2,16,2,16,128]{4,3,2,1,0:T(8,128)(2,1)S(1)}, s32[3,1,16]{2,1,0:T(1,128)S(1)}) custom-call(bf16[16,16,256]{2,1,0:T(8,128)(2,1)} %bitcast.21, bf16[16,16,256]{2,1,0:T(8,128)(2,1)} %bitcast.22, s32[3,1,16]{2,1,0:T(1,128)} %bitcast.23), custom_call_target="tpu_custom_call" | custom-call | tf_op jit(solution)/shard_map/pallas_call | solution.py:50
  1.0 14.5 %all_to_all.10 = bf16[32,2,16,128]{3,2,1,0:T(8,128)(2,1)S(1)} all-to-all(bf16[32,2,16,128]{3,2,1,0:T(8,128)(2,1)S(1)} %bitcast.19), channel_id=1, replica_groups=mesh['head'=2,'ctx'=16] {'head','ctx'}, dimensions={0} | all-to-all | bytes 524288 | tf_op jit(solution)/shard_map/all_to_all | solution.py:270
  15.4 0.9 %shard_map.47 = bf16[16,2,2,2,16,128]{5,4,3,2,1,0:T(8,128)(2,1)} custom-call(s32[3,1,16]{2,1,0:T(1,128)S(1)} %get-tuple-element.15.slots_ref, bf16[2,16,2,16,128]{4,3,2,1,0:T(8,128)(2,1)S(1)} %bitcast.18), custom_call_target="tpu_custom_call" | custom-call | tf_op jit(solution)/shard_map/pallas_call | solution.py:77
  16.4 0.0 copy-start.1
  16.4 0.0 copy-start.2
  16.4 4.3 %all-to-all-start.1 = ((bf16[16,2,2,2,16,128]{5,4,3,2,1,0:T(8,128)(2,1)}), bf16[16,2,2,2,16,128]{5,4,3,2,1,0:T(8,128)(2,1)S(1)}, u32[]{:S(2)}, u32[]{:S(2)}) async-start(bf16[16,2,2,2,16,128]{5,4,3,2,1,0:T(8,128)(2,1)} %shard_map.47), calls=%async_computation.1 | async-start | bytes 1048576 | tf_op jit(solution)/shard_map/all_to_all | solution.py:276
  20.7 0.0 copy-done.1
  20.7 0.0 copy-done.2
  20.7 0.1 dynamic-slice_bitcast_fusion.2
  20.8 0.6 %collective-permute-start = (bf16[2,256,128]{2,1,0:T(8,128)(2,1)S(1)}, bf16[2,256,128]{2,1,0:T(8,128)(2,1)S(1)}, u32[]{:S(2)}, u32[]{:S(2)}) collective-permute-start(bf16[2,256,128]{2,1,0:T(8,128)(2,1)S(1)} %pad_maximum_fusion), channel_id=1, source_target_pairs={{0,16},{16,0},{1,17},{17,1},{2,18},{18,2},{3,19},{19,3},{4,20},{20... | collective-permute-start | bytes 393224 | tf_op jit(solution)/shard_map/ppermute | solution.py:248
  21.4 0.0 copy-start.3
  21.4 0.7 %copy-done.3 = s32[1,16,3]{1,0,2:T(1,128)S(1)} copy-done((s32[1,16,3]{1,0,2:T(1,128)S(1)}, s32[1,16,3]{1,0,2:T(1,128)}, u32[]{:S(2)}) %copy-start.3) | copy-done | bytes 216
  22.1 0.2 fusion
  22.2 4.4 %collective-permute-done = bf16[2,256,128]{2,1,0:T(8,128)(2,1)S(1)} collective-permute-done((bf16[2,256,128]{2,1,0:T(8,128)(2,1)S(1)}, bf16[2,256,128]{2,1,0:T(8,128)(2,1)S(1)}, u32[]{:S(2)}, u32[]{:S(2)}) %collective-permute-start) | collective-permute-done | bytes 131104 | tf_op jit(solution)/shard_map/ppermute | solution.py:248
  26.7 0.0 copy-start
  26.7 0.1 maximum_select_fusion
  26.8 0.9 %copy-done = bf16[512,512]{1,0:T(8,128)(2,1)S(1)} copy-done((bf16[512,512]{1,0:T(8,128)(2,1)S(1)}, bf16[512,512]{1,0:T(8,128)(2,1)}, u32[]{:S(2)}) %copy-start) | copy-done | bytes 524312
  27.7 2.1 %shard_map.48 = (f32[4,512,128]{2,1,0:T(8,128)S(1)}, f32[4,512,128]{2,1,0:T(8,128)S(1)}) custom-call(bf16[512,512]{1,0:T(8,128)(2,1)S(1)} %copy-done, bf16[512,128]{1,0:T(8,128)(2,1)S(1)} %get-tuple-element.22.key_ref, bf16[512,128]{1,0:T(8,128)(2,1)S(1)} %get-tuple-element.21.value_ref), custom_call_target="tpu_custom_call" | custom-call | flops 536870912 | bytes 4194304 | tf_op jit(solution)/shard_map/pallas_call | solution.py:133
  29.8 6.1 %all-to-all-done.1.far_ref = bf16[16,2,2,2,16,128]{5,4,3,2,1,0:T(8,128)(2,1)S(1)} async-done(((bf16[16,2,2,2,16,128]{5,4,3,2,1,0:T(8,128)(2,1)}), bf16[16,2,2,2,16,128]{5,4,3,2,1,0:T(8,128)(2,1)S(1)}, u32[]{:S(2)}, u32[]{:S(2)}) %all-to-all-start.1) | async-done | bytes 524320 | tf_op jit(solution)/shard_map/all_to_all | solution.py:276
  35.9 4.0 %shard_map.49 = bf16[512,512]{1,0:T(8,128)(2,1)} custom-call(s32[1,2]{1,0:T(1,128)S(1)} %bitcast.20, bf16[512,512]{1,0:T(8,128)(2,1)S(1)} %copy-done, bf16[16,2,2,2,16,128]{5,4,3,2,1,0:T(8,128)(2,1)S(1)} %all-to-all-done.1.far_ref, f32[4,512,128]{2,1,0:T(8,128)S(1)} %get-tuple-element.19.level_ref, f32[4,512,128]{2,1,0:T(8,128)S(1)} %get-tuple-element.20.mean_ref), custom_call_target="tpu_custom_call" | custom-call | tf_op jit(solution)/shard_map/pallas_call | solution.py:223
  (2 shorter events, 0.0 us)
Async XLA Ops:
  16.4 4.3 %copy-start.1 = (bf16[256,256]{1,0:T(8,128)(2,1)S(1)}, bf16[256,256]{1,0:T(8,128)(2,1)}, u32[]{:S(2)}) copy-start(bf16[256,256]{1,0:T(8,128)(2,1)} %param.5) | copy-start | bytes 393220
  16.4 4.3 %copy-start.2 = (bf16[256,256]{1,0:T(8,128)(2,1)S(1)}, bf16[256,256]{1,0:T(8,128)(2,1)}, u32[]{:S(2)}) copy-start(bf16[256,256]{1,0:T(8,128)(2,1)} %param.6) | copy-start | bytes 393220
  16.4 19.5 %all-to-all-start.1 = ((bf16[16,2,2,2,16,128]{5,4,3,2,1,0:T(8,128)(2,1)}), bf16[16,2,2,2,16,128]{5,4,3,2,1,0:T(8,128)(2,1)S(1)}, u32[]{:S(2)}, u32[]{:S(2)}) async-start(bf16[16,2,2,2,16,128]{5,4,3,2,1,0:T(8,128)(2,1)} %shard_map.47), calls=%async_computation.1 | async-start | bytes 1048576 | tf_op jit(solution)/shard_map/all_to_all | solution.py:276
  20.8 5.9 %collective-permute-start = (bf16[2,256,128]{2,1,0:T(8,128)(2,1)S(1)}, bf16[2,256,128]{2,1,0:T(8,128)(2,1)S(1)}, u32[]{:S(2)}, u32[]{:S(2)}) collective-permute-start(bf16[2,256,128]{2,1,0:T(8,128)(2,1)S(1)} %pad_maximum_fusion), channel_id=1, source_target_pairs={{0,16},{16,0},{1,17},{17,1},{2,18},{18,2},{3,19},{19,3},{4,20},{20... | collective-permute-start | bytes 393224 | tf_op jit(solution)/shard_map/ppermute | solution.py:248
  21.4 0.7 %copy-start.3 = (s32[1,16,3]{1,0,2:T(1,128)S(1)}, s32[1,16,3]{1,0,2:T(1,128)}, u32[]{:S(2)}) copy-start(s32[1,16,3]{1,0,2:T(1,128)} %param.7) | copy-start | bytes 580
  26.7 1.0 %copy-start = (bf16[512,512]{1,0:T(8,128)(2,1)S(1)}, bf16[512,512]{1,0:T(8,128)(2,1)}, u32[]{:S(2)}) copy-start(bf16[512,512]{1,0:T(8,128)(2,1)} %query_ref.1) | copy-start | bytes 1572868

commit v9 on v8

--- a/solution.py
+++ b/solution.py
@@ -25,62 +25,83 @@
 
 
 def pack_kernel(key_ref, value_ref, slots_ref, out_ref, slots_out, sems, slots_sem):
-    heads = out_ref.shape[0]
-    copies = [
-        pltpu.make_async_copy(
-            ref.at[:, :, h * HD : (h + 1) * HD], out_ref.at[h, :, kv], sems.at[kv, h]
-        )
-        for kv, ref in enumerate((key_ref, value_ref))
-        for h in range(heads)
-    ]
-    copies.append(pltpu.make_async_copy(slots_ref, slots_out, slots_sem))
+    group = lax.rem(lax.axis_index("head") + lax.axis_index("ctx"), 2)
+    copies = [pltpu.make_async_copy(slots_ref, slots_out, slots_sem)]
+    for turn in range(2):
+        head = lax.rem(group + 1 - turn, 2)
+        columns = pl.ds(pl.multiple_of(head * HD, HD), HD)
+        for kv, ref in enumerate((key_ref, value_ref)):
+            copies.append(
+                pltpu.make_async_copy(
+                    ref.at[:, :, columns], out_ref.at[:, turn, kv], sems.at[kv, turn]
+                )
+            )
     for copy in copies:
         copy.start()
     for copy in copies:
         copy.wait()
 
 
-def pack(keys, values, slots, heads, ranks):
+def pack(keys, values, slots, ranks):
     rows, columns = keys.shape
-    share = rows // ranks
-    if share % 16:
-        both = jnp.stack([keys, values]).reshape(2, ranks, share, heads, HD)
-        return both.transpose(3, 1, 0, 2, 4), slots
-    operands = [keys.reshape(ranks, share, columns), values.reshape(ranks, share, columns), slots]
+    pairs = ranks // 2
+    operands = [x.reshape(pairs, rows // pairs, columns) for x in (keys, values)] + [slots]
     return pl.pallas_call(
         pack_kernel,
         out_shape=[
-            pltpu.VMEM((heads, ranks, 2, share, HD), keys.dtype),
+            pltpu.VMEM((pairs, 2, 2, rows // pairs, HD), keys.dtype),
             pltpu.VMEM(slots.shape, slots.dtype),
         ],
         in_specs=[ANY] * 3,
         out_specs=[VMEM] * 2,
-        scratch_shapes=[pltpu.SemaphoreType.DMA((2, heads)), pltpu.SemaphoreType.DMA],
+        scratch_shapes=[pltpu.SemaphoreType.DMA((2, 2)), pltpu.SemaphoreType.DMA],
         compiler_params=SMALL,
     )(*[pltpu.with_memory_space_constraint(x, pltpu.HBM) for x in operands])
 
 
 def pick_kernel(order, slots_ref, pieces_ref, out_ref):
-    _, picks, parts = out_ref.shape[:3]
+    ranks, picks = out_ref.shape[:2]
     slots = slots_ref[...]
     for place, receiver in enumerate(order):
         for s in range(picks):
-            block = slots[s + 1, 0, receiver]
-            for part in range(parts):
-                out_ref[place, s, part] = pieces_ref[part, block]
+            out_ref[place, s] = pieces_ref[ranks - 1 - slots[s + 1, 0, receiver]]
 
 
 def pick_pieces(slots, pieces, order):
-    heads, ranks, _, share, _ = pieces.shape
-    if share % 16:
-        return pieces.swapaxes(0, 1)[slots[1:, 0].T[jnp.array(order)]]
+    ranks, *rest = pieces.shape
     return pl.pallas_call(
         functools.partial(pick_kernel, order),
-        out_shape=pltpu.VMEM((ranks, slots.shape[0] - 1, heads, 2, share, HD), pieces.dtype),
+        out_shape=pltpu.VMEM((ranks, slots.shape[0] - 1, *rest), pieces.dtype),
         in_specs=[VMEM, VMEM],
         out_specs=VMEM,
         compiler_params=SMALL,
     )(*in_vmem(slots, pieces))
+
+
+def send_selected(keys, values, slots, ranks, order):
+    pieces, slots = pack(keys, values, slots, ranks)
+    pieces = pieces.reshape(ranks, *pieces.shape[2:])
+    groups = [
+        [((g + r) % 2) * ranks + r for r in reversed(range(ranks))] for g in range(2)
+    ]
+    pieces = lax.all_to_all(
+        pieces,
+        ("head", "ctx"),
+        split_axis=0,
+        concat_axis=0,
+        axis_index_groups=groups,
+        tiled=True,
+    )
+    return pieces, slots
+
+
+def send_selected_of_many(keys, values, heads, ranks):
+    share = keys.shape[0] // ranks
+    pieces = jnp.stack([keys, values]).reshape(2, ranks, share, heads, HD)
+    pieces = pieces.transpose(3, 1, 0, 2, 4).reshape(heads * ranks, 2, share, HD)
+    pieces = lax.all_to_all(pieces, ("head", "ctx"), split_axis=0, concat_axis=0, tiled=True)
+    pieces = pieces.reshape(heads, ranks, 2, share, HD)
+    return pieces.transpose(1, 2, 0, 3, 4).reshape(ranks, 2, heads * share, HD)
 
 
 def units_of(heads_here, size):
@@ -158,8 +179,8 @@
 
     for s in range(picks):
         place = slice(s * BLK, (s + 1) * BLK)
-        turned[:HD, place] = far_ref[:, s, :, 0].reshape(BLK, HD).T
-        valued[place, :HD] = far_ref[:, s, :, 1].reshape(BLK, HD)
+        turned[:HD, place] = far_ref[:, s, 0].reshape(BLK, HD).T
+        valued[place, :HD] = far_ref[:, s, 1].reshape(BLK, HD)
     turned[HD:] = turned[:HD]
     valued[:, HD:] = jnp.ones((picks * BLK, HD), valued.dtype)
 
@@ -173,8 +194,13 @@
         def finish(h, begin, end, scores):
             rows = slice(begin, end)
             level = level_ref[h, rows]
-            top = jnp.maximum(jnp.max(scores, axis=1, keepdims=True), level[:, :1])
-            weights = jnp.exp2(scores - top).astype(jnp.bfloat16)
+            top = jnp.maximum(
+                jnp.broadcast_to(jnp.max(scores, axis=1, keepdims=True), level.shape), level
+            )
+            tiles = [scores[:, i : i + HD] for i in range(0, scores.shape[1], HD)]
+            weights = jnp.concatenate(
+                [jnp.exp2(tile - top).astype(jnp.bfloat16) for tile in tiles], axis=1
+            )
             product = jnp.dot(weights, valued[place], preferred_element_type=jnp.float32)
             scale = jnp.exp2(level - top)
             total = product[:, HD:] + scale
@@ -265,19 +291,24 @@
 
     order = [(i + ranks // 2) % ranks for i in range(ranks)]
 
-    pieces, slots = pack(keys, values, selected.transpose(2, 0, 1), heads, ranks)
-    pieces = pieces.reshape(heads * ranks, 2, share, HD)
-    pieces = lax.all_to_all(pieces, ("head", "ctx"), split_axis=0, concat_axis=0, tiled=True)
-    pieces = pieces.reshape(heads, ranks, 2, share, HD)
+    slots = selected.transpose(2, 0, 1)
+    plain = heads == 2 and share % 8 == 0 and ranks % 2 == 0
+    if plain:
+        pieces, slots = send_selected(keys, values, slots, ranks, order)
+    else:
+        pieces = send_selected_of_many(keys, values, heads, ranks)
 
     pieces, queries, keys, values = lax.optimization_barrier((pieces, queries, keys, values))
 
-    far = pick_pieces(slots, pieces, order)
+    if plain:
+        far = pick_pieces(slots, pieces, order)
+    else:
+        far = pieces[slots[1:, 0].T[jnp.array(order)]]
     far = lax.all_to_all(
         far, "ctx", split_axis=0, concat_axis=0, axis_index_groups=[order], tiled=True
     )
-    if share % 16:
-        far = far.transpose(1, 3, 0, 2, 4, 5).reshape(1, picks, 2, BLK, HD)[:, :, None]
+    if not plain:
+        far = far.transpose(1, 2, 0, 3, 4).reshape(1, picks, 2, BLK, HD)
 
     own = own_block(keys, values, heads, head_rank)
     near = attend_near(queries, own[0], own[1])

time: 40.3 us -> 37.8 us (0.938)
  blocking collectives: 14.5 us -> 12.4 us
  waiting for transfers between devices: 10.5 us -> 9.95 us
  starting transfers between devices: 4.88 us -> 5.32 us
    all_to_all x1, blocking collectives: 14.5 us -> 12.4 us  [send_selected(): lax.all_to_all(pieces, ('head', 'ctx'), split_axis=0, concat_axis=0, axis...]
    ppermute x1, starting transfers between devices: 0.61 us -> 1.18 us  [own_block(): came = lax.ppermute(columns(1 - head_rank), 'head', [(0, 1), (1, 0)])]
    ppermute x1, waiting for transfers between devices: 4.41 us -> 3.95 us  [own_block(): came = lax.ppermute(columns(1 - head_rank), 'head', [(0, 1), (1, 0)])]
  transfers between devices with their start and end apart: 2 -> 2, of which waited for: 2 -> 2; matrix products, arithmetic and copies ran while one was open for 1% -> 1% of each run, Pallas kernels for 5% -> 6%
where the time goes in v9:
time: 37.8 us; the launch traced here: 37.4 us
  blocking collectives  12.4 us (33%)
  waiting for transfers between devices  9.95 us (26%)
  Pallas kernels  7.75 us (21%)
  starting transfers between devices  5.32 us (14%)
  local copies, waits for them, and re-layouts  1.69 us (4%)
    all_to_all x1, blocking collectives, send_selected(): lax.all_to_all(pieces, ('head', 'ctx'), split_axis=0, concat_axis=0, axis...  12.4 us
    all_to_all x1, waiting for transfers between devices, on_device(): lax.all_to_all(far, 'ctx', split_axis=0, concat_axis=0, axis_index_groups...  6 us
    all_to_all x1, starting transfers between devices, on_device(): lax.all_to_all(far, 'ctx', split_axis=0, concat_axis=0, axis_index_groups...  4.14 us
    ppermute x1, waiting for transfers between devices, own_block(): came = lax.ppermute(columns(1 - head_rank), 'head', [(0, 1), (1, 0)])  3.95 us
    pallas_call x1, Pallas kernels, attend_far(): pl.pallas_call(far_kernel, out_shape=jax.ShapeDtypeStruct(queries.shape,...  3.72 us
    pallas_call x1, Pallas kernels, attend_near(): pl.pallas_call(near_kernel, out_shape=[pltpu.VMEM((columns // HD, rows, H...  2.11 us
    unnamed x8, local copies, waits for them, and re-layouts  1.62 us
    ppermute x1, starting transfers between devices, own_block(): came = lax.ppermute(columns(1 - head_rank), 'head', [(0, 1), (1, 0)])  1.18 us
  transfers between devices with their start and end apart: 2, of which 2 were waited for; matrix products, arithmetic and copies ran while one was open for 1% of the time, Pallas kernels for 6%

profile of v9, /device:TPU:16, one launch (start us, length us, event | category | flops | bytes accessed | tf_op | source)
XLA Modules:
  0.0 37.4 jit_solution(8567429373436210639)
XLA Ops:
  0.0 1.0 %shard_map.46 = (bf16[8,2,2,32,128]{4,3,2,1,0:T(8,128)(2,1)S(1)}, s32[3,1,16]{2,1,0:T(1,128)S(1)}) custom-call(bf16[8,32,256]{2,1,0:T(8,128)(2,1)} %bitcast.19, bf16[8,32,256]{2,1,0:T(8,128)(2,1)} %bitcast.20, s32[3,1,16]{2,1,0:T(1,128)} %bitcast.21), custom_call_target="tpu_custom_call" | custom-call | tf_op jit(solution)/shard_map/pallas_call | solution.py:49
  1.0 12.4 %all_to_all.10.pieces_ref = bf16[16,2,32,128]{3,2,1,0:T(8,128)(2,1)S(1)} all-to-all(bf16[16,2,32,128]{3,2,1,0:T(8,128)(2,1)S(1)} %bitcast.17), channel_id=1, replica_groups={{31,14,29,12,27,10,25,8,23,6,21,4,19,2,17,0},{15,30,13,28,11,26,9,24,7,..., dimensions={0} | all-to-all | bytes 524288 | tf_op jit(solution)/shard_map/all_to_all | solution.py:87
  13.4 0.9 %shard_map.47 = bf16[16,2,2,32,128]{4,3,2,1,0:T(8,128)(2,1)} custom-call(s32[3,1,16]{2,1,0:T(1,128)S(1)} %get-tuple-element.15.slots_ref, bf16[16,2,32,128]{3,2,1,0:T(8,128)(2,1)S(1)} %all_to_all.10.pieces_ref), custom_call_target="tpu_custom_call" | custom-call | tf_op jit(solution)/shard_map/pallas_call | solution.py:72
  14.3 0.0 copy-start.1
  14.3 0.0 copy-start.2
  14.3 4.1 %all-to-all-start.1 = ((bf16[16,2,2,32,128]{4,3,2,1,0:T(8,128)(2,1)}), bf16[16,2,2,32,128]{4,3,2,1,0:T(8,128)(2,1)S(1)}, u32[]{:S(2)}, u32[]{:S(2)}) async-start(bf16[16,2,2,32,128]{4,3,2,1,0:T(8,128)(2,1)} %shard_map.47), calls=%async_computation.1 | async-start | bytes 1048576 | tf_op jit(solution)/shard_map/all_to_all | solution.py:307
  18.5 0.0 copy-done.1
  18.5 0.0 copy-done.2
  18.5 0.1 dynamic-slice_bitcast_fusion.2
  18.6 1.2 %collective-permute-start = (bf16[2,256,128]{2,1,0:T(8,128)(2,1)S(1)}, bf16[2,256,128]{2,1,0:T(8,128)(2,1)S(1)}, u32[]{:S(2)}, u32[]{:S(2)}) collective-permute-start(bf16[2,256,128]{2,1,0:T(8,128)(2,1)S(1)} %pad_maximum_fusion), channel_id=1, source_target_pairs={{0,16},{16,0},{1,17},{17,1},{2,18},{18,2},{3,19},{19,3},{4,20},{20... | collective-permute-start | bytes 393224 | tf_op jit(solution)/shard_map/ppermute | solution.py:274
  19.8 0.0 copy-start.3
  19.8 0.7 %copy-done.3 = s32[1,16,3]{1,0,2:T(1,128)S(1)} copy-done((s32[1,16,3]{1,0,2:T(1,128)S(1)}, s32[1,16,3]{1,0,2:T(1,128)}, u32[]{:S(2)}) %copy-start.3) | copy-done | bytes 216
  20.4 0.2 fusion
  20.6 3.9 %collective-permute-done = bf16[2,256,128]{2,1,0:T(8,128)(2,1)S(1)} collective-permute-done((bf16[2,256,128]{2,1,0:T(8,128)(2,1)S(1)}, bf16[2,256,128]{2,1,0:T(8,128)(2,1)S(1)}, u32[]{:S(2)}, u32[]{:S(2)}) %collective-permute-start) | collective-permute-done | bytes 131104 | tf_op jit(solution)/shard_map/ppermute | solution.py:274
  24.6 0.0 copy-start
  24.6 0.1 maximum_select_fusion
  24.7 0.9 %copy-done = bf16[512,512]{1,0:T(8,128)(2,1)S(1)} copy-done((bf16[512,512]{1,0:T(8,128)(2,1)S(1)}, bf16[512,512]{1,0:T(8,128)(2,1)}, u32[]{:S(2)}) %copy-start) | copy-done | bytes 524312
  25.6 2.1 %shard_map.48 = (f32[4,512,128]{2,1,0:T(8,128)S(1)}, f32[4,512,128]{2,1,0:T(8,128)S(1)}) custom-call(bf16[512,512]{1,0:T(8,128)(2,1)S(1)} %copy-done, bf16[512,128]{1,0:T(8,128)(2,1)S(1)} %get-tuple-element.22.key_ref, bf16[512,128]{1,0:T(8,128)(2,1)S(1)} %get-tuple-element.21.value_ref), custom_call_target="tpu_custom_call" | custom-call | flops 536870912 | bytes 4194304 | tf_op jit(solution)/shard_map/pallas_call | solution.py:154
  27.7 6.0 %all-to-all-done.1.far_ref = bf16[16,2,2,32,128]{4,3,2,1,0:T(8,128)(2,1)S(1)} async-done(((bf16[16,2,2,32,128]{4,3,2,1,0:T(8,128)(2,1)}), bf16[16,2,2,32,128]{4,3,2,1,0:T(8,128)(2,1)S(1)}, u32[]{:S(2)}, u32[]{:S(2)}) %all-to-all-start.1) | async-done | bytes 524320 | tf_op jit(solution)/shard_map/all_to_all | solution.py:307
  33.7 3.7 %shard_map.49 = bf16[512,512]{1,0:T(8,128)(2,1)} custom-call(s32[1,2]{1,0:T(1,128)S(1)} %bitcast.18, bf16[512,512]{1,0:T(8,128)(2,1)S(1)} %copy-done, bf16[16,2,2,32,128]{4,3,2,1,0:T(8,128)(2,1)S(1)} %all-to-all-done.1.far_ref, f32[4,512,128]{2,1,0:T(8,128)S(1)} %get-tuple-element.19.level_ref, f32[4,512,128]{2,1,0:T(8,128)S(1)} %get-tuple-element.20.mean_ref), custom_call_target="tpu_custom_call" | custom-call | tf_op jit(solution)/shard_map/pallas_call | solution.py:249
  (2 shorter events, 0.0 us)
Async XLA Ops:
  14.3 4.2 %copy-start.1 = (bf16[256,256]{1,0:T(8,128)(2,1)S(1)}, bf16[256,256]{1,0:T(8,128)(2,1)}, u32[]{:S(2)}) copy-start(bf16[256,256]{1,0:T(8,128)(2,1)} %param.5) | copy-start | bytes 393220
  14.3 4.2 %copy-start.2 = (bf16[256,256]{1,0:T(8,128)(2,1)S(1)}, bf16[256,256]{1,0:T(8,128)(2,1)}, u32[]{:S(2)}) copy-start(bf16[256,256]{1,0:T(8,128)(2,1)} %param.6) | copy-start | bytes 393220
  14.3 19.4 %all-to-all-start.1 = ((bf16[16,2,2,32,128]{4,3,2,1,0:T(8,128)(2,1)}), bf16[16,2,2,32,128]{4,3,2,1,0:T(8,128)(2,1)S(1)}, u32[]{:S(2)}, u32[]{:S(2)}) async-start(bf16[16,2,2,32,128]{4,3,2,1,0:T(8,128)(2,1)} %shard_map.47), calls=%async_computation.1 | async-start | bytes 1048576 | tf_op jit(solution)/shard_map/all_to_all | solution.py:307
  18.6 6.0 %collective-permute-start = (bf16[2,256,128]{2,1,0:T(8,128)(2,1)S(1)}, bf16[2,256,128]{2,1,0:T(8,128)(2,1)S(1)}, u32[]{:S(2)}, u32[]{:S(2)}) collective-permute-start(bf16[2,256,128]{2,1,0:T(8,128)(2,1)S(1)} %pad_maximum_fusion), channel_id=1, source_target_pairs={{0,16},{16,0},{1,17},{17,1},{2,18},{18,2},{3,19},{19,3},{4,20},{20... | collective-permute-start | bytes 393224 | tf_op jit(solution)/shard_map/ppermute | solution.py:274
  19.8 0.7 %copy-start.3 = (s32[1,16,3]{1,0,2:T(1,128)S(1)}, s32[1,16,3]{1,0,2:T(1,128)}, u32[]{:S(2)}) copy-start(s32[1,16,3]{1,0,2:T(1,128)} %param.7) | copy-start | bytes 580
  24.6 1.0 %copy-start = (bf16[512,512]{1,0:T(8,128)(2,1)S(1)}, bf16[512,512]{1,0:T(8,128)(2,1)}, u32[]{:S(2)}) copy-start(bf16[512,512]{1,0:T(8,128)(2,1)} %query_ref.1) | copy-start | bytes 1572868

commit v10 on v9

--- a/solution.py
+++ b/solution.py
@@ -27,15 +27,18 @@
 def pack_kernel(key_ref, value_ref, slots_ref, out_ref, slots_out, sems, slots_sem):
     group = lax.rem(lax.axis_index("head") + lax.axis_index("ctx"), 2)
     copies = [pltpu.make_async_copy(slots_ref, slots_out, slots_sem)]
+    half = key_ref.shape[0] // 2
     for turn in range(2):
         head = lax.rem(group + 1 - turn, 2)
         columns = pl.ds(pl.multiple_of(head * HD, HD), HD)
         for kv, ref in enumerate((key_ref, value_ref)):
-            copies.append(
-                pltpu.make_async_copy(
-                    ref.at[:, :, columns], out_ref.at[:, turn, kv], sems.at[kv, turn]
+            for part in range(2):
+                some = slice(part * half, (part + 1) * half)
+                copies.append(
+                    pltpu.make_async_copy(
+                        ref.at[some, :, columns], out_ref.at[some, turn, kv], sems.at[kv, turn, part]
+                    )
                 )
-            )
     for copy in copies:
         copy.start()
     for copy in copies:
@@ -54,26 +57,29 @@
         ],
         in_specs=[ANY] * 3,
         out_specs=[VMEM] * 2,
-        scratch_shapes=[pltpu.SemaphoreType.DMA((2, 2)), pltpu.SemaphoreType.DMA],
+        scratch_shapes=[pltpu.SemaphoreType.DMA((2, 2, 2)), pltpu.SemaphoreType.DMA],
         compiler_params=SMALL,
     )(*[pltpu.with_memory_space_constraint(x, pltpu.HBM) for x in operands])
 
 
-def pick_kernel(order, slots_ref, pieces_ref, out_ref):
+def pick_kernel(order, slots_ref, pieces_ref, out_ref, sem):
     ranks, picks = out_ref.shape[:2]
     slots = slots_ref[...]
     for place, receiver in enumerate(order):
         for s in range(picks):
-            out_ref[place, s] = pieces_ref[ranks - 1 - slots[s + 1, 0, receiver]]
+            piece = pieces_ref.at[ranks - 1 - slots[s + 1, 0, receiver]]
+            pltpu.make_async_copy(piece, out_ref.at[place, s], sem).start()
+    pltpu.make_async_copy(out_ref, out_ref, sem).wait()
 
 
 def pick_pieces(slots, pieces, order):
     ranks, *rest = pieces.shape
     return pl.pallas_call(
         functools.partial(pick_kernel, order),
-        out_shape=pltpu.VMEM((ranks, slots.shape[0] - 1, *rest), pieces.dtype),
+        out_shape=jax.ShapeDtypeStruct((ranks, slots.shape[0] - 1, *rest), pieces.dtype),
         in_specs=[VMEM, VMEM],
-        out_specs=VMEM,
+        out_specs=ANY,
+        scratch_shapes=[pltpu.SemaphoreType.DMA],
         compiler_params=SMALL,
     )(*in_vmem(slots, pieces))
 
@@ -116,23 +122,15 @@
         finish(*unit, held.pop(0))
 
 
-def split_queries(query_rows):
-    scaled = query_rows.astype(jnp.float32) * FACTOR
-    high = scaled.astype(jnp.bfloat16)
-    low = (scaled - high.astype(jnp.float32)).astype(jnp.bfloat16)
-    return jnp.concatenate([high, low], axis=1)
-
-
 def near_kernel(
     query_ref, key_ref, value_ref, level_ref, mean_ref, turned, valued
 ):
-    turned[:HD] = key_ref[...].T
-    turned[HD:] = turned[:HD]
+    turned[...] = key_ref[...].T
     valued[:, :HD] = value_ref[...]
     valued[:, HD:] = jnp.ones(value_ref.shape, valued.dtype)
 
     def score(h, begin, end):
-        query_rows = split_queries(query_ref[begin:end, h * HD : (h + 1) * HD])
+        query_rows = query_ref[begin:end, h * HD : (h + 1) * HD]
         scores = jnp.dot(query_rows, turned[:, :end], preferred_element_type=jnp.float32)
         row_ids = lax.broadcasted_iota(jnp.int32, scores.shape, 0) + begin
         col_ids = lax.broadcasted_iota(jnp.int32, scores.shape, 1)
@@ -141,9 +139,9 @@
     def finish(h, begin, end, scores):
         rows = slice(begin, end)
         top = jnp.max(scores, axis=1, keepdims=True)
-        weights = jnp.exp2(scores - top).astype(jnp.bfloat16)
+        weights = jnp.exp2((scores - top) * FACTOR).astype(jnp.bfloat16)
         product = jnp.dot(weights, valued[:end], preferred_element_type=jnp.float32)
-        level_ref[h, rows] = top + jnp.log2(product[:, HD:])
+        level_ref[h, rows] = top + jnp.log2(product[:, HD:]) / FACTOR
         mean_ref[h, rows] = product[:, :HD] / product[:, HD:]
 
     in_turn(units_of(query_ref.shape[1] // HD, CHUNK), score, finish)
@@ -157,7 +155,7 @@
         in_specs=[VMEM] * 3,
         out_specs=[VMEM] * 2,
         scratch_shapes=[
-            pltpu.VMEM((2 * HD, BLK), jnp.bfloat16),
+            pltpu.VMEM((HD, BLK), jnp.bfloat16),
             pltpu.VMEM((BLK, 2 * HD), jnp.bfloat16),
         ],
         compiler_params=LARGE,
@@ -179,16 +177,15 @@
 
     for s in range(picks):
         place = slice(s * BLK, (s + 1) * BLK)
-        turned[:HD, place] = far_ref[:, s, 0].reshape(BLK, HD).T
+        turned[:, place] = far_ref[:, s, 0].reshape(BLK, HD).T
         valued[place, :HD] = far_ref[:, s, 1].reshape(BLK, HD)
-    turned[HD:] = turned[:HD]
     valued[:, HD:] = jnp.ones((picks * BLK, HD), valued.dtype)
 
     def attend(first, last):
         place = slice(first * BLK, (last + 1) * BLK)
 
         def score(h, begin, end):
-            query_rows = split_queries(query_ref[begin:end, h * HD : (h + 1) * HD])
+            query_rows = query_ref[begin:end, h * HD : (h + 1) * HD]
             return jnp.dot(query_rows, turned[:, place], preferred_element_type=jnp.float32)
 
         def finish(h, begin, end, scores):
@@ -199,18 +196,17 @@
             )
             tiles = [scores[:, i : i + HD] for i in range(0, scores.shape[1], HD)]
             weights = jnp.concatenate(
-                [jnp.exp2(tile - top).astype(jnp.bfloat16) for tile in tiles], axis=1
+                [jnp.exp2((tile - top) * FACTOR).astype(jnp.bfloat16) for tile in tiles], axis=1
             )
             product = jnp.dot(weights, valued[place], preferred_element_type=jnp.float32)
-            scale = jnp.exp2(level - top)
+            scale = jnp.exp2((level - top) * FACTOR)
             total = product[:, HD:] + scale
             product = product[:, :HD] + mean_ref[h, rows] * scale
             ready[h, rows] = (product / total).astype(ready.dtype)
             if end == BLK:
                 leave(h).start()
 
-        size = CHUNK if last > first else 2 * CHUNK
-        in_turn(units_of(heads_here, size), score, finish)
+        in_turn(units_of(heads_here, 2 * CHUNK), score, finish)
 
     rank = lax.axis_index("ctx")
 
@@ -252,7 +248,7 @@
         in_specs=[VMEM] * 5,
         out_specs=ANY,
         scratch_shapes=[
-            pltpu.VMEM((2 * HD, keys_here), jnp.bfloat16),
+            pltpu.VMEM((HD, keys_here), jnp.bfloat16),
             pltpu.VMEM((keys_here, 2 * HD), jnp.bfloat16),
             pltpu.VMEM((columns // HD, rows, HD), jnp.bfloat16),
             pltpu.SemaphoreType.DMA((columns // HD,)),

time: 37.8 us -> 37.6 us (level)
  Pallas kernels: 7.75 us -> 7.22 us
  transfers between devices with their start and end apart: 2 -> 2, of which waited for: 2 -> 2; matrix products, arithmetic and copies ran while one was open for 1% -> 1% of each run, Pallas kernels for 6% -> 5%
where the time goes in v10:
time: 37.6 us; the launch traced here: 37.2 us
  blocking collectives  12.4 us (33%)
  waiting for transfers between devices  10.2 us (27%)
  Pallas kernels  7.22 us (19%)
  starting transfers between devices  5.33 us (14%)
  local copies, waits for them, and re-layouts  1.69 us (4%)
    all_to_all x1, blocking collectives, send_selected(): lax.all_to_all(pieces, ('head', 'ctx'), split_axis=0, concat_axis=0, axis...  12.4 us
    all_to_all x1, waiting for transfers between devices, on_device(): lax.all_to_all(far, 'ctx', split_axis=0, concat_axis=0, axis_index_groups...  6.26 us
    all_to_all x1, starting transfers between devices, on_device(): lax.all_to_all(far, 'ctx', split_axis=0, concat_axis=0, axis_index_groups...  4.15 us
    ppermute x1, waiting for transfers between devices, own_block(): came = lax.ppermute(columns(1 - head_rank), 'head', [(0, 1), (1, 0)])  3.95 us
    pallas_call x1, Pallas kernels, attend_far(): pl.pallas_call(far_kernel, out_shape=jax.ShapeDtypeStruct(queries.shape,...  3.52 us
    pallas_call x1, Pallas kernels, attend_near(): pl.pallas_call(near_kernel, out_shape=[pltpu.VMEM((columns // HD, rows, H...  1.85 us
    unnamed x8, local copies, waits for them, and re-layouts  1.62 us
    ppermute x1, starting transfers between devices, own_block(): came = lax.ppermute(columns(1 - head_rank), 'head', [(0, 1), (1, 0)])  1.18 us
  transfers between devices with their start and end apart: 2, of which 2 were waited for; matrix products, arithmetic and copies ran while one was open for 1% of the time, Pallas kernels for 5%

profile of v10, /device:TPU:16, one launch (start us, length us, event | category | flops | bytes accessed | tf_op | source)
XLA Modules:
  0.0 37.2 jit_solution(10918543756180504422)
XLA Ops:
  0.0 1.0 %shard_map.46 = (bf16[8,2,2,32,128]{4,3,2,1,0:T(8,128)(2,1)S(1)}, s32[3,1,16]{2,1,0:T(1,128)S(1)}) custom-call(bf16[8,32,256]{2,1,0:T(8,128)(2,1)} %bitcast.19, bf16[8,32,256]{2,1,0:T(8,128)(2,1)} %bitcast.20, s32[3,1,16]{2,1,0:T(1,128)} %bitcast.21), custom_call_target="tpu_custom_call" | custom-call | tf_op jit(solution)/shard_map/pallas_call | solution.py:52
  1.0 12.4 %all_to_all.10.pieces_ref = bf16[16,2,32,128]{3,2,1,0:T(8,128)(2,1)S(1)} all-to-all(bf16[16,2,32,128]{3,2,1,0:T(8,128)(2,1)S(1)} %bitcast.17), channel_id=1, replica_groups={{31,14,29,12,27,10,25,8,23,6,21,4,19,2,17,0},{15,30,13,28,11,26,9,24,7,..., dimensions={0} | all-to-all | bytes 524288 | tf_op jit(solution)/shard_map/all_to_all | solution.py:93
  13.3 0.9 %shard_map.47 = bf16[16,2,2,32,128]{4,3,2,1,0:T(8,128)(2,1)} custom-call(s32[3,1,16]{2,1,0:T(1,128)S(1)} %get-tuple-element.15.slots_ref, bf16[16,2,32,128]{3,2,1,0:T(8,128)(2,1)S(1)} %all_to_all.10.pieces_ref), custom_call_target="tpu_custom_call" | custom-call | tf_op jit(solution)/shard_map/pallas_call | solution.py:77
  14.2 0.0 copy-start.1
  14.2 0.0 copy-start.2
  14.3 4.2 %all-to-all-start.1 = ((bf16[16,2,2,32,128]{4,3,2,1,0:T(8,128)(2,1)}), bf16[16,2,2,32,128]{4,3,2,1,0:T(8,128)(2,1)S(1)}, u32[]{:S(2)}, u32[]{:S(2)}) async-start(bf16[16,2,2,32,128]{4,3,2,1,0:T(8,128)(2,1)} %shard_map.47), calls=%async_computation.1 | async-start | bytes 1048576 | tf_op jit(solution)/shard_map/all_to_all | solution.py:303
  18.4 0.0 copy-done.1
  18.4 0.0 copy-done.2
  18.4 0.1 dynamic-slice_bitcast_fusion.2
  18.5 1.2 %collective-permute-start = (bf16[2,256,128]{2,1,0:T(8,128)(2,1)S(1)}, bf16[2,256,128]{2,1,0:T(8,128)(2,1)S(1)}, u32[]{:S(2)}, u32[]{:S(2)}) collective-permute-start(bf16[2,256,128]{2,1,0:T(8,128)(2,1)S(1)} %pad_maximum_fusion), channel_id=1, source_target_pairs={{0,16},{16,0},{1,17},{17,1},{2,18},{18,2},{3,19},{19,3},{4,20},{20... | collective-permute-start | bytes 393224 | tf_op jit(solution)/shard_map/ppermute | solution.py:270
  19.7 0.0 copy-start.3
  19.7 0.7 %copy-done.3 = s32[1,16,3]{1,0,2:T(1,128)S(1)} copy-done((s32[1,16,3]{1,0,2:T(1,128)S(1)}, s32[1,16,3]{1,0,2:T(1,128)}, u32[]{:S(2)}) %copy-start.3) | copy-done | bytes 216
  20.4 0.2 fusion
  20.6 3.9 %collective-permute-done = bf16[2,256,128]{2,1,0:T(8,128)(2,1)S(1)} collective-permute-done((bf16[2,256,128]{2,1,0:T(8,128)(2,1)S(1)}, bf16[2,256,128]{2,1,0:T(8,128)(2,1)S(1)}, u32[]{:S(2)}, u32[]{:S(2)}) %collective-permute-start) | collective-permute-done | bytes 131104 | tf_op jit(solution)/shard_map/ppermute | solution.py:270
  24.5 0.0 copy-start
  24.5 0.1 maximum_select_fusion
  24.6 0.9 %copy-done = bf16[512,512]{1,0:T(8,128)(2,1)S(1)} copy-done((bf16[512,512]{1,0:T(8,128)(2,1)S(1)}, bf16[512,512]{1,0:T(8,128)(2,1)}, u32[]{:S(2)}) %copy-start) | copy-done | bytes 524312
  25.6 1.8 %shard_map.48 = (f32[4,512,128]{2,1,0:T(8,128)S(1)}, f32[4,512,128]{2,1,0:T(8,128)S(1)}) custom-call(bf16[512,512]{1,0:T(8,128)(2,1)S(1)} %copy-done, bf16[512,128]{1,0:T(8,128)(2,1)S(1)} %get-tuple-element.22.key_ref, bf16[512,128]{1,0:T(8,128)(2,1)S(1)} %get-tuple-element.21.value_ref), custom_call_target="tpu_custom_call" | custom-call | flops 536870912 | bytes 4194304 | tf_op jit(solution)/shard_map/pallas_call | solution.py:152
  27.4 6.3 %all-to-all-done.1.far_ref = bf16[16,2,2,32,128]{4,3,2,1,0:T(8,128)(2,1)S(1)} async-done(((bf16[16,2,2,32,128]{4,3,2,1,0:T(8,128)(2,1)}), bf16[16,2,2,32,128]{4,3,2,1,0:T(8,128)(2,1)S(1)}, u32[]{:S(2)}, u32[]{:S(2)}) %all-to-all-start.1) | async-done | bytes 524320 | tf_op jit(solution)/shard_map/all_to_all | solution.py:303
  33.7 3.5 %shard_map.49 = bf16[512,512]{1,0:T(8,128)(2,1)} custom-call(s32[1,2]{1,0:T(1,128)S(1)} %bitcast.18, bf16[512,512]{1,0:T(8,128)(2,1)S(1)} %copy-done, bf16[16,2,2,32,128]{4,3,2,1,0:T(8,128)(2,1)S(1)} %all-to-all-done.1.far_ref, f32[4,512,128]{2,1,0:T(8,128)S(1)} %get-tuple-element.19.level_ref, f32[4,512,128]{2,1,0:T(8,128)S(1)} %get-tuple-element.20.mean_ref), custom_call_target="tpu_custom_call" | custom-call | tf_op jit(solution)/shard_map/pallas_call | solution.py:245
  (2 shorter events, 0.0 us)
Async XLA Ops:
  14.2 4.2 %copy-start.1 = (bf16[256,256]{1,0:T(8,128)(2,1)S(1)}, bf16[256,256]{1,0:T(8,128)(2,1)}, u32[]{:S(2)}) copy-start(bf16[256,256]{1,0:T(8,128)(2,1)} %param.5) | copy-start | bytes 393220
  14.2 4.2 %copy-start.2 = (bf16[256,256]{1,0:T(8,128)(2,1)S(1)}, bf16[256,256]{1,0:T(8,128)(2,1)}, u32[]{:S(2)}) copy-start(bf16[256,256]{1,0:T(8,128)(2,1)} %param.6) | copy-start | bytes 393220
  14.3 19.4 %all-to-all-start.1 = ((bf16[16,2,2,32,128]{4,3,2,1,0:T(8,128)(2,1)}), bf16[16,2,2,32,128]{4,3,2,1,0:T(8,128)(2,1)S(1)}, u32[]{:S(2)}, u32[]{:S(2)}) async-start(bf16[16,2,2,32,128]{4,3,2,1,0:T(8,128)(2,1)} %shard_map.47), calls=%async_computation.1 | async-start | bytes 1048576 | tf_op jit(solution)/shard_map/all_to_all | solution.py:303
  18.5 6.0 %collective-permute-start = (bf16[2,256,128]{2,1,0:T(8,128)(2,1)S(1)}, bf16[2,256,128]{2,1,0:T(8,128)(2,1)S(1)}, u32[]{:S(2)}, u32[]{:S(2)}) collective-permute-start(bf16[2,256,128]{2,1,0:T(8,128)(2,1)S(1)} %pad_maximum_fusion), channel_id=1, source_target_pairs={{0,16},{16,0},{1,17},{17,1},{2,18},{18,2},{3,19},{19,3},{4,20},{20... | collective-permute-start | bytes 393224 | tf_op jit(solution)/shard_map/ppermute | solution.py:270
  19.7 0.7 %copy-start.3 = (s32[1,16,3]{1,0,2:T(1,128)S(1)}, s32[1,16,3]{1,0,2:T(1,128)}, u32[]{:S(2)}) copy-start(s32[1,16,3]{1,0,2:T(1,128)} %param.7) | copy-start | bytes 580
  24.5 1.0 %copy-start = (bf16[512,512]{1,0:T(8,128)(2,1)S(1)}, bf16[512,512]{1,0:T(8,128)(2,1)}, u32[]{:S(2)}) copy-start(bf16[512,512]{1,0:T(8,128)(2,1)} %query_ref.1) | copy-start | bytes 1572868

commit v11 on v10

--- a/solution.py
+++ b/solution.py
@@ -1,5 +1,4 @@
 import functools
-import itertools
 import math
 
 import jax
@@ -175,14 +174,14 @@
         columns = slice(h * HD, (h + 1) * HD)
         return pltpu.make_async_copy(ready.at[h], out_ref.at[:, columns], sems.at[h])
 
-    for s in range(picks):
-        place = slice(s * BLK, (s + 1) * BLK)
-        turned[:, place] = far_ref[:, s, 0].reshape(BLK, HD).T
-        valued[place, :HD] = far_ref[:, s, 1].reshape(BLK, HD)
     valued[:, HD:] = jnp.ones((picks * BLK, HD), valued.dtype)
 
-    def attend(first, last):
-        place = slice(first * BLK, (last + 1) * BLK)
+    def attend(slots):
+        place = slice(0, len(slots) * BLK)
+        for i, s in enumerate(slots):
+            part = slice(i * BLK, (i + 1) * BLK)
+            turned[:, part] = far_ref[:, s, 0].reshape(BLK, HD).T
+            valued[part, :HD] = far_ref[:, s, 1].reshape(BLK, HD)
 
         def score(h, begin, end):
             query_rows = query_ref[begin:end, h * HD : (h + 1) * HD]
@@ -212,28 +211,21 @@
 
     @pl.when(rank >= picks)
     def _():
-        attend(0, picks - 1)
-
-    @pl.when(rank < picks)
+        attend(range(picks))
+
+    @pl.when(rank == 1)
     def _():
         flags = live_ref[...]
-        live = [flags[0, s] > 0 for s in range(picks)]
-        for which in itertools.product((False, True), repeat=picks):
-            slots = [s for s in range(picks) if which[s]]
-            met = functools.reduce(
-                jnp.logical_and, [flag if on else ~flag for flag, on in zip(live, which)]
-            )
-            if len(slots) == picks:
-                continue
-
-            @pl.when(met)
-            def _():
-                if slots:
-                    attend(slots[0], slots[-1])
-                else:
-                    for h in range(heads_here):
-                        ready[h] = mean_ref[h].astype(ready.dtype)
-                        leave(h).start()
+        slot = jnp.int32(0)
+        for s in range(1, picks):
+            slot = jnp.where(flags[0, s] > 0, s, slot)
+        attend([slot])
+
+    @pl.when(rank == 0)
+    def _():
+        for h in range(heads_here):
+            ready[h] = mean_ref[h].astype(ready.dtype)
+            leave(h).start()
 
     for h in range(heads_here):
         leave(h).wait()
@@ -285,7 +277,7 @@
     ctx_rank = lax.axis_index("ctx")
     share = keys.shape[0] // ranks
 
-    order = [(i + ranks // 2) % ranks for i in range(ranks)]
+    order = [(i + 5 * ranks // 8) % ranks for i in range(ranks)]
 
     slots = selected.transpose(2, 0, 1)
     plain = heads == 2 and share % 8 == 0 and ranks % 2 == 0

time: 37.6 us -> 37.5 us (level)
  the two profiles are of different devices: /device:TPU:16 before, /device:TPU:5 now
where the time goes in v11:
time: 37.5 us; the launch traced here: 37.1 us
  blocking collectives  14.2 us (38%)
  waiting for transfers between devices  8.19 us (22%)
  Pallas kernels  7.14 us (19%)
  starting transfers between devices  5.47 us (15%)
  local copies, waits for them, and re-layouts  1.69 us (5%)
    all_to_all x1, blocking collectives, send_selected(): lax.all_to_all(pieces, ('head', 'ctx'), split_axis=0, concat_axis=0, axis...  14.2 us
    all_to_all x1, waiting for transfers between devices, on_device(): lax.all_to_all(far, 'ctx', split_axis=0, concat_axis=0, axis_index_groups...  4.87 us
    all_to_all x1, starting transfers between devices, on_device(): lax.all_to_all(far, 'ctx', split_axis=0, concat_axis=0, axis_index_groups...  4.87 us
    pallas_call x1, Pallas kernels, attend_far(): pl.pallas_call(far_kernel, out_shape=jax.ShapeDtypeStruct(queries.shape,...  3.44 us
    ppermute x1, waiting for transfers between devices, own_block(): came = lax.ppermute(columns(1 - head_rank), 'head', [(0, 1), (1, 0)])  3.31 us
    pallas_call x1, Pallas kernels, attend_near(): pl.pallas_call(near_kernel, out_shape=[pltpu.VMEM((columns // HD, rows, H...  1.85 us
    unnamed x8, local copies, waits for them, and re-layouts  1.62 us
    pallas_call x1, Pallas kernels, pack(): pl.pallas_call(pack_kernel, out_shape=[pltpu.VMEM((pairs, 2, 2, rows // p...  0.96 us
  transfers between devices with their start and end apart: 2, of which 2 were waited for; matrix products, arithmetic and copies ran while one was open for 1% of the time, Pallas kernels for 5%

profile of v11, /device:TPU:5, one launch (start us, length us, event | category | flops | bytes accessed | tf_op | source)
XLA Modules:
  0.0 37.1 jit_solution(17010099247765471187)
XLA Ops:
  0.0 1.0 %shard_map.46 = (bf16[8,2,2,32,128]{4,3,2,1,0:T(8,128)(2,1)S(1)}, s32[3,1,16]{2,1,0:T(1,128)S(1)}) custom-call(bf16[8,32,256]{2,1,0:T(8,128)(2,1)} %bitcast.19, bf16[8,32,256]{2,1,0:T(8,128)(2,1)} %bitcast.20, s32[3,1,16]{2,1,0:T(1,128)} %bitcast.21), custom_call_target="tpu_custom_call" | custom-call | tf_op jit(solution)/shard_map/pallas_call | solution.py:51
  1.0 14.2 %all_to_all.10.pieces_ref = bf16[16,2,32,128]{3,2,1,0:T(8,128)(2,1)S(1)} all-to-all(bf16[16,2,32,128]{3,2,1,0:T(8,128)(2,1)S(1)} %bitcast.17), channel_id=1, replica_groups={{31,14,29,12,27,10,25,8,23,6,21,4,19,2,17,0},{15,30,13,28,11,26,9,24,7,..., dimensions={0} | all-to-all | bytes 524288 | tf_op jit(solution)/shard_map/all_to_all | solution.py:92
  15.2 0.9 %shard_map.47 = bf16[16,2,2,32,128]{4,3,2,1,0:T(8,128)(2,1)} custom-call(s32[3,1,16]{2,1,0:T(1,128)S(1)} %get-tuple-element.15.slots_ref, bf16[16,2,32,128]{3,2,1,0:T(8,128)(2,1)S(1)} %all_to_all.10.pieces_ref), custom_call_target="tpu_custom_call" | custom-call | tf_op jit(solution)/shard_map/pallas_call | solution.py:76
  16.1 0.0 copy-start.1
  16.1 0.0 copy-start.2
  16.1 4.9 %all-to-all-start.1 = ((bf16[16,2,2,32,128]{4,3,2,1,0:T(8,128)(2,1)}), bf16[16,2,2,32,128]{4,3,2,1,0:T(8,128)(2,1)S(1)}, u32[]{:S(2)}, u32[]{:S(2)}) async-start(bf16[16,2,2,32,128]{4,3,2,1,0:T(8,128)(2,1)} %shard_map.47), calls=%async_computation.1 | async-start | bytes 1048576 | tf_op jit(solution)/shard_map/all_to_all | solution.py:295
  20.9 0.0 copy-done.1
  21.0 0.0 copy-done.2
  21.0 0.1 dynamic-slice_bitcast_fusion.2
  21.0 0.6 %collective-permute-start = (bf16[2,256,128]{2,1,0:T(8,128)(2,1)S(1)}, bf16[2,256,128]{2,1,0:T(8,128)(2,1)S(1)}, u32[]{:S(2)}, u32[]{:S(2)}) collective-permute-start(bf16[2,256,128]{2,1,0:T(8,128)(2,1)S(1)} %pad_maximum_fusion), channel_id=1, source_target_pairs={{0,16},{16,0},{1,17},{17,1},{2,18},{18,2},{3,19},{19,3},{4,20},{20... | collective-permute-start | bytes 393224 | tf_op jit(solution)/shard_map/ppermute | solution.py:262
  21.7 0.0 copy-start.3
  21.7 0.7 %copy-done.3 = s32[1,16,3]{1,0,2:T(1,128)S(1)} copy-done((s32[1,16,3]{1,0,2:T(1,128)S(1)}, s32[1,16,3]{1,0,2:T(1,128)}, u32[]{:S(2)}) %copy-start.3) | copy-done | bytes 216
  22.3 0.2 fusion
  22.5 3.3 %collective-permute-done = bf16[2,256,128]{2,1,0:T(8,128)(2,1)S(1)} collective-permute-done((bf16[2,256,128]{2,1,0:T(8,128)(2,1)S(1)}, bf16[2,256,128]{2,1,0:T(8,128)(2,1)S(1)}, u32[]{:S(2)}, u32[]{:S(2)}) %collective-permute-start) | collective-permute-done | bytes 131104 | tf_op jit(solution)/shard_map/ppermute | solution.py:262
  25.8 0.0 copy-start
  25.8 0.1 maximum_select_fusion
  26.0 0.9 %copy-done = bf16[512,512]{1,0:T(8,128)(2,1)S(1)} copy-done((bf16[512,512]{1,0:T(8,128)(2,1)S(1)}, bf16[512,512]{1,0:T(8,128)(2,1)}, u32[]{:S(2)}) %copy-start) | copy-done | bytes 524312
  26.9 1.8 %shard_map.48 = (f32[4,512,128]{2,1,0:T(8,128)S(1)}, f32[4,512,128]{2,1,0:T(8,128)S(1)}) custom-call(bf16[512,512]{1,0:T(8,128)(2,1)S(1)} %copy-done, bf16[512,128]{1,0:T(8,128)(2,1)S(1)} %get-tuple-element.22.key_ref, bf16[512,128]{1,0:T(8,128)(2,1)S(1)} %get-tuple-element.21.value_ref), custom_call_target="tpu_custom_call" | custom-call | flops 536870912 | bytes 4194304 | tf_op jit(solution)/shard_map/pallas_call | solution.py:151
  28.7 4.9 %all-to-all-done.1.far_ref = bf16[16,2,2,32,128]{4,3,2,1,0:T(8,128)(2,1)S(1)} async-done(((bf16[16,2,2,32,128]{4,3,2,1,0:T(8,128)(2,1)}), bf16[16,2,2,32,128]{4,3,2,1,0:T(8,128)(2,1)S(1)}, u32[]{:S(2)}, u32[]{:S(2)}) %all-to-all-start.1) | async-done | bytes 524320 | tf_op jit(solution)/shard_map/all_to_all | solution.py:295
  33.6 3.4 %shard_map.49 = bf16[512,512]{1,0:T(8,128)(2,1)} custom-call(s32[1,2]{1,0:T(1,128)S(1)} %bitcast.18, bf16[512,512]{1,0:T(8,128)(2,1)S(1)} %copy-done, bf16[16,2,2,32,128]{4,3,2,1,0:T(8,128)(2,1)S(1)} %all-to-all-done.1.far_ref, f32[4,512,128]{2,1,0:T(8,128)S(1)} %get-tuple-element.19.level_ref, f32[4,512,128]{2,1,0:T(8,128)S(1)} %get-tuple-element.20.mean_ref), custom_call_target="tpu_custom_call" | custom-call | tf_op jit(solution)/shard_map/pallas_call | solution.py:237
  (2 shorter events, 0.0 us)
Async XLA Ops:
  16.1 4.9 %copy-start.1 = (bf16[256,256]{1,0:T(8,128)(2,1)S(1)}, bf16[256,256]{1,0:T(8,128)(2,1)}, u32[]{:S(2)}) copy-start(bf16[256,256]{1,0:T(8,128)(2,1)} %param.5) | copy-start | bytes 393220
  16.1 4.9 %copy-start.2 = (bf16[256,256]{1,0:T(8,128)(2,1)S(1)}, bf16[256,256]{1,0:T(8,128)(2,1)}, u32[]{:S(2)}) copy-start(bf16[256,256]{1,0:T(8,128)(2,1)} %param.6) | copy-start | bytes 393220
  16.1 17.5 %all-to-all-start.1 = ((bf16[16,2,2,32,128]{4,3,2,1,0:T(8,128)(2,1)}), bf16[16,2,2,32,128]{4,3,2,1,0:T(8,128)(2,1)S(1)}, u32[]{:S(2)}, u32[]{:S(2)}) async-start(bf16[16,2,2,32,128]{4,3,2,1,0:T(8,128)(2,1)} %shard_map.47), calls=%async_computation.1 | async-start | bytes 1048576 | tf_op jit(solution)/shard_map/all_to_all | solution.py:295
  21.0 4.8 %collective-permute-start = (bf16[2,256,128]{2,1,0:T(8,128)(2,1)S(1)}, bf16[2,256,128]{2,1,0:T(8,128)(2,1)S(1)}, u32[]{:S(2)}, u32[]{:S(2)}) collective-permute-start(bf16[2,256,128]{2,1,0:T(8,128)(2,1)S(1)} %pad_maximum_fusion), channel_id=1, source_target_pairs={{0,16},{16,0},{1,17},{17,1},{2,18},{18,2},{3,19},{19,3},{4,20},{20... | collective-permute-start | bytes 393224 | tf_op jit(solution)/shard_map/ppermute | solution.py:262
  21.7 0.7 %copy-start.3 = (s32[1,16,3]{1,0,2:T(1,128)S(1)}, s32[1,16,3]{1,0,2:T(1,128)}, u32[]{:S(2)}) copy-start(s32[1,16,3]{1,0,2:T(1,128)} %param.7) | copy-start | bytes 580
  25.8 1.0 %copy-start = (bf16[512,512]{1,0:T(8,128)(2,1)S(1)}, bf16[512,512]{1,0:T(8,128)(2,1)}, u32[]{:S(2)}) copy-start(bf16[512,512]{1,0:T(8,128)(2,1)} %query_ref.1) | copy-start | bytes 1572868

commit v12 on v11

--- a/solution.py
+++ b/solution.py
@@ -202,8 +202,9 @@
             total = product[:, HD:] + scale
             product = product[:, :HD] + mean_ref[h, rows] * scale
             ready[h, rows] = (product / total).astype(ready.dtype)
-            if end == BLK:
-                leave(h).start()
+            pltpu.make_async_copy(
+                ready.at[h, rows], out_ref.at[rows, h * HD : (h + 1) * HD], sems.at[h]
+            ).start()
 
         in_turn(units_of(heads_here, 2 * CHUNK), score, finish)
 

time: 37.5 us -> 37.5 us (level)
  no operation moved by 1% of the time
where the time goes in v12:
time: 37.5 us; the launch traced here: 37.1 us
  blocking collectives  14.2 us (38%)
  waiting for transfers between devices  8.19 us (22%)
  Pallas kernels  7.14 us (19%)
  starting transfers between devices  5.47 us (15%)
  local copies, waits for them, and re-layouts  1.69 us (5%)
    all_to_all x1, blocking collectives, send_selected(): lax.all_to_all(pieces, ('head', 'ctx'), split_axis=0, concat_axis=0, axis...  14.2 us
    all_to_all x1, waiting for transfers between devices, on_device(): lax.all_to_all(far, 'ctx', split_axis=0, concat_axis=0, axis_index_groups...  4.87 us
    all_to_all x1, starting transfers between devices, on_device(): lax.all_to_all(far, 'ctx', split_axis=0, concat_axis=0, axis_index_groups...  4.87 us
    pallas_call x1, Pallas kernels, attend_far(): pl.pallas_call(far_kernel, out_shape=jax.ShapeDtypeStruct(queries.shape,...  3.45 us
    ppermute x1, waiting for transfers between devices, own_block(): came = lax.ppermute(columns(1 - head_rank), 'head', [(0, 1), (1, 0)])  3.31 us
    pallas_call x1, Pallas kernels, attend_near(): pl.pallas_call(near_kernel, out_shape=[pltpu.VMEM((columns // HD, rows, H...  1.85 us
    unnamed x8, local copies, waits for them, and re-layouts  1.62 us
    pallas_call x1, Pallas kernels, pack(): pl.pallas_call(pack_kernel, out_shape=[pltpu.VMEM((pairs, 2, 2, rows // p...  0.96 us
  transfers between devices with their start and end apart: 2, of which 2 were waited for; matrix products, arithmetic and copies ran while one was open for 1% of the time, Pallas kernels for 5%

profile of v12, /device:TPU:5, one launch (start us, length us, event | category | flops | bytes accessed | tf_op | source)
XLA Modules:
  0.0 37.1 jit_solution(8181782594330594927)
XLA Ops:
  0.0 1.0 %shard_map.46 = (bf16[8,2,2,32,128]{4,3,2,1,0:T(8,128)(2,1)S(1)}, s32[3,1,16]{2,1,0:T(1,128)S(1)}) custom-call(bf16[8,32,256]{2,1,0:T(8,128)(2,1)} %bitcast.19, bf16[8,32,256]{2,1,0:T(8,128)(2,1)} %bitcast.20, s32[3,1,16]{2,1,0:T(1,128)} %bitcast.21), custom_call_target="tpu_custom_call" | custom-call | tf_op jit(solution)/shard_map/pallas_call | solution.py:51
  1.0 14.2 %all_to_all.10.pieces_ref = bf16[16,2,32,128]{3,2,1,0:T(8,128)(2,1)S(1)} all-to-all(bf16[16,2,32,128]{3,2,1,0:T(8,128)(2,1)S(1)} %bitcast.17), channel_id=1, replica_groups={{31,14,29,12,27,10,25,8,23,6,21,4,19,2,17,0},{15,30,13,28,11,26,9,24,7,..., dimensions={0} | all-to-all | bytes 524288 | tf_op jit(solution)/shard_map/all_to_all | solution.py:92
  15.2 0.9 %shard_map.47 = bf16[16,2,2,32,128]{4,3,2,1,0:T(8,128)(2,1)} custom-call(s32[3,1,16]{2,1,0:T(1,128)S(1)} %get-tuple-element.15.slots_ref, bf16[16,2,32,128]{3,2,1,0:T(8,128)(2,1)S(1)} %all_to_all.10.pieces_ref), custom_call_target="tpu_custom_call" | custom-call | tf_op jit(solution)/shard_map/pallas_call | solution.py:76
  16.1 0.0 copy-start.1
  16.1 0.0 copy-start.2
  16.1 4.9 %all-to-all-start.1 = ((bf16[16,2,2,32,128]{4,3,2,1,0:T(8,128)(2,1)}), bf16[16,2,2,32,128]{4,3,2,1,0:T(8,128)(2,1)S(1)}, u32[]{:S(2)}, u32[]{:S(2)}) async-start(bf16[16,2,2,32,128]{4,3,2,1,0:T(8,128)(2,1)} %shard_map.47), calls=%async_computation.1 | async-start | bytes 1048576 | tf_op jit(solution)/shard_map/all_to_all | solution.py:296
  20.9 0.0 copy-done.1
  21.0 0.0 copy-done.2
  21.0 0.1 dynamic-slice_bitcast_fusion.2
  21.0 0.6 %collective-permute-start = (bf16[2,256,128]{2,1,0:T(8,128)(2,1)S(1)}, bf16[2,256,128]{2,1,0:T(8,128)(2,1)S(1)}, u32[]{:S(2)}, u32[]{:S(2)}) collective-permute-start(bf16[2,256,128]{2,1,0:T(8,128)(2,1)S(1)} %pad_maximum_fusion), channel_id=1, source_target_pairs={{0,16},{16,0},{1,17},{17,1},{2,18},{18,2},{3,19},{19,3},{4,20},{20... | collective-permute-start | bytes 393224 | tf_op jit(solution)/shard_map/ppermute | solution.py:263
  21.7 0.0 copy-start.3
  21.7 0.7 %copy-done.3 = s32[1,16,3]{1,0,2:T(1,128)S(1)} copy-done((s32[1,16,3]{1,0,2:T(1,128)S(1)}, s32[1,16,3]{1,0,2:T(1,128)}, u32[]{:S(2)}) %copy-start.3) | copy-done | bytes 216
  22.3 0.2 fusion
  22.5 3.3 %collective-permute-done = bf16[2,256,128]{2,1,0:T(8,128)(2,1)S(1)} collective-permute-done((bf16[2,256,128]{2,1,0:T(8,128)(2,1)S(1)}, bf16[2,256,128]{2,1,0:T(8,128)(2,1)S(1)}, u32[]{:S(2)}, u32[]{:S(2)}) %collective-permute-start) | collective-permute-done | bytes 131104 | tf_op jit(solution)/shard_map/ppermute | solution.py:263
  25.8 0.0 copy-start
  25.8 0.1 maximum_select_fusion
  26.0 0.9 %copy-done = bf16[512,512]{1,0:T(8,128)(2,1)S(1)} copy-done((bf16[512,512]{1,0:T(8,128)(2,1)S(1)}, bf16[512,512]{1,0:T(8,128)(2,1)}, u32[]{:S(2)}) %copy-start) | copy-done | bytes 524312
  26.9 1.8 %shard_map.48 = (f32[4,512,128]{2,1,0:T(8,128)S(1)}, f32[4,512,128]{2,1,0:T(8,128)S(1)}) custom-call(bf16[512,512]{1,0:T(8,128)(2,1)S(1)} %copy-done, bf16[512,128]{1,0:T(8,128)(2,1)S(1)} %get-tuple-element.22.key_ref, bf16[512,128]{1,0:T(8,128)(2,1)S(1)} %get-tuple-element.21.value_ref), custom_call_target="tpu_custom_call" | custom-call | flops 536870912 | bytes 4194304 | tf_op jit(solution)/shard_map/pallas_call | solution.py:151
  28.7 4.9 %all-to-all-done.1.far_ref = bf16[16,2,2,32,128]{4,3,2,1,0:T(8,128)(2,1)S(1)} async-done(((bf16[16,2,2,32,128]{4,3,2,1,0:T(8,128)(2,1)}), bf16[16,2,2,32,128]{4,3,2,1,0:T(8,128)(2,1)S(1)}, u32[]{:S(2)}, u32[]{:S(2)}) %all-to-all-start.1) | async-done | bytes 524320 | tf_op jit(solution)/shard_map/all_to_all | solution.py:296
  33.6 3.4 %shard_map.49 = bf16[512,512]{1,0:T(8,128)(2,1)} custom-call(s32[1,2]{1,0:T(1,128)S(1)} %bitcast.18, bf16[512,512]{1,0:T(8,128)(2,1)S(1)} %copy-done, bf16[16,2,2,32,128]{4,3,2,1,0:T(8,128)(2,1)S(1)} %all-to-all-done.1.far_ref, f32[4,512,128]{2,1,0:T(8,128)S(1)} %get-tuple-element.19.level_ref, f32[4,512,128]{2,1,0:T(8,128)S(1)} %get-tuple-element.20.mean_ref), custom_call_target="tpu_custom_call" | custom-call | tf_op jit(solution)/shard_map/pallas_call | solution.py:238
  (2 shorter events, 0.0 us)
Async XLA Ops:
  16.1 4.9 %copy-start.1 = (bf16[256,256]{1,0:T(8,128)(2,1)S(1)}, bf16[256,256]{1,0:T(8,128)(2,1)}, u32[]{:S(2)}) copy-start(bf16[256,256]{1,0:T(8,128)(2,1)} %param.5) | copy-start | bytes 393220
  16.1 4.9 %copy-start.2 = (bf16[256,256]{1,0:T(8,128)(2,1)S(1)}, bf16[256,256]{1,0:T(8,128)(2,1)}, u32[]{:S(2)}) copy-start(bf16[256,256]{1,0:T(8,128)(2,1)} %param.6) | copy-start | bytes 393220
  16.1 17.5 %all-to-all-start.1 = ((bf16[16,2,2,32,128]{4,3,2,1,0:T(8,128)(2,1)}), bf16[16,2,2,32,128]{4,3,2,1,0:T(8,128)(2,1)S(1)}, u32[]{:S(2)}, u32[]{:S(2)}) async-start(bf16[16,2,2,32,128]{4,3,2,1,0:T(8,128)(2,1)} %shard_map.47), calls=%async_computation.1 | async-start | bytes 1048576 | tf_op jit(solution)/shard_map/all_to_all | solution.py:296
  21.0 4.8 %collective-permute-start = (bf16[2,256,128]{2,1,0:T(8,128)(2,1)S(1)}, bf16[2,256,128]{2,1,0:T(8,128)(2,1)S(1)}, u32[]{:S(2)}, u32[]{:S(2)}) collective-permute-start(bf16[2,256,128]{2,1,0:T(8,128)(2,1)S(1)} %pad_maximum_fusion), channel_id=1, source_target_pairs={{0,16},{16,0},{1,17},{17,1},{2,18},{18,2},{3,19},{19,3},{4,20},{20... | collective-permute-start | bytes 393224 | tf_op jit(solution)/shard_map/ppermute | solution.py:263
  21.7 0.7 %copy-start.3 = (s32[1,16,3]{1,0,2:T(1,128)S(1)}, s32[1,16,3]{1,0,2:T(1,128)}, u32[]{:S(2)}) copy-start(s32[1,16,3]{1,0,2:T(1,128)} %param.7) | copy-start | bytes 580
  25.8 1.0 %copy-start = (bf16[512,512]{1,0:T(8,128)(2,1)S(1)}, bf16[512,512]{1,0:T(8,128)(2,1)}, u32[]{:S(2)}) copy-start(bf16[512,512]{1,0:T(8,128)(2,1)} %query_ref.1) | copy-start | bytes 1572868
